TPU v7x, 128 devices: a whole 4x4x4 slice. The times are simulated.
128 devices in a mesh: dp: 16 (over x, z_lo, core), tensor: 8 (over z_hi, y).
Axes of the slice: x: 4, y: 4, z: 4 (z_hi: 2, z_lo: 2; z = z_hi * 2 + z_lo), core: 2. Of those that a mesh axis runs over, the one named last changes fastest.
Arguments:
- tokens: bfloat16 [16384, 3072], P(('dp', 'tensor')), may hold values from -6 to 6
- cotangent: bfloat16 [16384, 3072], P(('dp', 'tensor')), may hold values from -6 to 6
- expert_ids: int32 [16384, 2], P(('dp', 'tensor')), may hold values from 0 to 7, as said below
- combine: float32 [16384], P(('dp', 'tensor')), may hold values from 0.2 to 1
- w_gate: bfloat16 [3072, 8192], P(None, 'tensor'), may hold values from -0.109375 to 0.109375
- w_up: bfloat16 [3072, 8192], P(None, 'tensor'), may hold values from -0.109375 to 0.109375
- w_down: bfloat16 [8192, 3072], P('tensor'), may hold values from -0.0625 to 0.0625
Outputs:
- expert_output: bfloat16 [16384, 3072], P(('dp', 'tensor'))
- token_grad: bfloat16 [16384, 3072], P(('dp', 'tensor'))
- gate_grad: bfloat16 [3072, 8192], P('dp', 'tensor')
- up_grad: bfloat16 [3072, 8192], P('dp', 'tensor')
- down_grad: bfloat16 [8192, 3072], P('tensor', 'dp')
Inputs may be any that keep to these rules, and one draw needn't show every extreme that they name: `expert_ids`: each row names two different experts. Within each aligned block of 128 rows (the rows of one device) expert 0 is named by at most 48 rows, and in every draw all blocks of some group of 1024 rows name it exactly 48 times.
All inputs are finite; a program needn't handle non-finite values.
Results may differ from a plain program's by a relative error of at most 0.022.
Values may be sent and summed in bfloat16 or wider, within the bound.
No kernel may reach another device: no remote copies, remote signals or barrier semaphores. Data moves between devices by JAX's collectives and lax.ppermute only.
A program may use at most 192 MiB of HBM per device.

v0:
```python
import functools
import itertools
import math

import jax
import jax.numpy as jnp
from jax import lax
from jax.experimental import pallas as pl
from jax.experimental.pallas import tpu as pltpu
from jax.sharding import PartitionSpec as P

SLOTS = 48
ROWS = 384
DW = 3072
FF = 1024
HALF = 512
FEAT = 384
BF = jnp.bfloat16
F32 = jnp.float32
VMEM = 10 * 1024 * 1024
COST = 1000

IN_VMEM = pl.BlockSpec(memory_space=pltpu.VMEM)
IN_SMEM = pl.BlockSpec(memory_space=pltpu.SMEM)
IN_HBM = pl.BlockSpec(memory_space=pltpu.HBM)

DIM = (4, 2, 2, 2, 4)


def linear(place):
    r = 0
    for q, n in zip(place, DIM):
        r = r * n + q % n
    return r


def shift(value, axis, by):
    pairs = []
    for place in itertools.product(*map(range, DIM)):
        to = list(place)
        to[axis] += by
        pairs.append((linear(place), linear(to)))
    return lax.ppermute(value, ("dp", "tensor"), pairs)


to_x = lambda v, by: shift(v, 0, by)
to_zlo = lambda v: shift(v, 1, 1)
to_core = lambda v: shift(v, 2, 1)
to_zhi = lambda v: shift(v, 3, 1)
to_y = lambda v, by: shift(v, 4, by)


def dot(a, b):
    return jnp.dot(a, b, preferred_element_type=F32)


def dot_t(a, b):
    return lax.dot_general(a, b, (((1,), (1,)), ((), ())), preferred_element_type=F32)


def t_dot(a, b):
    return lax.dot_general(a, b, (((0,), (0,)), ((), ())), preferred_element_type=F32)


def cost(flops, nbytes):
    return pl.CostEstimate(flops=int(flops / COST), bytes_accessed=int(nbytes / COST), transcendentals=0)


def params():
    return pltpu.CompilerParams(vmem_limit_bytes=VMEM)


def after(value, *others):
    return lax.optimization_barrier((value, *others))[0]


def picks_of(ids, weight):
    n = ids.shape[1]
    chosen = (ids[0:1] == 0) | (ids[1:2] == 0)
    ones = jnp.where(chosen, 1.0, 0.0).astype(BF)
    before = lax.broadcasted_iota(jnp.int32, (n, n), 0) <= lax.broadcasted_iota(jnp.int32, (n, n), 1)
    place = dot(jnp.broadcast_to(ones, (8, n)), jnp.where(before, 1.0, 0.0).astype(BF))[0:1]
    place = place.astype(jnp.int32) - 1
    slot = lax.broadcasted_iota(jnp.int32, (SLOTS, n), 0)
    picks = jnp.where((place == slot) & chosen, 1.0, 0.0)
    return picks.astype(BF), jnp.sum(picks * weight, axis=1, keepdims=True)


def select_kernel(ids, weight, x, d, out, ids_here, weight_here, x_here, d_here, sems):
    copies = [
        pltpu.make_async_copy(far, near, sems.at[k])
        for k, (far, near) in enumerate(
            ((ids, ids_here), (weight, weight_here), (x, x_here), (d, d_here))
        )
    ]
    for copy in copies:
        copy.start()
    copies[0].wait()
    copies[1].wait()
    picks, slot_weight = picks_of(ids_here[...], weight_here[...])
    copies[2].wait()
    out[0] = dot(picks, x_here[...]).astype(BF)
    copies[3].wait()
    out[1] = (dot(picks, d_here[...]) * slot_weight).astype(BF)


def in_hbm(array):
    return pltpu.with_memory_space_constraint(array, pltpu.HBM)


def select(*arrays):
    return pl.pallas_call(
        select_kernel,
        in_specs=[IN_HBM] * 4,
        out_specs=IN_VMEM,
        out_shape=pltpu.VMEM((2, SLOTS, DW), BF),
        scratch_shapes=[pltpu.VMEM(a.shape, a.dtype) for a in arrays]
        + [pltpu.SemaphoreType.DMA((4,))],
        compiler_params=params(),
        cost_estimate=cost(4 * SLOTS * 128 * DW, 2.2e6),
    )(*map(in_hbm, arrays))


def place_kernel(ids, weight, kept, got, output, token_grad):
    picks, slot_weight = picks_of(ids[...], weight[...])
    out = kept[0].astype(F32) + got[0].astype(F32)
    output[...] = t_dot(picks, (out * slot_weight).astype(BF)).astype(BF)
    back = kept[1].astype(F32) + got[1].astype(F32)
    token_grad[...] = t_dot(picks, back.astype(BF)).astype(BF)


def place_rows(ids, weight, kept, got):
    return pl.pallas_call(
        place_kernel,
        in_specs=[IN_VMEM] * 4,
        out_specs=[IN_VMEM] * 2,
        out_shape=[jax.ShapeDtypeStruct((128, DW), BF)] * 2,
        compiler_params=params(),
        cost_estimate=cost(4 * SLOTS * 128 * DW, 2.8e6),
    )(ids, weight, kept, got)


IN_ANY = pl.BlockSpec(memory_space=pl.ANY)


def without(first, count, kernel):
    def run(*refs):
        kernel(*refs[:first], *refs[first + count :])

    return run


def call(kernel, scalars, arrays, shapes, flops, earlier=(), hbm=(), scratch=()):
    shapes = [s if isinstance(s[0], tuple) else (s, BF) for s in shapes]
    size = sum(a.size for a in arrays) + sum(math.prod(s) for s, _ in shapes)
    inputs = len(scalars) + len(arrays) + len(hbm)
    return pl.pallas_call(
        without(inputs, len(earlier), kernel),
        in_specs=[IN_SMEM] * len(scalars)
        + [IN_VMEM] * len(arrays)
        + [IN_HBM] * len(hbm)
        + [IN_ANY] * len(earlier),
        out_specs=[IN_VMEM] * len(shapes),
        out_shape=[pltpu.VMEM(s, t) for s, t in shapes],
        scratch_shapes=list(scratch),
        compiler_params=params(),
        cost_estimate=cost(flops, size),
    )(*scalars, *arrays, *map(in_hbm, hbm), *earlier)


def stage_kernel(n, *refs):
    sems = refs[-1]
    copies = [pltpu.make_async_copy(refs[i], refs[n + i], sems.at[i]) for i in range(n)]
    for copy in copies:
        copy.start()
    for copy in copies:
        copy.wait()


def stage(arrays, *earlier):
    return call(
        functools.partial(stage_kernel, len(arrays)),
        [],
        [],
        [a.shape for a in arrays],
        1,
        earlier,
        hbm=arrays,
        scratch=[pltpu.SemaphoreType.DMA((len(arrays),))],
    )


def half(h):
    return pl.ds(pl.multiple_of(h * HALF, HALF), HALF)


def gather(which, chunks, rows):
    for k, chunk in enumerate(chunks):
        rows[k * SLOTS : (k + 1) * SLOTS] = chunk[...] if len(chunk.shape) == 2 else chunk[which]


def gather_kernel(*refs):
    gather(0, refs[:8], refs[8])


def gather_rows(chunks, *earlier):
    return call(gather_kernel, [], chunks, [(ROWS, DW)], 1, earlier)[0]


def split_kernel(a, b, x, d):
    x[...] = a[0]
    d[...] = b[1]


def split(a, b):
    return call(split_kernel, [], [a, b], [(SLOTS, DW)] * 2, 1)


def gate_kernel(core, rows, w_gate, w_up, hidden, sent, act, slope):
    for h in range(2):
        at = slice(h * HALF, (h + 1) * HALF)
        gate = dot(rows[...], w_gate[:, at])
        up = dot(rows[...], w_up[:, at])
        s = jax.nn.sigmoid(gate)
        silu = gate * s
        act[:, at] = silu
        slope[:, at] = up * s * (1.0 + gate * (1.0 - s))
        hidden[:, at] = (silu * up).astype(BF)
    sent[...] = hidden[:, half(1 - core[0])]


def gate_up(core, rows, w_gate, w_up):
    shapes = [(ROWS, FF), (ROWS, HALF), ((ROWS, FF), F32), ((ROWS, FF), F32)]
    return call(gate_kernel, [core], [rows, w_gate, w_up], shapes, 4 * ROWS * DW * FF)


def back_kernel(core, *refs):
    chunks, (w_down, act, slope, rows, d_gate, d_up, sent) = refs[:8], refs[8:]
    gather(1, chunks, rows)
    for h in range(2):
        at = slice(h * HALF, (h + 1) * HALF)
        d_hidden = dot_t(rows[...], w_down[at, :])
        d_up[:, at] = (d_hidden * act[:, at]).astype(BF)
        d_gate[:, at] = (d_hidden * slope[:, at]).astype(BF)
    sent[0] = d_gate[:, half(1 - core[0])]
    sent[1] = d_up[:, half(1 - core[0])]


def back_hidden(core, chunks, w_down, act, slope):
    shapes = [(ROWS, DW), (ROWS, FF), (ROWS, FF), (2, ROWS, HALF)]
    return call(back_kernel, [core], [*chunks, w_down, act, slope], shapes, 2 * ROWS * DW * FF)


def out_kernel(hidden, w_down, out):
    for j in range(0, DW, 768):
        at = slice(j, j + 768)
        out[:, at] = dot(hidden[...], w_down[:, at]).astype(BF)


def out_terms(hidden, w_down, *earlier):
    return call(out_kernel, [], [hidden, w_down], [(ROWS, DW)], 2 * ROWS * DW * FF, earlier)[0]


def token_kernel(d_gate, d_up, w_gate, w_up, out, far_a, far_b, above, below, own):
    targets = [far_a, far_b] + [t.at[dz] for t in (above, below, own) for dz in range(2)]
    for j in range(0, DW, 768):
        at = slice(j, j + 768)
        back = dot_t(d_gate[...], w_gate[at, :]) + dot_t(d_up[...], w_up[at, :])
        for k, target in enumerate(targets):
            rows = slice(k * SLOTS, (k + 1) * SLOTS)
            target[0, :, at] = out[rows, at]
            target[1, :, at] = back[rows].astype(BF)


def row_terms(d_gate, d_up, w_gate, w_up, out, *earlier):
    shapes = [(2, SLOTS, DW)] * 2 + [(2, 2, SLOTS, DW)] * 3
    arrays = [d_gate, d_up, w_gate, w_up, out]
    return call(token_kernel, [], arrays, shapes, 4 * ROWS * DW * FF, earlier)


def both(own, other):
    return jnp.concatenate([own, other], axis=0)


def features(place, dx):
    at = ((place[2] + dx) % 4) * (2 * FEAT)
    return pl.ds(pl.multiple_of(at, 2 * FEAT), 2 * FEAT)


def store_pair(place, first, second, low, high):
    @pl.when(place[1] == 0)
    def _():
        first[...] = low
        second[...] = high

    @pl.when(place[1] == 1)
    def _():
        first[...] = high
        second[...] = low


def grads_kernel(pairs, place, x_own, x_other, d_gate, d_up, got, *outs):
    mine = half(place[0])
    terms = [both(t[:, mine], got[m]) for m, t in enumerate((d_gate, d_up))]
    outs = list(outs)
    for dx, dz in pairs:
        if dz is None:
            at = features(place, dx)
        else:
            at = ((place[2] + dx) % 4) * (2 * FEAT) + ((place[1] + dz) % 2) * FEAT
            at = pl.ds(pl.multiple_of(at, FEAT), FEAT)
        x = both(x_own[:, at], x_other[:, at])
        here = [outs.pop(0) for _ in range(2 if dz is None else 1)]
        for m in range(2):
            result = t_dot(x, terms[m]).astype(BF)
            if dz is None:
                store_pair(place, here[0].at[m], here[1].at[m], result[:FEAT], result[FEAT:])
            else:
                here[0][m] = result


def gate_up_grads(place, pairs, x_own, x_other, d_gate, d_up, got, *earlier):
    n = sum(2 if dz is None else 1 for _, dz in pairs)
    return call(
        functools.partial(grads_kernel, pairs),
        [place],
        [x_own, x_other, d_gate, d_up, got],
        [(2, FEAT, HALF)] * n,
        n * ROWS * DW * FF / 2,
        earlier,
    )


def down_kernel(place, d_own, d_other, hidden, got, kept, sent):
    h = both(hidden[:, half(place[0])], got[...])
    for k, dx in enumerate((2, 1, 3, 0)):
        at = features(place, dx)
        result = t_dot(both(d_own[:, at], d_other[:, at]), h).astype(BF)
        store_pair(place, kept.at[k], sent.at[k], result[:FEAT], result[FEAT:])


def down_grads(place, d_own, d_other, hidden, got, *earlier):
    shapes = [(4, FEAT, HALF)] * 2
    return call(down_kernel, [place], [d_own, d_other, hidden, got], shapes, 2 * ROWS * DW * FF, earlier)


def add(*terms):
    return sum(t[...].astype(F32) for t in terms).astype(BF)


def add_pairs_kernel(n, *refs):
    for k in range(n):
        refs[2 * n + k][...] = add(refs[2 * k], refs[2 * k + 1])


def add_pairs(*terms):
    n = len(terms) // 2
    shapes = [t.shape for t in terms[::2]]
    flops = sum(math.prod(s) for s in shapes)
    return call(functools.partial(add_pairs_kernel, n), [], terms, shapes, flops)


def add_all_kernel(*refs):
    refs[-1][...] = add(*refs[:-1])


def add_all(*terms):
    return call(add_all_kernel, [], terms, [terms[0].shape], 2 * terms[0].size)[0]


def add_into_kernel(above, got_a, below, got_b, new_above, new_below):
    new_above[0] = add(above.at[0], got_a)
    new_above[1] = above[1]
    new_below[0] = below[0]
    new_below[1] = add(below.at[1], got_b)


def add_into(above, got_a, below, got_b, *earlier):
    return call(
        add_into_kernel, [], [above, got_a, below, got_b], [above.shape] * 2, above.size, earlier
    )


def add_three_kernel(own, above, below, kept, sent):
    kept[...] = add(own.at[0], above.at[0], below.at[0])
    sent[...] = add(own.at[1], above.at[1], below.at[1])


def add_three(own, above, below):
    return call(add_three_kernel, [], [own, above, below], [own.shape[1:]] * 2, 2 * own.size)


def halves_kernel(place, *refs):
    *terms, mine, theirs = refs
    total = add(*terms)
    low, high = total[:, : FEAT // 2], total[:, FEAT // 2 :]

    @pl.when(place[0] == 0)
    def _():
        mine[...] = low
        theirs[...] = high

    @pl.when(place[0] == 1)
    def _():
        mine[...] = high
        theirs[...] = low


def halves(place, *terms):
    n = terms[0].shape[0]
    return call(halves_kernel, [place], terms, [(n, FEAT // 2, HALF)] * 2, 2 * terms[0].size)


def join_kernel(place, mine, got, *outs):
    for k, out in enumerate(outs):

        @pl.when(place[0] == 0)
        def _():
            out[:, :HALF] = mine[k]
            out[:, HALF:] = got[k]

        @pl.when(place[0] == 1)
        def _():
            out[:, :HALF] = got[k]
            out[:, HALF:] = mine[k]


def join(place, mine, got):
    n = mine.shape[0]
    return pl.pallas_call(
        join_kernel,
        in_specs=[IN_SMEM, IN_VMEM, IN_VMEM],
        out_specs=[IN_VMEM] * n,
        out_shape=[jax.ShapeDtypeStruct((FEAT // 2, FF), BF)] * n,
        compiler_params=params(),
        cost_estimate=cost(mine.size, 8 * mine.size),
    )(place, mine, got)


def cut_kernel(kept, got, far_a, far_b, above, below, own):
    n = FEAT // 2
    far = add(kept.at[0], got.at[0])
    far_a[...] = far[:n]
    far_b[...] = far[n:]
    for k, out in enumerate((above, below)):
        total = add(kept.at[1 + k], got.at[1 + k])
        out[0] = total[:n]
        out[1] = total[n:]
    own[0] = add(kept.at[3], got.at[3])


def cut(kept, got, *earlier):
    n = FEAT // 2
    shapes = [(n, HALF)] * 2 + [(2, n, HALF)] * 2 + [(1, FEAT, HALF)]
    return call(cut_kernel, [], [kept, got], shapes, kept.size, earlier)


def local(tokens, cotangent, expert_ids, combine, w_gate, w_up, w_down):
    dp = lax.axis_index("dp")
    place = jnp.stack([dp % 2, (dp // 2) % 2, dp // 4]).astype(jnp.int32)
    ids, weight = expert_ids.T, combine.reshape(1, -1)

    sel = select(ids, weight, tokens, cotangent)
    zhi, up0, down0 = to_zhi(sel), to_y(sel, -1), to_y(sel, 1)
    far0, down1 = to_y(down0, 1), to_zhi(down0)
    up1 = to_y(after(zhi, up0), -1)
    w_gate, w_up, w_down = stage([w_gate, w_up, w_down], up0, zhi)
    x_far1, d_far1 = split(up1, down1)
    x_far1, d_far1 = to_y(x_far1, -1), to_y(d_far1, 1)
    x_rows = gather_rows([far0, x_far1, up0, up1, down0, down1, sel, zhi])
    x_other = to_core(x_rows)
    hidden, hidden_sent, act, slope = gate_up(place, x_rows, w_gate, w_up)
    hidden_got = to_core(hidden_sent)
    d_chunks = [far0, d_far1, up0, up1, down0, down1, sel, zhi]
    d_rows, d_gate, d_up, d_sent = back_hidden(place, d_chunks, w_down, act, slope)
    d_got = to_core(d_sent)
    d_other = to_core(d_rows)
    out = out_terms(hidden, w_down, d_gate)

    far_a, far_b = gate_up_grads(place, [(2, None)], x_rows, x_other, d_gate, d_up, d_got, out)
    far_got_a, far_got_b = to_x(far_a, 1), to_x(far_b, -1)
    down_kept, down_sent = down_grads(place, d_rows, d_other, hidden, hidden_got, far_a)
    down_got = to_zlo(down_sent)
    row_far_a, row_far_b, row_above, row_below, row_own = row_terms(
        d_gate, d_up, w_gate, w_up, out, down_kept
    )
    row_got_a, row_got_b = to_y(row_far_a, 1), to_y(row_far_b, -1)
    above1, below1 = gate_up_grads(
        place, [(1, 1), (3, 1)], x_rows, x_other, d_gate, d_up, d_got, row_own
    )
    above0, below0, own0, own1 = gate_up_grads(
        place, [(1, 0), (3, 0), (0, None)], x_rows, x_other, d_gate, d_up, d_got, above1
    )
    below1, above0 = add_pairs(below1, far_got_b, above0, far_got_a)
    row_above, row_below = add_into(row_above, row_got_a, row_below, row_got_b, above0)
    above1, below1 = to_x(after(above1, above0), 1), to_x(below1, -1)
    row_above, row_below = to_y(row_above, 1), to_y(row_below, -1)
    sum1 = add_all(own1, above1, below1)
    far_a, far_b, above, below, down_own = cut(down_kept, down_got, sum1)
    above0, below0, *_ = lax.optimization_barrier((above0, below0, above1, below1, down_got))
    above0, below0 = to_x(above0, 1), to_x(below0, -1)
    sum1 = to_zlo(sum1)
    far_a, far_b = to_x(far_a, 1), to_x(far_b, -1)
    row_kept, row_sent = add_three(row_own, row_above, row_below)
    row_got = to_zhi(row_sent)
    expert_output, token_grad = place_rows(ids, weight, row_kept, row_got)
    mine, theirs = halves(place, own0, above0, below0, sum1)
    gate_grad, up_grad = join(place, mine, to_core(theirs))
    above, below = add_into(above, far_a, below, far_b)
    whole = lambda v: v.reshape(1, FEAT, HALF)
    above, below = whole(to_x(above, 1)), whole(to_x(below, -1))
    mine, theirs = halves(place, down_own, above, below)
    (down_grad,) = join(place, mine, to_core(theirs))
    return (expert_output, token_grad, gate_grad, up_grad, down_grad.T)


def solution(mesh):
    placed = (
        P(("dp", "tensor"), None),
        P(("dp", "tensor"), None),
        P(("dp", "tensor"), None),
        P(("dp", "tensor")),
        P(None, "tensor"),
        P(None, "tensor"),
        P("tensor", None),
    )
    return jax.shard_map(
        local,
        mesh=mesh,
        in_specs=placed,
        out_specs=(
            P(("dp", "tensor"), None),
            P(("dp", "tensor"), None),
            P("dp", "tensor"),
            P("dp", "tensor"),
            P("tensor", "dp"),
        ),
        check_vma=False,
    )
```

profile of v0, /device:TPU:1, one launch (start us, length us, event | category | flops | bytes accessed | tf_op | source)
XLA Modules:
  0.0 155.5 jit_solution(11249710944542316896)
XLA Ops:
  0.6 1.7 %shard_map.110.refs_6_.refs_7_ = bf16[2,48,3072]{2,1,0:T(8,128)(2,1)S(1)} custom-call(s32[2,128]{1,0:T(2,128)} %bitcast.10, f32[1,128]{1,0:T(1,128)} %bitcast.12, bf16[128,3072]{1,0:T(8,128)(2,1)} %x.1, bf16[128,3072]{1,0:T(8,128)(2,1)} %d.1), custom_call_target="tpu_custom_call" | custom-call | flops 75497 | bytes 2200 | tf_op jit(solution)/shard_map/pallas_call | solution.py:112
  2.4 4.5 %collective-permute-start.2 = (bf16[2,48,3072]{2,1,0:T(8,128)(2,1)S(1)}, bf16[2,48,3072]{2,1,0:T(8,128)(2,1)S(1)}, u32[]{:S(2)}, u32[]{:S(2)}) collective-permute-start(bf16[2,48,3072]{2,1,0:T(8,128)(2,1)S(1)} %shard_map.110.refs_6_.refs_7_), channel_id=1, source_target_pairs={{0,4},{1,5},{2,6},{3,7},{4,0},{5,1},{6,2},{7,3},{8,12},{9,13},{10,... | collective-permute-start | bytes 1769480 | tf_op jit(solution)/shard_map/ppermute | solution.py:43
  6.9 2.7 %collective-permute-start.3 = (bf16[2,48,3072]{2,1,0:T(8,128)(2,1)S(1)}, bf16[2,48,3072]{2,1,0:T(8,128)(2,1)S(1)}, u32[]{:S(2)}, u32[]{:S(2)}) collective-permute-start(bf16[2,48,3072]{2,1,0:T(8,128)(2,1)S(1)} %shard_map.110.refs_6_.refs_7_), channel_id=1, source_target_pairs={{0,3},{1,0},{2,1},{3,2},{4,7},{5,4},{6,5},{7,6},{8,11},{9,8},{10,9... | collective-permute-start | bytes 1769480 | tf_op jit(solution)/shard_map/ppermute | solution.py:43
  9.6 10.3 %collective-permute-done.2.refs_4_.refs_7_.refs_8_ = bf16[2,48,3072]{2,1,0:T(8,128)(2,1)S(1)} collective-permute-done((bf16[2,48,3072]{2,1,0:T(8,128)(2,1)S(1)}, bf16[2,48,3072]{2,1,0:T(8,128)(2,1)S(1)}, u32[]{:S(2)}, u32[]{:S(2)}) %collective-permute-start.2) | collective-permute-done | bytes 589856 | tf_op jit(solution)/shard_map/ppermute | solution.py:43
  19.9 1.4 collective-permute-done.3.refs_3_.refs_2_
  21.3 3.4 %collective-permute-start.4 = (bf16[2,48,3072]{2,1,0:T(8,128)(2,1)S(1)}, bf16[2,48,3072]{2,1,0:T(8,128)(2,1)S(1)}, u32[]{:S(2)}, u32[]{:S(2)}) collective-permute-start(bf16[2,48,3072]{2,1,0:T(8,128)(2,1)S(1)} %collective-permute-done.2.refs_4_.refs_7_.refs_8_), channel_id=1, source_target_pairs={{0,3},{1,0},{2,1},{3,2},{4,7},{5,4},{6,5},{7,6},{8,11},{9,8},{10,9... | collective-permute-start | bytes 1769480 | tf_op jit(solution)/shard_map/ppermute | solution.py:43
  24.7 0.6 collective-permute-start.5
  25.3 10.1 %collective-permute-done.4.refs_0_.refs_3_.refs_4_ = bf16[2,48,3072]{2,1,0:T(8,128)(2,1)S(1)} collective-permute-done((bf16[2,48,3072]{2,1,0:T(8,128)(2,1)S(1)}, bf16[2,48,3072]{2,1,0:T(8,128)(2,1)S(1)}, u32[]{:S(2)}, u32[]{:S(2)}) %collective-permute-start.4) | collective-permute-done | bytes 589856 | tf_op jit(solution)/shard_map/ppermute | solution.py:43
  35.4 3.4 %collective-permute-done.5.refs_1_.refs_5_.refs_6_ = bf16[2,48,3072]{2,1,0:T(8,128)(2,1)S(1)} collective-permute-done((bf16[2,48,3072]{2,1,0:T(8,128)(2,1)S(1)}, bf16[2,48,3072]{2,1,0:T(8,128)(2,1)S(1)}, u32[]{:S(2)}, u32[]{:S(2)}) %collective-permute-start.5) | collective-permute-done | bytes 589856 | tf_op jit(solution)/shard_map/ppermute | solution.py:43
  38.9 0.8 shard_map.111
  39.7 0.3 collective-permute-start.7
  40.0 1.2 collective-permute-start.6
  41.2 0.1 pad_add_fusion.refs_0_.place
  41.3 6.4 %shard_map.112 = (bf16[3072,1024]{1,0:T(8,128)(2,1)S(1)}, bf16[3072,1024]{1,0:T(8,128)(2,1)S(1)}, bf16[1024,3072]{1,0:T(8,128)(2,1)S(1)}) custom-call(bf16[3072,1024]{1,0:T(8,128)(2,1)} %refs_0_.1, bf16[3072,1024]{1,0:T(8,128)(2,1)} %refs_1_.1, bf16[1024,3072]{1,0:T(8,128)(2,1)} %refs_2_.1, bf16[2,48,3072]{2,1,0:T(8,128)(2,1)S(1)} %collective-permute-done.3.refs_3_.refs_2_, ...), custom_call_target="tpu_custom_call" | custom-call | bytes 9437 | tf_op jit(solution)/shard_map/pallas_call | solution.py:157
  47.7 1.3 shard_map.113.refs_1_
  49.0 3.7 %collective-permute-start.10 = (bf16[384,3072]{1,0:T(8,128)(2,1)S(1)}, bf16[384,3072]{1,0:T(8,128)(2,1)S(1)}, u32[]{:S(2)}, u32[]{:S(2)}) collective-permute-start(bf16[384,3072]{1,0:T(8,128)(2,1)S(1)} %shard_map.113.refs_1_), channel_id=1, source_target_pairs={{0,8},{1,9},{2,10},{3,11},{4,12},{5,13},{6,14},{7,15},{8,0},{9,1},... | collective-permute-start | bytes 7077896 | tf_op jit(solution)/shard_map/ppermute | solution.py:43
  52.7 5.9 %shard_map.114 = (bf16[384,1024]{1,0:T(8,128)(2,1)S(1)}, bf16[384,512]{1,0:T(8,128)(2,1)S(1)}, f32[384,1024]{1,0:T(8,128)S(1)}, f32[384,1024]{1,0:T(8,128)S(1)}) custom-call(s32[3]{0:T(128)S(1)} %pad_add_fusion.refs_0_.place, bf16[384,3072]{1,0:T(8,128)(2,1)S(1)} %shard_map.113.refs_1_, bf16[3072,1024]{1,0:T(8,128)(2,1)S(1)} %get-tuple-element.62.refs_2_, ...), custom_call_target="tpu_custom_call" | custom-call | flops 4831838 | bytes 8847 | tf_op jit(solution)/shard_map/pallas_call | solution.py:157
  58.6 3.9 %shard_map.115 = (bf16[384,3072]{1,0:T(8,128)(2,1)S(1)}, bf16[384,1024]{1,0:T(8,128)(2,1)S(1)}, bf16[384,1024]{1,0:T(8,128)(2,1)S(1)}, bf16[2,384,512]{2,1,0:T(8,128)(2,1)S(1)}) custom-call(s32[3]{0:T(128)S(1)} %pad_add_fusion.refs_0_.place, bf16[2,48,3072]{2,1,0:T(8,128)(2,1)} %collective-permute-done.1.refs_0_.refs_1_, ...), custom_call_target="tpu_custom_call" | custom-call | flops 2415919 | bytes 8503 | tf_op jit(solution)/shard_map/pallas_call | solution.py:157
  62.5 0.1 collective-permute-start.8
  62.6 0.5 collective-permute-start.11
  63.1 0.1 collective-permute-start.9
  63.2 2.6 %shard_map.116.refs_6_.refs_4_ = bf16[384,3072]{1,0:T(8,128)(2,1)S(1)} custom-call(bf16[384,1024]{1,0:T(8,128)(2,1)S(1)} %get-tuple-element.68.refs_0_.refs_3_, bf16[1024,3072]{1,0:T(8,128)(2,1)S(1)} %get-tuple-element.60.refs_9_.refs_1_, bf16[384,1024]{1,0:T(8,128)(2,1)S(1)} %get-tuple-element.66.refs_2_.refs_3_.refs_0_), custom_call_target="tpu_custom_call" | custom-call | flops 2415919 | bytes 4718 | tf_op jit(solution)/shard_map/pallas_call | solution.py:157
  65.8 2.4 %collective-permute-done.11.refs_5_ = bf16[2,384,512]{2,1,0:T(8,128)(2,1)S(1)} collective-permute-done((bf16[2,384,512]{2,1,0:T(8,128)(2,1)S(1)}, bf16[2,384,512]{2,1,0:T(8,128)(2,1)S(1)}, u32[]{:S(2)}, u32[]{:S(2)}) %collective-permute-start.11) | collective-permute-done | bytes 786464 | tf_op jit(solution)/shard_map/ppermute | solution.py:43
  68.2 2.3 %shard_map.117 = (bf16[2,384,512]{2,1,0:T(8,128)(2,1)S(1)}, bf16[2,384,512]{2,1,0:T(8,128)(2,1)S(1)}) custom-call(s32[3]{0:T(128)S(1)} %pad_add_fusion.refs_0_.place, bf16[384,3072]{1,0:T(8,128)(2,1)S(1)} %shard_map.113.refs_1_, bf16[384,3072]{1,0:T(8,128)(2,1)S(1)} %collective-permute-done.10.refs_2_, ...), custom_call_target="tpu_custom_call" | custom-call | flops 1207959 | bytes 4325 | tf_op jit(solution)/shard_map/pallas_call | solution.py:157
  70.6 2.5 %collective-permute-start.14 = (bf16[2,384,512]{2,1,0:T(8,128)(2,1)S(1)}, bf16[2,384,512]{2,1,0:T(8,128)(2,1)S(1)}, u32[]{:S(2)}, u32[]{:S(2)}) collective-permute-start(bf16[2,384,512]{2,1,0:T(8,128)(2,1)S(1)} %get-tuple-element.80), channel_id=1, source_target_pairs={{0,96},{1,97},{2,98},{3,99},{4,100},{5,101},{6,102},{7,103},{8,104... | collective-permute-start | bytes 2359304 | tf_op jit(solution)/shard_map/ppermute | solution.py:43
  73.1 4.1 %shard_map.118 = (bf16[4,384,512]{2,1,0:T(8,128)(2,1)S(1)}, bf16[4,384,512]{2,1,0:T(8,128)(2,1)S(1)}) custom-call(s32[3]{0:T(128)S(1)} %pad_add_fusion.refs_0_.place, bf16[384,3072]{1,0:T(8,128)(2,1)S(1)} %get-tuple-element.69.refs_1_, bf16[384,3072]{1,0:T(8,128)(2,1)S(1)} %collective-permute-done.8.refs_2_, ...), custom_call_target="tpu_custom_call" | custom-call | flops 2415919 | bytes 4521 | tf_op jit(solution)/shard_map/pallas_call | solution.py:157
  77.3 0.8 collective-permute-start.21
  78.1 5.1 %shard_map.119 = (bf16[2,48,3072]{2,1,0:T(8,128)(2,1)S(1)}, bf16[2,48,3072]{2,1,0:T(8,128)(2,1)S(1)}, bf16[2,2,48,3072]{3,2,1,0:T(8,128)(2,1)S(1)}, bf16[2,2,48,...) custom-call(bf16[384,1024]{1,0:T(8,128)(2,1)S(1)} %get-tuple-element.66.refs_2_.refs_3_.refs_0_, ...), custom_call_target="tpu_custom_call" | custom-call | flops 4831838 | bytes 10616 | tf_op jit(solution)/shard_map/pallas_call | solution.py:157
  83.2 0.1 collective-permute-start.12
  83.3 2.7 %collective-permute-start.13 = (bf16[2,48,3072]{2,1,0:T(8,128)(2,1)S(1)}, bf16[2,48,3072]{2,1,0:T(8,128)(2,1)S(1)}, u32[]{:S(2)}, u32[]{:S(2)}) collective-permute-start(bf16[2,48,3072]{2,1,0:T(8,128)(2,1)S(1)} %get-tuple-element.78), channel_id=1, source_target_pairs={{0,3},{1,0},{2,1},{3,2},{4,7},{5,4},{6,5},{7,6},{8,11},{9,8},{10,9... | collective-permute-start | bytes 1769480 | tf_op jit(solution)/shard_map/ppermute | solution.py:43
  85.9 2.0 %shard_map.120 = (bf16[2,384,512]{2,1,0:T(8,128)(2,1)S(1)}, bf16[2,384,512]{2,1,0:T(8,128)(2,1)S(1)}) custom-call(s32[3]{0:T(128)S(1)} %pad_add_fusion.refs_0_.place, bf16[384,3072]{1,0:T(8,128)(2,1)S(1)} %shard_map.113.refs_1_, bf16[384,3072]{1,0:T(8,128)(2,1)S(1)} %collective-permute-done.10.refs_2_, ...), custom_call_target="tpu_custom_call" | custom-call | flops 1207959 | bytes 4325 | tf_op jit(solution)/shard_map/pallas_call | solution.py:157
  87.9 3.5 %shard_map.121 = (bf16[2,384,512]{2,1,0:T(8,128)(2,1)S(1)}, bf16[2,384,512]{2,1,0:T(8,128)(2,1)S(1)}, bf16[2,384,512]{2,1,0:T(8,128)(2,1)S(1)}, bf16[2,384,512]{2,1,0:T(8,128)(2,1)S(1)}) custom-call(s32[3]{0:T(128)S(1)} %pad_add_fusion.refs_0_.place, bf16[384,3072]{1,0:T(8,128)(2,1)S(1)} %shard_map.113.refs_1_, ...), custom_call_target="tpu_custom_call" | custom-call | flops 2415919 | bytes 5111 | tf_op jit(solution)/shard_map/pallas_call | solution.py:157
  91.5 1.6 collective-permute-done.15.refs_3_
  93.0 0.4 shard_map.122
  93.4 0.1 collective-permute-start.19
  93.5 2.7 %collective-permute-start.20 = (bf16[2,384,512]{2,1,0:T(8,128)(2,1)S(1)}, bf16[2,384,512]{2,1,0:T(8,128)(2,1)S(1)}, u32[]{:S(2)}, u32[]{:S(2)}) collective-permute-start(bf16[2,384,512]{2,1,0:T(8,128)(2,1)S(1)} %get-tuple-element.93), channel_id=1, source_target_pairs={{0,96},{1,97},{2,98},{3,99},{4,100},{5,101},{6,102},{7,103},{8,104... | collective-permute-start | bytes 2359304 | tf_op jit(solution)/shard_map/ppermute | solution.py:43
  96.1 2.5 %collective-permute-done.12.refs_1_ = bf16[2,48,3072]{2,1,0:T(8,128)(2,1)S(1)} collective-permute-done((bf16[2,48,3072]{2,1,0:T(8,128)(2,1)S(1)}, bf16[2,48,3072]{2,1,0:T(8,128)(2,1)S(1)}, u32[]{:S(2)}, u32[]{:S(2)}) %collective-permute-start.12) | collective-permute-done | bytes 589856 | tf_op jit(solution)/shard_map/ppermute | solution.py:43
  98.6 0.3 shard_map.123
  98.9 0.1 collective-permute-start.16
  99.0 2.7 %collective-permute-start.17 = (bf16[2,2,48,3072]{3,2,1,0:T(8,128)(2,1)S(1)}, bf16[2,2,48,3072]{3,2,1,0:T(8,128)(2,1)S(1)}, u32[]{:S(2)}, u32[]{:S(2)}) collective-permute-start(bf16[2,2,48,3072]{3,2,1,0:T(8,128)(2,1)S(1)} %get-tuple-element.85), channel_id=1, source_target_pairs={{0,3},{1,0},{2,1},{3,2},{4,7},{5,4},{6,5},{7,6},{8,11},{9,8},{10,9... | collective-permute-start | bytes 3538952 | tf_op jit(solution)/shard_map/ppermute | solution.py:43
  101.7 10.8 %collective-permute-done.19.refs_1_ = bf16[2,384,512]{2,1,0:T(8,128)(2,1)S(1)} collective-permute-done((bf16[2,384,512]{2,1,0:T(8,128)(2,1)S(1)}, bf16[2,384,512]{2,1,0:T(8,128)(2,1)S(1)}, u32[]{:S(2)}, u32[]{:S(2)}) %collective-permute-start.19) | collective-permute-done | bytes 786464 | tf_op jit(solution)/shard_map/ppermute | solution.py:43
  112.4 0.3 shard_map.126.refs_2_
  112.7 0.2 collective-permute-done.21.refs_1_
  112.9 0.4 shard_map.129
  113.2 0.1 collective-permute-start.26
  113.3 2.7 %collective-permute-start.27 = (bf16[192,512]{1,0:T(8,128)(2,1)S(1)}, bf16[192,512]{1,0:T(8,128)(2,1)S(1)}, u32[]{:S(2)}, u32[]{:S(2)}) collective-permute-start(bf16[192,512]{1,0:T(8,128)(2,1)S(1)} %get-tuple-element.106), channel_id=1, source_target_pairs={{0,96},{1,97},{2,98},{3,99},{4,100},{5,101},{6,102},{7,103},{8,104... | collective-permute-start | bytes 589832 | tf_op jit(solution)/shard_map/ppermute | solution.py:43
  116.0 0.7 collective-permute-start.24
  116.7 2.6 %collective-permute-done.26.refs_1_ = bf16[192,512]{1,0:T(8,128)(2,1)S(1)} collective-permute-done((bf16[192,512]{1,0:T(8,128)(2,1)S(1)}, bf16[192,512]{1,0:T(8,128)(2,1)S(1)}, u32[]{:S(2)}, u32[]{:S(2)}) %collective-permute-start.26) | collective-permute-done | bytes 196640 | tf_op jit(solution)/shard_map/ppermute | solution.py:43
  119.3 2.7 %collective-permute-start.23 = (bf16[2,384,512]{2,1,0:T(8,128)(2,1)S(1)}, bf16[2,384,512]{2,1,0:T(8,128)(2,1)S(1)}, u32[]{:S(2)}, u32[]{:S(2)}) collective-permute-start(bf16[2,384,512]{2,1,0:T(8,128)(2,1)S(1)} %get-tuple-element.96), channel_id=1, source_target_pairs={{0,96},{1,97},{2,98},{3,99},{4,100},{5,101},{6,102},{7,103},{8,104... | collective-permute-start | bytes 2359304 | tf_op jit(solution)/shard_map/ppermute | solution.py:43
  122.0 0.1 shard_map.130
  122.1 3.9 %collective-permute-done.16.refs_1_ = bf16[2,2,48,3072]{3,2,1,0:T(8,128)(2,1)S(1)} collective-permute-done((bf16[2,2,48,3072]{3,2,1,0:T(8,128)(2,1)S(1)}, bf16[2,2,48,3072]{3,2,1,0:T(8,128)(2,1)S(1)}, u32[]{:S(2)}, u32[]{:S(2)}) %collective-permute-start.16) | collective-permute-done | bytes 1179680 | tf_op jit(solution)/shard_map/ppermute | solution.py:43
  126.1 2.7 %collective-permute-start.29 = (bf16[2,192,512]{2,1,0:T(8,128)(2,1)S(1)}, bf16[2,192,512]{2,1,0:T(8,128)(2,1)S(1)}, u32[]{:S(2)}, u32[]{:S(2)}) collective-permute-start(bf16[2,192,512]{2,1,0:T(8,128)(2,1)S(1)} %get-tuple-element.108), channel_id=1, source_target_pairs={{0,96},{1,97},{2,98},{3,99},{4,100},{5,101},{6,102},{7,103},{8,104... | collective-permute-start | bytes 1179656 | tf_op jit(solution)/shard_map/ppermute | solution.py:43
  128.8 0.4 shard_map.124
  129.2 3.3 %collective-permute-done.24.refs_4_ = bf16[2,384,512]{2,1,0:T(8,128)(2,1)S(1)} collective-permute-done((bf16[2,384,512]{2,1,0:T(8,128)(2,1)S(1)}, bf16[2,384,512]{2,1,0:T(8,128)(2,1)S(1)}, u32[]{:S(2)}, u32[]{:S(2)}) %collective-permute-start.24) | collective-permute-done | bytes 786464 | tf_op jit(solution)/shard_map/ppermute | solution.py:43
  132.4 0.6 collective-permute-start.18
  133.1 3.6 %collective-permute-done.22.refs_2_ = bf16[2,384,512]{2,1,0:T(8,128)(2,1)S(1)} collective-permute-done((bf16[2,384,512]{2,1,0:T(8,128)(2,1)S(1)}, bf16[2,384,512]{2,1,0:T(8,128)(2,1)S(1)}, u32[]{:S(2)}, u32[]{:S(2)}) %collective-permute-start.22) | collective-permute-done | bytes 786464 | tf_op jit(solution)/shard_map/ppermute | solution.py:43
  136.7 1.3 shard_map.127
  138.1 7.3 %collective-permute-start.25 = (bf16[2,192,512]{2,1,0:T(8,128)(2,1)S(1)}, bf16[2,192,512]{2,1,0:T(8,128)(2,1)S(1)}, u32[]{:S(2)}, u32[]{:S(2)}) collective-permute-start(bf16[2,192,512]{2,1,0:T(8,128)(2,1)S(1)} %get-tuple-element.99), channel_id=1, source_target_pairs={{0,8},{1,9},{2,10},{3,11},{4,12},{5,13},{6,14},{7,15},{8,0},{9,1},... | collective-permute-start | bytes 1179656 | tf_op jit(solution)/shard_map/ppermute | solution.py:43
  145.4 0.8 shard_map.131
  146.2 3.6 %collective-permute-start.30 = (bf16[1,192,512]{2,1,0:T(8,128)(2,1)S(1)}, bf16[1,192,512]{2,1,0:T(8,128)(2,1)S(1)}, u32[]{:S(2)}, u32[]{:S(2)}) collective-permute-start(bf16[1,192,512]{2,1,0:T(8,128)(2,1)S(1)} %get-tuple-element.110), channel_id=1, source_target_pairs={{0,8},{1,9},{2,10},{3,11},{4,12},{5,13},{6,14},{7,15},{8,0},{9,1},... | collective-permute-start | bytes 589832 | tf_op jit(solution)/shard_map/ppermute | solution.py:43
  149.8 1.1 collective-permute-done.30.got
  150.9 1.3 shard_map.132
  152.3 1.7 %shard_map.125 = (bf16[128,3072]{1,0:T(8,128)(2,1)}, bf16[128,3072]{1,0:T(8,128)(2,1)}) custom-call(s32[2,128]{1,0:T(2,128)S(1)} %bitcast.11, f32[1,128]{1,0:T(1,128)S(1)} %bitcast.13, bf16[2,48,3072]{2,1,0:T(8,128)(2,1)S(1)} %get-tuple-element.86.kept, bf16[2,48,3072]{2,1,0:T(8,128)(2,1)S(1)} %collective-permute-done.18.got), custom_call_target="tpu_custom_call" | custom-call | flops 75497 | bytes 2800 | tf_op jit(solution)/shard_map/pallas_call | solution.py:133
  154.0 1.5 shard_map.128
  (26 shorter events, 0.1 us)
Async XLA Ops:
  2.4 17.6 %collective-permute-start.2 = (bf16[2,48,3072]{2,1,0:T(8,128)(2,1)S(1)}, bf16[2,48,3072]{2,1,0:T(8,128)(2,1)S(1)}, u32[]{:S(2)}, u32[]{:S(2)}) collective-permute-start(bf16[2,48,3072]{2,1,0:T(8,128)(2,1)S(1)} %shard_map.110.refs_6_.refs_7_), channel_id=1, source_target_pairs={{0,4},{1,5},{2,6},{3,7},{4,0},{5,1},{6,2},{7,3},{8,12},{9,13},{10,... | collective-permute-start | bytes 1769480 | tf_op jit(solution)/shard_map/ppermute | solution.py:43
  6.9 14.4 %collective-permute-start.3 = (bf16[2,48,3072]{2,1,0:T(8,128)(2,1)S(1)}, bf16[2,48,3072]{2,1,0:T(8,128)(2,1)S(1)}, u32[]{:S(2)}, u32[]{:S(2)}) collective-permute-start(bf16[2,48,3072]{2,1,0:T(8,128)(2,1)S(1)} %shard_map.110.refs_6_.refs_7_), channel_id=1, source_target_pairs={{0,3},{1,0},{2,1},{3,2},{4,7},{5,4},{6,5},{7,6},{8,11},{9,8},{10,9... | collective-permute-start | bytes 1769480 | tf_op jit(solution)/shard_map/ppermute | solution.py:43
  9.6 15.1 %collective-permute-start = (bf16[2,48,3072]{2,1,0:T(8,128)(2,1)S(1)}, bf16[2,48,3072]{2,1,0:T(8,128)(2,1)S(1)}, u32[]{:S(2)}, u32[]{:S(2)}) collective-permute-start(bf16[2,48,3072]{2,1,0:T(8,128)(2,1)S(1)} %shard_map.110.refs_6_.refs_7_), channel_id=1, source_target_pairs={{0,1},{1,2},{2,3},{3,0},{4,5},{5,6},{6,7},{7,4},{8,9},{9,10},{10,1... | collective-permute-start | bytes 1769480 | tf_op jit(solution)/shard_map/ppermute | solution.py:43
  21.3 14.2 %collective-permute-start.4 = (bf16[2,48,3072]{2,1,0:T(8,128)(2,1)S(1)}, bf16[2,48,3072]{2,1,0:T(8,128)(2,1)S(1)}, u32[]{:S(2)}, u32[]{:S(2)}) collective-permute-start(bf16[2,48,3072]{2,1,0:T(8,128)(2,1)S(1)} %collective-permute-done.2.refs_4_.refs_7_.refs_8_), channel_id=1, source_target_pairs={{0,3},{1,0},{2,1},{3,2},{4,7},{5,4},{6,5},{7,6},{8,11},{9,8},{10,9... | collective-permute-start | bytes 1769480 | tf_op jit(solution)/shard_map/ppermute | solution.py:43
  24.7 14.2 %collective-permute-start.5 = (bf16[2,48,3072]{2,1,0:T(8,128)(2,1)S(1)}, bf16[2,48,3072]{2,1,0:T(8,128)(2,1)S(1)}, u32[]{:S(2)}, u32[]{:S(2)}) collective-permute-start(bf16[2,48,3072]{2,1,0:T(8,128)(2,1)S(1)} %collective-permute-done.refs_4_.refs_5_), channel_id=1, source_target_pairs={{0,4},{1,5},{2,6},{3,7},{4,0},{5,1},{6,2},{7,3},{8,12},{9,13},{10,... | collective-permute-start | bytes 1769480 | tf_op jit(solution)/shard_map/ppermute | solution.py:43
  25.3 22.4 %collective-permute-start.1 = (bf16[2,48,3072]{2,1,0:T(8,128)(2,1)S(1)}, bf16[2,48,3072]{2,1,0:T(8,128)(2,1)}, u32[]{:S(2)}, u32[]{:S(2)}) collective-permute-start(bf16[2,48,3072]{2,1,0:T(8,128)(2,1)S(1)} %collective-permute-done.refs_4_.refs_5_), channel_id=1, source_target_pairs={{0,1},{1,2},{2,3},{3,0},{4,5},{5,6},{6,7},{7,4},{8,9},{9,10},{10,1... | collective-permute-start | bytes 1769480 | tf_op jit(solution)/shard_map/ppermute | solution.py:43
  39.7 8.0 %collective-permute-start.7 = (bf16[48,3072]{1,0:T(8,128)(2,1)}, bf16[48,3072]{1,0:T(8,128)(2,1)}, u32[]{:S(2)}, u32[]{:S(2)}) collective-permute-start(bf16[48,3072]{1,0:T(8,128)(2,1)} %get-tuple-element.61), channel_id=1, source_target_pairs={{0,3},{1,0},{2,1},{3,2},{4,7},{5,4},{6,5},{7,6},{8,11},{9,8},{10,9... | collective-permute-start | bytes 884744 | tf_op jit(solution)/shard_map/ppermute | solution.py:43
  40.0 18.6 %collective-permute-start.6 = (bf16[48,3072]{1,0:T(8,128)(2,1)}, bf16[48,3072]{1,0:T(8,128)(2,1)}, u32[]{:S(2)}, u32[]{:S(2)}) collective-permute-start(bf16[48,3072]{1,0:T(8,128)(2,1)} %get-tuple-element.59), channel_id=1, source_target_pairs={{0,1},{1,2},{2,3},{3,0},{4,5},{5,6},{6,7},{7,4},{8,9},{9,10},{10,1... | collective-permute-start | bytes 884744 | tf_op jit(solution)/shard_map/ppermute | solution.py:43
  49.0 19.2 %collective-permute-start.10 = (bf16[384,3072]{1,0:T(8,128)(2,1)S(1)}, bf16[384,3072]{1,0:T(8,128)(2,1)S(1)}, u32[]{:S(2)}, u32[]{:S(2)}) collective-permute-start(bf16[384,3072]{1,0:T(8,128)(2,1)S(1)} %shard_map.113.refs_1_), channel_id=1, source_target_pairs={{0,8},{1,9},{2,10},{3,11},{4,12},{5,13},{6,14},{7,15},{8,0},{9,1},... | collective-permute-start | bytes 7077896 | tf_op jit(solution)/shard_map/ppermute | solution.py:43
  62.5 10.6 %collective-permute-start.8 = (bf16[384,3072]{1,0:T(8,128)(2,1)S(1)}, bf16[384,3072]{1,0:T(8,128)(2,1)S(1)}, u32[]{:S(2)}, u32[]{:S(2)}) collective-permute-start(bf16[384,3072]{1,0:T(8,128)(2,1)S(1)} %get-tuple-element.69.refs_1_), channel_id=1, source_target_pairs={{0,8},{1,9},{2,10},{3,11},{4,12},{5,13},{6,14},{7,15},{8,0},{9,1},... | collective-permute-start | bytes 7077896 | tf_op jit(solution)/shard_map/ppermute | solution.py:43
  62.6 5.6 %collective-permute-start.11 = (bf16[2,384,512]{2,1,0:T(8,128)(2,1)S(1)}, bf16[2,384,512]{2,1,0:T(8,128)(2,1)S(1)}, u32[]{:S(2)}, u32[]{:S(2)}) collective-permute-start(bf16[2,384,512]{2,1,0:T(8,128)(2,1)S(1)} %get-tuple-element.71), channel_id=1, source_target_pairs={{0,8},{1,9},{2,10},{3,11},{4,12},{5,13},{6,14},{7,15},{8,0},{9,1},... | collective-permute-start | bytes 2359304 | tf_op jit(solution)/shard_map/ppermute | solution.py:43
  63.1 10.0 %collective-permute-start.9 = (bf16[384,512]{1,0:T(8,128)(2,1)S(1)}, bf16[384,512]{1,0:T(8,128)(2,1)S(1)}, u32[]{:S(2)}, u32[]{:S(2)}) collective-permute-start(bf16[384,512]{1,0:T(8,128)(2,1)S(1)} %get-tuple-element.70), channel_id=1, source_target_pairs={{0,8},{1,9},{2,10},{3,11},{4,12},{5,13},{6,14},{7,15},{8,0},{9,1},... | collective-permute-start | bytes 1179656 | tf_op jit(solution)/shard_map/ppermute | solution.py:43
  70.6 20.9 %collective-permute-start.14 = (bf16[2,384,512]{2,1,0:T(8,128)(2,1)S(1)}, bf16[2,384,512]{2,1,0:T(8,128)(2,1)S(1)}, u32[]{:S(2)}, u32[]{:S(2)}) collective-permute-start(bf16[2,384,512]{2,1,0:T(8,128)(2,1)S(1)} %get-tuple-element.80), channel_id=1, source_target_pairs={{0,96},{1,97},{2,98},{3,99},{4,100},{5,101},{6,102},{7,103},{8,104... | collective-permute-start | bytes 2359304 | tf_op jit(solution)/shard_map/ppermute | solution.py:43
  73.1 19.9 %collective-permute-start.15 = (bf16[2,384,512]{2,1,0:T(8,128)(2,1)S(1)}, bf16[2,384,512]{2,1,0:T(8,128)(2,1)S(1)}, u32[]{:S(2)}, u32[]{:S(2)}) collective-permute-start(bf16[2,384,512]{2,1,0:T(8,128)(2,1)S(1)} %get-tuple-element.72.refs_5_), channel_id=1, source_target_pairs={{0,32},{1,33},{2,34},{3,35},{4,36},{5,37},{6,38},{7,39},{8,40},{9,... | collective-permute-start | bytes 2359304 | tf_op jit(solution)/shard_map/ppermute | solution.py:43
  77.3 35.6 %collective-permute-start.21 = (bf16[4,384,512]{2,1,0:T(8,128)(2,1)S(1)}, bf16[4,384,512]{2,1,0:T(8,128)(2,1)S(1)}, u32[]{:S(2)}, u32[]{:S(2)}) collective-permute-start(bf16[4,384,512]{2,1,0:T(8,128)(2,1)S(1)} %get-tuple-element.94), channel_id=1, source_target_pairs={{0,16},{1,17},{2,18},{3,19},{4,20},{5,21},{6,22},{7,23},{8,24},{9,... | collective-permute-start | bytes 4718600 | tf_op jit(solution)/shard_map/ppermute | solution.py:43
  83.2 15.4 %collective-permute-start.12 = (bf16[2,48,3072]{2,1,0:T(8,128)(2,1)S(1)}, bf16[2,48,3072]{2,1,0:T(8,128)(2,1)S(1)}, u32[]{:S(2)}, u32[]{:S(2)}) collective-permute-start(bf16[2,48,3072]{2,1,0:T(8,128)(2,1)S(1)} %get-tuple-element.76), channel_id=1, source_target_pairs={{0,1},{1,2},{2,3},{3,0},{4,5},{5,6},{6,7},{7,4},{8,9},{9,10},{10,1... | collective-permute-start | bytes 1769480 | tf_op jit(solution)/shard_map/ppermute | solution.py:43
  83.3 15.4 %collective-permute-start.13 = (bf16[2,48,3072]{2,1,0:T(8,128)(2,1)S(1)}, bf16[2,48,3072]{2,1,0:T(8,128)(2,1)S(1)}, u32[]{:S(2)}, u32[]{:S(2)}) collective-permute-start(bf16[2,48,3072]{2,1,0:T(8,128)(2,1)S(1)} %get-tuple-element.78), channel_id=1, source_target_pairs={{0,3},{1,0},{2,1},{3,2},{4,7},{5,4},{6,5},{7,6},{8,11},{9,8},{10,9... | collective-permute-start | bytes 1769480 | tf_op jit(solution)/shard_map/ppermute | solution.py:43
  93.4 19.0 %collective-permute-start.19 = (bf16[2,384,512]{2,1,0:T(8,128)(2,1)S(1)}, bf16[2,384,512]{2,1,0:T(8,128)(2,1)S(1)}, u32[]{:S(2)}, u32[]{:S(2)}) collective-permute-start(bf16[2,384,512]{2,1,0:T(8,128)(2,1)S(1)} %get-tuple-element.92.refs_6_), channel_id=1, source_target_pairs={{0,32},{1,33},{2,34},{3,35},{4,36},{5,37},{6,38},{7,39},{8,40},{9,... | collective-permute-start | bytes 2359304 | tf_op jit(solution)/shard_map/ppermute | solution.py:43
  93.5 19.0 %collective-permute-start.20 = (bf16[2,384,512]{2,1,0:T(8,128)(2,1)S(1)}, bf16[2,384,512]{2,1,0:T(8,128)(2,1)S(1)}, u32[]{:S(2)}, u32[]{:S(2)}) collective-permute-start(bf16[2,384,512]{2,1,0:T(8,128)(2,1)S(1)} %get-tuple-element.93), channel_id=1, source_target_pairs={{0,96},{1,97},{2,98},{3,99},{4,100},{5,101},{6,102},{7,103},{8,104... | collective-permute-start | bytes 2359304 | tf_op jit(solution)/shard_map/ppermute | solution.py:43
  98.9 27.1 %collective-permute-start.16 = (bf16[2,2,48,3072]{3,2,1,0:T(8,128)(2,1)S(1)}, bf16[2,2,48,3072]{3,2,1,0:T(8,128)(2,1)S(1)}, u32[]{:S(2)}, u32[]{:S(2)}) collective-permute-start(bf16[2,2,48,3072]{3,2,1,0:T(8,128)(2,1)S(1)} %get-tuple-element.84), channel_id=1, source_target_pairs={{0,1},{1,2},{2,3},{3,0},{4,5},{5,6},{6,7},{7,4},{8,9},{9,10},{10,1... | collective-permute-start | bytes 3538952 | tf_op jit(solution)/shard_map/ppermute | solution.py:43
  99.0 27.1 %collective-permute-start.17 = (bf16[2,2,48,3072]{3,2,1,0:T(8,128)(2,1)S(1)}, bf16[2,2,48,3072]{3,2,1,0:T(8,128)(2,1)S(1)}, u32[]{:S(2)}, u32[]{:S(2)}) collective-permute-start(bf16[2,2,48,3072]{3,2,1,0:T(8,128)(2,1)S(1)} %get-tuple-element.85), channel_id=1, source_target_pairs={{0,3},{1,0},{2,1},{3,2},{4,7},{5,4},{6,5},{7,6},{8,11},{9,8},{10,9... | collective-permute-start | bytes 3538952 | tf_op jit(solution)/shard_map/ppermute | solution.py:43
  113.2 6.1 %collective-permute-start.26 = (bf16[192,512]{1,0:T(8,128)(2,1)S(1)}, bf16[192,512]{1,0:T(8,128)(2,1)S(1)}, u32[]{:S(2)}, u32[]{:S(2)}) collective-permute-start(bf16[192,512]{1,0:T(8,128)(2,1)S(1)} %get-tuple-element.104), channel_id=1, source_target_pairs={{0,32},{1,33},{2,34},{3,35},{4,36},{5,37},{6,38},{7,39},{8,40},{9,... | collective-permute-start | bytes 589832 | tf_op jit(solution)/shard_map/ppermute | solution.py:43
  113.3 6.0 %collective-permute-start.27 = (bf16[192,512]{1,0:T(8,128)(2,1)S(1)}, bf16[192,512]{1,0:T(8,128)(2,1)S(1)}, u32[]{:S(2)}, u32[]{:S(2)}) collective-permute-start(bf16[192,512]{1,0:T(8,128)(2,1)S(1)} %get-tuple-element.106), channel_id=1, source_target_pairs={{0,96},{1,97},{2,98},{3,99},{4,100},{5,101},{6,102},{7,103},{8,104... | collective-permute-start | bytes 589832 | tf_op jit(solution)/shard_map/ppermute | solution.py:43
  116.0 16.4 %collective-permute-start.24 = (bf16[2,384,512]{2,1,0:T(8,128)(2,1)S(1)}, bf16[2,384,512]{2,1,0:T(8,128)(2,1)S(1)}, u32[]{:S(2)}, u32[]{:S(2)}) collective-permute-start(bf16[2,384,512]{2,1,0:T(8,128)(2,1)S(1)} %shard_map.126.refs_2_), channel_id=1, source_target_pairs={{0,16},{1,17},{2,18},{3,19},{4,20},{5,21},{6,22},{7,23},{8,24},{9,... | collective-permute-start | bytes 2359304 | tf_op jit(solution)/shard_map/ppermute | solution.py:43
  119.3 17.4 %collective-permute-start.22 = (bf16[2,384,512]{2,1,0:T(8,128)(2,1)S(1)}, bf16[2,384,512]{2,1,0:T(8,128)(2,1)S(1)}, u32[]{:S(2)}, u32[]{:S(2)}) collective-permute-start(bf16[2,384,512]{2,1,0:T(8,128)(2,1)S(1)} %get-tuple-element.95.refs_4_), channel_id=1, source_target_pairs={{0,32},{1,33},{2,34},{3,35},{4,36},{5,37},{6,38},{7,39},{8,40},{9,... | collective-permute-start | bytes 2359304 | tf_op jit(solution)/shard_map/ppermute | solution.py:43
  119.3 17.4 %collective-permute-start.23 = (bf16[2,384,512]{2,1,0:T(8,128)(2,1)S(1)}, bf16[2,384,512]{2,1,0:T(8,128)(2,1)S(1)}, u32[]{:S(2)}, u32[]{:S(2)}) collective-permute-start(bf16[2,384,512]{2,1,0:T(8,128)(2,1)S(1)} %get-tuple-element.96), channel_id=1, source_target_pairs={{0,96},{1,97},{2,98},{3,99},{4,100},{5,101},{6,102},{7,103},{8,104... | collective-permute-start | bytes 2359304 | tf_op jit(solution)/shard_map/ppermute | solution.py:43
  126.1 19.3 %collective-permute-start.28 = (bf16[2,192,512]{2,1,0:T(8,128)(2,1)S(1)}, bf16[2,192,512]{2,1,0:T(8,128)(2,1)S(1)}, u32[]{:S(2)}, u32[]{:S(2)}) collective-permute-start(bf16[2,192,512]{2,1,0:T(8,128)(2,1)S(1)} %get-tuple-element.107), channel_id=1, source_target_pairs={{0,32},{1,33},{2,34},{3,35},{4,36},{5,37},{6,38},{7,39},{8,40},{9,... | collective-permute-start | bytes 1179656 | tf_op jit(solution)/shard_map/ppermute | solution.py:43
  126.1 19.3 %collective-permute-start.29 = (bf16[2,192,512]{2,1,0:T(8,128)(2,1)S(1)}, bf16[2,192,512]{2,1,0:T(8,128)(2,1)S(1)}, u32[]{:S(2)}, u32[]{:S(2)}) collective-permute-start(bf16[2,192,512]{2,1,0:T(8,128)(2,1)S(1)} %get-tuple-element.108), channel_id=1, source_target_pairs={{0,96},{1,97},{2,98},{3,99},{4,100},{5,101},{6,102},{7,103},{8,104... | collective-permute-start | bytes 1179656 | tf_op jit(solution)/shard_map/ppermute | solution.py:43
  132.4 19.8 %collective-permute-start.18 = (bf16[2,48,3072]{2,1,0:T(8,128)(2,1)S(1)}, bf16[2,48,3072]{2,1,0:T(8,128)(2,1)S(1)}, u32[]{:S(2)}, u32[]{:S(2)}) collective-permute-start(bf16[2,48,3072]{2,1,0:T(8,128)(2,1)S(1)} %get-tuple-element.87), channel_id=1, source_target_pairs={{0,4},{1,5},{2,6},{3,7},{4,0},{5,1},{6,2},{7,3},{8,12},{9,13},{10,... | collective-permute-start | bytes 1769480 | tf_op jit(solution)/shard_map/ppermute | solution.py:43
  138.0 14.2 %copy-start = (s32[128,2]{0,1:T(2,128)S(1)}, s32[128,2]{0,1:T(2,128)}, u32[]{:S(2)}) copy-start(s32[128,2]{0,1:T(2,128)} %param.9) | copy-start | bytes 3076
  138.1 14.2 %copy-start.1 = (f32[128]{0:T(128)S(1)}, f32[128]{0:T(128)}, u32[]{:S(2)}) copy-start(f32[128]{0:T(128)} %param.10) | copy-start | bytes 1540
  138.1 15.9 %collective-permute-start.25 = (bf16[2,192,512]{2,1,0:T(8,128)(2,1)S(1)}, bf16[2,192,512]{2,1,0:T(8,128)(2,1)S(1)}, u32[]{:S(2)}, u32[]{:S(2)}) collective-permute-start(bf16[2,192,512]{2,1,0:T(8,128)(2,1)S(1)} %get-tuple-element.99), channel_id=1, source_target_pairs={{0,8},{1,9},{2,10},{3,11},{4,12},{5,13},{6,14},{7,15},{8,0},{9,1},... | collective-permute-start | bytes 1179656 | tf_op jit(solution)/shard_map/ppermute | solution.py:43
  146.2 4.7 %collective-permute-start.30 = (bf16[1,192,512]{2,1,0:T(8,128)(2,1)S(1)}, bf16[1,192,512]{2,1,0:T(8,128)(2,1)S(1)}, u32[]{:S(2)}, u32[]{:S(2)}) collective-permute-start(bf16[1,192,512]{2,1,0:T(8,128)(2,1)S(1)} %get-tuple-element.110), channel_id=1, source_target_pairs={{0,8},{1,9},{2,10},{3,11},{4,12},{5,13},{6,14},{7,15},{8,0},{9,1},... | collective-permute-start | bytes 589832 | tf_op jit(solution)/shard_map/ppermute | solution.py:43
where the time goes:
time: 156 us; the launch traced here: 155 us
  waiting for transfers between devices  57.2 us (37%)
  starting transfers between devices  49.1 us (31%)
  Pallas kernels  48.2 us (31%)
    ppermute x31, waiting for transfers between devices, shift(): return lax.ppermute(value, ('dp', 'tensor'), pairs)  57.2 us
    ppermute x31, starting transfers between devices, shift(): return lax.ppermute(value, ('dp', 'tensor'), pairs)  49.1 us
    pallas_call x19, Pallas kernels, call(): pl.pallas_call(without(inputs, len(earlier), kernel), in_specs=[IN_SMEM]...  42 us
  transfers between devices with their start and end apart: 31, of which 14 were waited for; matrix products, arithmetic and copies ran while one was open for 0% of the time, Pallas kernels for 29%

commit v1 on v0

--- a/solution.py
+++ b/solution.py
@@ -150,7 +150,7 @@
     return run
 
 
-def call(kernel, scalars, arrays, shapes, flops, earlier=(), hbm=(), scratch=()):
+def call(kernel, scalars, arrays, shapes, flops, earlier=(), hbm=(), scratch=(), aliases=None):
     shapes = [s if isinstance(s[0], tuple) else (s, BF) for s in shapes]
     size = sum(a.size for a in arrays) + sum(math.prod(s) for s, _ in shapes)
     inputs = len(scalars) + len(arrays) + len(hbm)
@@ -163,16 +163,18 @@
         out_specs=[IN_VMEM] * len(shapes),
         out_shape=[pltpu.VMEM(s, t) for s, t in shapes],
         scratch_shapes=list(scratch),
+        input_output_aliases=aliases or {},
         compiler_params=params(),
         cost_estimate=cost(flops, size),
     )(*scalars, *arrays, *map(in_hbm, hbm), *earlier)
 
 
 def stage_kernel(n, *refs):
-    sems = refs[-1]
+    *refs, token, sems = refs
     copies = [pltpu.make_async_copy(refs[i], refs[n + i], sems.at[i]) for i in range(n)]
     for copy in copies:
         copy.start()
+    token[...] = jnp.zeros_like(token)
     for copy in copies:
         copy.wait()
 
@@ -182,7 +184,7 @@
         functools.partial(stage_kernel, len(arrays)),
         [],
         [],
-        [a.shape for a in arrays],
+        [a.shape for a in arrays] + [((8, 128), F32)],
         1,
         earlier,
         hbm=arrays,
@@ -190,21 +192,32 @@
     )
 
 
+def place_of():
+    dp = lax.axis_index("dp")
+    return dp % 2, (dp // 2) % 2, dp // 4
+
+
 def half(h):
     return pl.ds(pl.multiple_of(h * HALF, HALF), HALF)
 
 
-def gather(which, chunks, rows):
+def pack_kernel(*refs):
+    *chunks, out = refs
     for k, chunk in enumerate(chunks):
-        rows[k * SLOTS : (k + 1) * SLOTS] = chunk[...] if len(chunk.shape) == 2 else chunk[which]
-
-
-def gather_kernel(*refs):
-    gather(0, refs[:8], refs[8])
-
-
-def gather_rows(chunks, *earlier):
-    return call(gather_kernel, [], chunks, [(ROWS, DW)], 1, earlier)[0]
+        out[:, k * SLOTS : (k + 1) * SLOTS] = chunk[...]
+
+
+def pack(*chunks, earlier=()):
+    return call(pack_kernel, [], chunks, [(2, SLOTS * len(chunks), DW)], 1, earlier)[0]
+
+
+def pair_kernel(x, d, out):
+    out[0] = x[...]
+    out[1] = d[...]
+
+
+def pair(x, d):
+    return call(pair_kernel, [], [x, d], [(2, SLOTS, DW)], 1)[0]
 
 
 def split_kernel(a, b, x, d):
@@ -212,43 +225,94 @@
     d[...] = b[1]
 
 
-def split(a, b):
-    return call(split_kernel, [], [a, b], [(SLOTS, DW)] * 2, 1)
-
-
-def gate_kernel(core, rows, w_gate, w_up, hidden, sent, act, slope):
+def split(a, b, *earlier):
+    return call(split_kernel, [], [a, b], [(SLOTS, DW)] * 2, 1, earlier)
+
+
+FIRST = ROWS - SLOTS
+
+
+def gate_rows(r, rows, w_gate, w_up, hidden, act, slope):
     for h in range(2):
         at = slice(h * HALF, (h + 1) * HALF)
         gate = dot(rows[...], w_gate[:, at])
         up = dot(rows[...], w_up[:, at])
         s = jax.nn.sigmoid(gate)
         silu = gate * s
-        act[:, at] = silu
-        slope[:, at] = up * s * (1.0 + gate * (1.0 - s))
-        hidden[:, at] = (silu * up).astype(BF)
-    sent[...] = hidden[:, half(1 - core[0])]
-
-
-def gate_up(core, rows, w_gate, w_up):
-    shapes = [(ROWS, FF), (ROWS, HALF), ((ROWS, FF), F32), ((ROWS, FF), F32)]
-    return call(gate_kernel, [core], [rows, w_gate, w_up], shapes, 4 * ROWS * DW * FF)
-
-
-def back_kernel(core, *refs):
-    chunks, (w_down, act, slope, rows, d_gate, d_up, sent) = refs[:8], refs[8:]
-    gather(1, chunks, rows)
-    for h in range(2):
-        at = slice(h * HALF, (h + 1) * HALF)
-        d_hidden = dot_t(rows[...], w_down[at, :])
-        d_up[:, at] = (d_hidden * act[:, at]).astype(BF)
-        d_gate[:, at] = (d_hidden * slope[:, at]).astype(BF)
-    sent[0] = d_gate[:, half(1 - core[0])]
-    sent[1] = d_up[:, half(1 - core[0])]
-
-
-def back_hidden(core, chunks, w_down, act, slope):
-    shapes = [(ROWS, DW), (ROWS, FF), (ROWS, FF), (2, ROWS, HALF)]
-    return call(back_kernel, [core], [*chunks, w_down, act, slope], shapes, 2 * ROWS * DW * FF)
+        act[r, at] = silu
+        slope[r, at] = up * s * (1.0 + gate * (1.0 - s))
+        hidden[r, at] = (silu * up).astype(BF)
+
+
+GATE_SHAPES = [(ROWS, FF), ((ROWS, FF), F32), ((ROWS, FF), F32)]
+
+
+def gate_first_kernel(a, b, w_gate, w_up, hidden, act, slope, rows):
+    n = a.shape[1]
+    rows[:n] = a[0]
+    rows[n:] = b[0]
+    gate_rows(slice(0, FIRST), rows, w_gate, w_up, hidden, act, slope)
+
+
+def gate_first(a, b, w_gate, w_up, *earlier):
+    return call(
+        gate_first_kernel,
+        [],
+        [a, b, w_gate, w_up],
+        GATE_SHAPES,
+        4 * FIRST * DW * FF,
+        earlier,
+        scratch=[pltpu.VMEM((FIRST, DW), BF)],
+    )
+
+
+def gate_last_kernel(chunk, w_gate, w_up, *refs):
+    hidden, act, slope = refs[3:]
+    gate_rows(slice(FIRST, ROWS), chunk, w_gate, w_up, hidden, act, slope)
+
+
+def gate_last(chunk, w_gate, w_up, first, *earlier):
+    return call(
+        gate_last_kernel,
+        [],
+        [chunk, w_gate, w_up, *first],
+        GATE_SHAPES,
+        4 * SLOTS * DW * FF,
+        earlier,
+        aliases={3 + k: k for k in range(3)},
+    )
+
+
+def back_half(mine, rows, w_down, act, slope, out):
+    at = half(mine)
+    d_hidden = dot_t(rows[...], w_down[at, :])
+    out[0] = (d_hidden * slope[:, at]).astype(BF)
+    out[1] = (d_hidden * act[:, at]).astype(BF)
+
+
+def back_other_kernel(a, b, last, w_down, hidden, act, slope, rows, out):
+    n = a.shape[1]
+    rows[:n] = a[1]
+    rows[n:FIRST] = b[1]
+    rows[FIRST:] = last[...]
+    other = 1 - place_of()[0]
+    out[2] = hidden[:, half(other)]
+    back_half(other, rows, w_down, act, slope, out)
+
+
+def back_other(a, b, last, w_down, hidden, act, slope):
+    arrays = [a, b, last, w_down, hidden, act, slope]
+    shapes = [(ROWS, DW), (3, ROWS, HALF)]
+    return call(back_other_kernel, [], arrays, shapes, ROWS * DW * FF)
+
+
+def back_own_kernel(rows, w_down, act, slope, out):
+    back_half(place_of()[0], rows, w_down, act, slope, out)
+
+
+def back_own(rows, w_down, act, slope):
+    shapes = [(2, ROWS, HALF)]
+    return call(back_own_kernel, [], [rows, w_down, act, slope], shapes, ROWS * DW * FF)[0]
 
 
 def out_kernel(hidden, w_down, out):
@@ -261,25 +325,31 @@
     return call(out_kernel, [], [hidden, w_down], [(ROWS, DW)], 2 * ROWS * DW * FF, earlier)[0]
 
 
-def token_kernel(d_gate, d_up, w_gate, w_up, out, far_a, far_b, above, below, own):
-    targets = [far_a, far_b] + [t.at[dz] for t in (above, below, own) for dz in range(2)]
+def token_kernel(mine, other, w_gate, w_up, out, far_a, far_b, above, below, own):
+    targets = [above.at[0], below.at[0], own.at[0], own.at[1], far_a, above.at[1], below.at[1], far_b]
+    core = place_of()[0]
     for j in range(0, DW, 768):
         at = slice(j, j + 768)
-        back = dot_t(d_gate[...], w_gate[at, :]) + dot_t(d_up[...], w_up[at, :])
+        back = sum(
+            dot_t(d[m], w[at, half(h)])
+            for d, h in ((mine, core), (other, 1 - core))
+            for m, w in enumerate((w_gate, w_up))
+        )
         for k, target in enumerate(targets):
             rows = slice(k * SLOTS, (k + 1) * SLOTS)
             target[0, :, at] = out[rows, at]
             target[1, :, at] = back[rows].astype(BF)
 
 
-def row_terms(d_gate, d_up, w_gate, w_up, out, *earlier):
+def row_terms(mine, other, w_gate, w_up, out, *earlier):
     shapes = [(2, SLOTS, DW)] * 2 + [(2, 2, SLOTS, DW)] * 3
-    arrays = [d_gate, d_up, w_gate, w_up, out]
-    return call(token_kernel, [], arrays, shapes, 4 * ROWS * DW * FF, earlier)
-
-
-def both(own, other):
-    return jnp.concatenate([own, other], axis=0)
+    return call(
+        token_kernel, [], [mine, other, w_gate, w_up, out], shapes, 4 * ROWS * DW * FF, earlier
+    )
+
+
+def both(*rows):
+    return jnp.concatenate(rows, axis=0)
 
 
 def features(place, dx):
@@ -299,17 +369,21 @@
         second[...] = low
 
 
-def grads_kernel(pairs, place, x_own, x_other, d_gate, d_up, got, *outs):
-    mine = half(place[0])
-    terms = [both(t[:, mine], got[m]) for m, t in enumerate((d_gate, d_up))]
-    outs = list(outs)
+def rows_at(which, parts, at):
+    return both(*(p[which, :, at] for p in parts))
+
+
+def grads_kernel(pairs, *refs):
+    x_parts, (mine, got, *outs) = refs[:6], refs[6:]
+    place = place_of()
+    terms = [both(mine[m], got[m]) for m in range(2)]
     for dx, dz in pairs:
         if dz is None:
             at = features(place, dx)
         else:
             at = ((place[2] + dx) % 4) * (2 * FEAT) + ((place[1] + dz) % 2) * FEAT
             at = pl.ds(pl.multiple_of(at, FEAT), FEAT)
-        x = both(x_own[:, at], x_other[:, at])
+        x = rows_at(0, x_parts, at)
         here = [outs.pop(0) for _ in range(2 if dz is None else 1)]
         for m in range(2):
             result = t_dot(x, terms[m]).astype(BF)
@@ -319,29 +393,31 @@
                 here[0][m] = result
 
 
-def gate_up_grads(place, pairs, x_own, x_other, d_gate, d_up, got, *earlier):
+def gate_up_grads(pairs, x_parts, mine, got, *earlier):
     n = sum(2 if dz is None else 1 for _, dz in pairs)
     return call(
         functools.partial(grads_kernel, pairs),
-        [place],
-        [x_own, x_other, d_gate, d_up, got],
+        [],
+        [*x_parts, mine, got],
         [(2, FEAT, HALF)] * n,
         n * ROWS * DW * FF / 2,
         earlier,
     )
 
 
-def down_kernel(place, d_own, d_other, hidden, got, kept, sent):
-    h = both(hidden[:, half(place[0])], got[...])
+def down_kernel(*refs):
+    d_parts, (hidden, got, kept, sent) = refs[:6], refs[6:]
+    place = place_of()
+    h = both(hidden[:, half(place[0])], got[2])
     for k, dx in enumerate((2, 1, 3, 0)):
         at = features(place, dx)
-        result = t_dot(both(d_own[:, at], d_other[:, at]), h).astype(BF)
+        result = t_dot(rows_at(1, d_parts, at), h).astype(BF)
         store_pair(place, kept.at[k], sent.at[k], result[:FEAT], result[FEAT:])
 
 
-def down_grads(place, d_own, d_other, hidden, got, *earlier):
+def down_grads(parts, hidden, got, *earlier):
     shapes = [(4, FEAT, HALF)] * 2
-    return call(down_kernel, [place], [d_own, d_other, hidden, got], shapes, 2 * ROWS * DW * FF, earlier)
+    return call(down_kernel, [], [*parts, hidden, got], shapes, 2 * ROWS * DW * FF, earlier)
 
 
 def add(*terms):
@@ -390,8 +466,9 @@
     return call(add_three_kernel, [], [own, above, below], [own.shape[1:]] * 2, 2 * own.size)
 
 
-def halves_kernel(place, *refs):
+def halves_kernel(*refs):
     *terms, mine, theirs = refs
+    place = place_of()
     total = add(*terms)
     low, high = total[:, : FEAT // 2], total[:, FEAT // 2 :]
 
@@ -406,12 +483,13 @@
         theirs[...] = low
 
 
-def halves(place, *terms):
+def halves(*terms):
     n = terms[0].shape[0]
-    return call(halves_kernel, [place], terms, [(n, FEAT // 2, HALF)] * 2, 2 * terms[0].size)
-
-
-def join_kernel(place, mine, got, *outs):
+    return call(halves_kernel, [], terms, [(n, FEAT // 2, HALF)] * 2, 2 * terms[0].size)
+
+
+def join_kernel(mine, got, *outs):
+    place = place_of()
     for k, out in enumerate(outs):
 
         @pl.when(place[0] == 0)
@@ -425,16 +503,16 @@
             out[:, HALF:] = mine[k]
 
 
-def join(place, mine, got):
+def join(mine, got):
     n = mine.shape[0]
     return pl.pallas_call(
         join_kernel,
-        in_specs=[IN_SMEM, IN_VMEM, IN_VMEM],
+        in_specs=[IN_VMEM, IN_VMEM],
         out_specs=[IN_VMEM] * n,
         out_shape=[jax.ShapeDtypeStruct((FEAT // 2, FF), BF)] * n,
         compiler_params=params(),
         cost_estimate=cost(mine.size, 8 * mine.size),
-    )(place, mine, got)
+    )(mine, got)
 
 
 def cut_kernel(kept, got, far_a, far_b, above, below, own):
@@ -456,44 +534,44 @@
 
 
 def local(tokens, cotangent, expert_ids, combine, w_gate, w_up, w_down):
-    dp = lax.axis_index("dp")
-    place = jnp.stack([dp % 2, (dp // 2) % 2, dp // 4]).astype(jnp.int32)
     ids, weight = expert_ids.T, combine.reshape(1, -1)
 
     sel = select(ids, weight, tokens, cotangent)
     zhi, up0, down0 = to_zhi(sel), to_y(sel, -1), to_y(sel, 1)
     far0, down1 = to_y(down0, 1), to_zhi(down0)
     up1 = to_y(after(zhi, up0), -1)
-    w_gate, w_up, w_down = stage([w_gate, w_up, w_down], up0, zhi)
-    x_far1, d_far1 = split(up1, down1)
+    w_gate, w_up, w_down, there = stage([w_gate, w_up, w_down], up0, zhi)
+    four = pack(up0, down0, sel, zhi, earlier=[there])
+    x_far1, d_far1 = split(up1, down1, there)
+    three = pack(far0, up1, down1)
+    first = gate_first(four, three, w_gate, w_up, x_far1)
     x_far1, d_far1 = to_y(x_far1, -1), to_y(d_far1, 1)
-    x_rows = gather_rows([far0, x_far1, up0, up1, down0, down1, sel, zhi])
-    x_other = to_core(x_rows)
-    hidden, hidden_sent, act, slope = gate_up(place, x_rows, w_gate, w_up)
-    hidden_got = to_core(hidden_sent)
-    d_chunks = [far0, d_far1, up0, up1, down0, down1, sel, zhi]
-    d_rows, d_gate, d_up, d_sent = back_hidden(place, d_chunks, w_down, act, slope)
+    four_other, three_other = to_core(four), to_core(three)
+    far1 = pair(x_far1, d_far1)
+    parts = [four, three, far1, four_other, three_other, to_core(far1)]
+    hidden, act, slope = gate_last(x_far1, w_gate, w_up, first, four_other, three_other)
+    d_rows, d_sent = back_other(four, three, d_far1, w_down, hidden, act, slope)
     d_got = to_core(d_sent)
-    d_other = to_core(d_rows)
-    out = out_terms(hidden, w_down, d_gate)
-
-    far_a, far_b = gate_up_grads(place, [(2, None)], x_rows, x_other, d_gate, d_up, d_got, out)
+    d_mine = back_own(d_rows, w_down, act, slope)
+
+    down_kept, down_sent = down_grads(parts, hidden, d_got, d_mine)
+    down_got = to_zlo(down_sent)
+    far_a, far_b = gate_up_grads([(2, None)], parts, d_mine, d_got, down_kept)
     far_got_a, far_got_b = to_x(far_a, 1), to_x(far_b, -1)
-    down_kept, down_sent = down_grads(place, d_rows, d_other, hidden, hidden_got, far_a)
-    down_got = to_zlo(down_sent)
+    out = out_terms(hidden, w_down, far_a)
     row_far_a, row_far_b, row_above, row_below, row_own = row_terms(
-        d_gate, d_up, w_gate, w_up, out, down_kept
+        d_mine, d_sent, w_gate, w_up, out
     )
     row_got_a, row_got_b = to_y(row_far_a, 1), to_y(row_far_b, -1)
-    above1, below1 = gate_up_grads(
-        place, [(1, 1), (3, 1)], x_rows, x_other, d_gate, d_up, d_got, row_own
-    )
+    above1, below1 = gate_up_grads([(1, 1), (3, 1)], parts, d_mine, d_got, row_own)
+    (below1,) = add_pairs(below1, far_got_b)
+    above1 = after(above1, below1)
     above0, below0, own0, own1 = gate_up_grads(
-        place, [(1, 0), (3, 0), (0, None)], x_rows, x_other, d_gate, d_up, d_got, above1
-    )
-    below1, above0 = add_pairs(below1, far_got_b, above0, far_got_a)
+        [(1, 0), (3, 0), (0, None)], parts, d_mine, d_got, below1
+    )
+    above1, below1 = to_x(above1, 1), to_x(below1, -1)
+    (above0,) = add_pairs(above0, far_got_a)
     row_above, row_below = add_into(row_above, row_got_a, row_below, row_got_b, above0)
-    above1, below1 = to_x(after(above1, above0), 1), to_x(below1, -1)
     row_above, row_below = to_y(row_above, 1), to_y(row_below, -1)
     sum1 = add_all(own1, above1, below1)
     far_a, far_b, above, below, down_own = cut(down_kept, down_got, sum1)
@@ -504,13 +582,13 @@
     row_kept, row_sent = add_three(row_own, row_above, row_below)
     row_got = to_zhi(row_sent)
     expert_output, token_grad = place_rows(ids, weight, row_kept, row_got)
-    mine, theirs = halves(place, own0, above0, below0, sum1)
-    gate_grad, up_grad = join(place, mine, to_core(theirs))
+    mine, theirs = halves(own0, above0, below0, sum1)
+    gate_grad, up_grad = join(mine, to_core(theirs))
     above, below = add_into(above, far_a, below, far_b)
     whole = lambda v: v.reshape(1, FEAT, HALF)
     above, below = whole(to_x(above, 1)), whole(to_x(below, -1))
-    mine, theirs = halves(place, down_own, above, below)
-    (down_grad,) = join(place, mine, to_core(theirs))
+    mine, theirs = halves(down_own, above, below)
+    (down_grad,) = join(mine, to_core(theirs))
     return (expert_output, token_grad, gate_grad, up_grad, down_grad.T)
 
 

time: 156 us -> 146 us (0.936)
  waiting for transfers between devices: 57.2 us -> 49.7 us
  Pallas kernels: 48.2 us -> 42 us
  starting transfers between devices: 49.1 us -> 52.9 us
    ppermute x31, waiting for transfers between devices: 57.2 us -> 49.7 us  [shift(): return lax.ppermute(value, ('dp', 'tensor'), pairs)]
    pallas_call x19 -> x24, Pallas kernels: 42 us -> 36.9 us  [call(): pl.pallas_call(without(inputs, len(earlier), kernel), in_specs=[IN_SMEM]...]
    ppermute x31, starting transfers between devices: 49.1 us -> 52.9 us  [shift(): return lax.ppermute(value, ('dp', 'tensor'), pairs)]
  transfers between devices with their start and end apart: 31 -> 31, of which waited for: 14 -> 16; matrix products, arithmetic and copies ran while one was open for 0% -> 0% of each run, Pallas kernels for 29% -> 22%
where the time goes in v1:
time: 146 us; the launch traced here: 145 us
  starting transfers between devices  52.9 us (36%)
  waiting for transfers between devices  49.7 us (34%)
  Pallas kernels  42 us (29%)
    ppermute x31, starting transfers between devices, shift(): return lax.ppermute(value, ('dp', 'tensor'), pairs)  52.9 us
    ppermute x31, waiting for transfers between devices, shift(): return lax.ppermute(value, ('dp', 'tensor'), pairs)  49.7 us
    pallas_call x24, Pallas kernels, call(): pl.pallas_call(without(inputs, len(earlier), kernel), in_specs=[IN_SMEM]...  36.9 us
  transfers between devices with their start and end apart: 31, of which 16 were waited for; matrix products, arithmetic and copies ran while one was open for 0% of the time, Pallas kernels for 22%

profile of v1, /device:TPU:1, one launch (start us, length us, event | category | flops | bytes accessed | tf_op | source)
XLA Modules:
  0.0 145.5 jit_solution(7863732070314564039)
XLA Ops:
  0.6 1.7 %shard_map.110.refs_2_ = bf16[2,48,3072]{2,1,0:T(8,128)(2,1)S(1)} custom-call(s32[2,128]{1,0:T(2,128)} %bitcast.7, f32[1,128]{1,0:T(1,128)} %bitcast.9, bf16[128,3072]{1,0:T(8,128)(2,1)} %x.1, bf16[128,3072]{1,0:T(8,128)(2,1)} %d.1), custom_call_target="tpu_custom_call" | custom-call | flops 75497 | bytes 2200 | tf_op jit(solution)/shard_map/pallas_call | solution.py:112
  2.4 4.5 %collective-permute-start.2 = (bf16[2,48,3072]{2,1,0:T(8,128)(2,1)S(1)}, bf16[2,48,3072]{2,1,0:T(8,128)(2,1)S(1)}, u32[]{:S(2)}, u32[]{:S(2)}) collective-permute-start(bf16[2,48,3072]{2,1,0:T(8,128)(2,1)S(1)} %shard_map.110.refs_2_), channel_id=1, source_target_pairs={{0,4},{1,5},{2,6},{3,7},{4,0},{5,1},{6,2},{7,3},{8,12},{9,13},{10,... | collective-permute-start | bytes 1769480 | tf_op jit(solution)/shard_map/ppermute | solution.py:43
  6.9 2.7 %collective-permute-start = (bf16[2,48,3072]{2,1,0:T(8,128)(2,1)S(1)}, bf16[2,48,3072]{2,1,0:T(8,128)(2,1)S(1)}, u32[]{:S(2)}, u32[]{:S(2)}) collective-permute-start(bf16[2,48,3072]{2,1,0:T(8,128)(2,1)S(1)} %shard_map.110.refs_2_), channel_id=1, source_target_pairs={{0,3},{1,0},{2,1},{3,2},{4,7},{5,4},{6,5},{7,6},{8,11},{9,8},{10,9... | collective-permute-start | bytes 1769480 | tf_op jit(solution)/shard_map/ppermute | solution.py:43
  9.6 10.3 %collective-permute-done.2.refs_4_.refs_3_ = bf16[2,48,3072]{2,1,0:T(8,128)(2,1)S(1)} collective-permute-done((bf16[2,48,3072]{2,1,0:T(8,128)(2,1)S(1)}, bf16[2,48,3072]{2,1,0:T(8,128)(2,1)S(1)}, u32[]{:S(2)}, u32[]{:S(2)}) %collective-permute-start.2) | collective-permute-done | bytes 589856 | tf_op jit(solution)/shard_map/ppermute | solution.py:43
  19.9 1.4 collective-permute-done.refs_3_.refs_0_
  21.3 3.4 %collective-permute-start.4 = (bf16[2,48,3072]{2,1,0:T(8,128)(2,1)S(1)}, bf16[2,48,3072]{2,1,0:T(8,128)(2,1)S(1)}, u32[]{:S(2)}, u32[]{:S(2)}) collective-permute-start(bf16[2,48,3072]{2,1,0:T(8,128)(2,1)S(1)} %collective-permute-done.2.refs_4_.refs_3_), channel_id=1, source_target_pairs={{0,3},{1,0},{2,1},{3,2},{4,7},{5,4},{6,5},{7,6},{8,11},{9,8},{10,9... | collective-permute-start | bytes 1769480 | tf_op jit(solution)/shard_map/ppermute | solution.py:43
  24.7 0.6 collective-permute-start.5
  25.3 6.4 %shard_map.111 = (bf16[3072,1024]{1,0:T(8,128)(2,1)S(1)}, bf16[3072,1024]{1,0:T(8,128)(2,1)S(1)}, bf16[1024,3072]{1,0:T(8,128)(2,1)S(1)}, f32[8,128]{1,0:T(8,128)S(1)}) custom-call(bf16[3072,1024]{1,0:T(8,128)(2,1)} %refs_0_.1, bf16[3072,1024]{1,0:T(8,128)(2,1)} %refs_1_.1, bf16[1024,3072]{1,0:T(8,128)(2,1)} %refs_2_.1, ...), custom_call_target="tpu_custom_call" | custom-call | bytes 9438 | tf_op jit(solution)/shard_map/pallas_call | solution.py:157
  31.7 0.2 shard_map.112.refs_0_
  31.9 2.2 %collective-permute-start.8 = (bf16[2,192,3072]{2,1,0:T(8,128)(2,1)S(1)}, bf16[2,192,3072]{2,1,0:T(8,128)(2,1)S(1)}, u32[]{:S(2)}, u32[]{:S(2)}) collective-permute-start(bf16[2,192,3072]{2,1,0:T(8,128)(2,1)S(1)} %shard_map.112.refs_0_), channel_id=1, source_target_pairs={{0,8},{1,9},{2,10},{3,11},{4,12},{5,13},{6,14},{7,15},{8,0},{9,1},... | collective-permute-start | bytes 7077896 | tf_op jit(solution)/shard_map/ppermute | solution.py:43
  34.1 4.8 %collective-permute-done.5.refs_2_.refs_1_ = bf16[2,48,3072]{2,1,0:T(8,128)(2,1)S(1)} collective-permute-done((bf16[2,48,3072]{2,1,0:T(8,128)(2,1)S(1)}, bf16[2,48,3072]{2,1,0:T(8,128)(2,1)S(1)}, u32[]{:S(2)}, u32[]{:S(2)}) %collective-permute-start.5) | collective-permute-done | bytes 589856 | tf_op jit(solution)/shard_map/ppermute | solution.py:43
  38.9 0.4 collective-permute-done.3.refs_0_
  39.4 3.1 %collective-permute-start.9 = (bf16[2,144,3072]{2,1,0:T(8,128)(2,1)S(1)}, bf16[2,144,3072]{2,1,0:T(8,128)(2,1)S(1)}, u32[]{:S(2)}, u32[]{:S(2)}) collective-permute-start(bf16[2,144,3072]{2,1,0:T(8,128)(2,1)S(1)} %shard_map.113.refs_1_), channel_id=1, source_target_pairs={{0,8},{1,9},{2,10},{3,11},{4,12},{5,13},{6,14},{7,15},{8,0},{9,1},... | collective-permute-start | bytes 5308424 | tf_op jit(solution)/shard_map/ppermute | solution.py:43
  42.6 1.5 collective-permute-start.6
  44.0 4.6 %shard_map.115 = (bf16[384,1024]{1,0:T(8,128)(2,1)S(1)}, f32[384,1024]{1,0:T(8,128)S(1)}, f32[384,1024]{1,0:T(8,128)S(1)}) custom-call(bf16[2,192,3072]{2,1,0:T(8,128)(2,1)S(1)} %shard_map.112.refs_0_, bf16[2,144,3072]{2,1,0:T(8,128)(2,1)S(1)} %shard_map.113.refs_1_, bf16[3072,1024]{1,0:T(8,128)(2,1)S(1)} %get-tuple-element.62.refs_2_.refs_1_, ...), custom_call_target="tpu_custom_call" | custom-call | flops 4227858 | bytes 9535 | tf_op jit(solution)/shard_map/pallas_call | solution.py:157
  48.6 2.6 %collective-permute-done.7.refs_0_ = bf16[48,3072]{1,0:T(8,128)(2,1)S(1)} collective-permute-done((bf16[48,3072]{1,0:T(8,128)(2,1)S(1)}, bf16[48,3072]{1,0:T(8,128)(2,1)S(1)}, u32[]{:S(2)}, u32[]{:S(2)}) %collective-permute-start.7) | collective-permute-done | bytes 294944 | tf_op jit(solution)/shard_map/ppermute | solution.py:43
  51.2 2.3 %shard_map.116 = (bf16[384,1024]{1,0:T(8,128)(2,1)S(1)}, f32[384,1024]{1,0:T(8,128)S(1)}, f32[384,1024]{1,0:T(8,128)S(1)}) custom-call(bf16[48,3072]{1,0:T(8,128)(2,1)S(1)} %collective-permute-done.7.refs_0_, bf16[3072,1024]{1,0:T(8,128)(2,1)S(1)} %get-tuple-element.62.refs_2_.refs_1_, ...), custom_call_target="tpu_custom_call", output_to_operand_aliasing={{0}: (3, {}), {1}: (4, {}), {2}: (5, {})} | custom-call | flops 603979 | bytes 8798 | tf_op jit(solution)/shard_map/pallas_call | solution.py:157
  53.5 1.4 shard_map.117
  55.0 0.9 collective-permute-start.11
  55.9 0.3 collective-permute-start.10
  56.2 1.4 shard_map.118.refs_8_.refs_6_.refs_0_
  57.6 1.6 %collective-permute-done.10.refs_5_ = bf16[2,48,3072]{2,1,0:T(8,128)(2,1)S(1)} collective-permute-done((bf16[2,48,3072]{2,1,0:T(8,128)(2,1)S(1)}, bf16[2,48,3072]{2,1,0:T(8,128)(2,1)S(1)}, u32[]{:S(2)}, u32[]{:S(2)}) %collective-permute-start.10) | collective-permute-done | bytes 589856 | tf_op jit(solution)/shard_map/ppermute | solution.py:43
  59.2 3.6 %shard_map.120 = (bf16[4,384,512]{2,1,0:T(8,128)(2,1)S(1)}, bf16[4,384,512]{2,1,0:T(8,128)(2,1)S(1)}) custom-call(bf16[2,192,3072]{2,1,0:T(8,128)(2,1)S(1)} %shard_map.112.refs_0_, bf16[2,144,3072]{2,1,0:T(8,128)(2,1)S(1)} %shard_map.113.refs_1_, bf16[2,48,3072]{2,1,0:T(8,128)(2,1)S(1)} %shard_map.119.refs_2_, ...), custom_call_target="tpu_custom_call" | custom-call | flops 2415919 | bytes 7274 | tf_op jit(solution)/shard_map/pallas_call | solution.py:157
  62.8 1.8 %shard_map.121 = (bf16[2,384,512]{2,1,0:T(8,128)(2,1)S(1)}, bf16[2,384,512]{2,1,0:T(8,128)(2,1)S(1)}) custom-call(bf16[2,192,3072]{2,1,0:T(8,128)(2,1)S(1)} %shard_map.112.refs_0_, bf16[2,144,3072]{2,1,0:T(8,128)(2,1)S(1)} %shard_map.113.refs_1_, bf16[2,48,3072]{2,1,0:T(8,128)(2,1)S(1)} %shard_map.119.refs_2_, ...), custom_call_target="tpu_custom_call" | custom-call | flops 1207959 | bytes 6488 | tf_op jit(solution)/shard_map/pallas_call | solution.py:157
  64.5 2.6 %collective-permute-start.14 = (bf16[2,384,512]{2,1,0:T(8,128)(2,1)S(1)}, bf16[2,384,512]{2,1,0:T(8,128)(2,1)S(1)}, u32[]{:S(2)}, u32[]{:S(2)}) collective-permute-start(bf16[2,384,512]{2,1,0:T(8,128)(2,1)S(1)} %get-tuple-element.80), channel_id=1, source_target_pairs={{0,96},{1,97},{2,98},{3,99},{4,100},{5,101},{6,102},{7,103},{8,104... | collective-permute-start | bytes 2359304 | tf_op jit(solution)/shard_map/ppermute | solution.py:43
  67.1 0.8 collective-permute-start.21
  67.9 2.6 %shard_map.122.refs_4_ = bf16[384,3072]{1,0:T(8,128)(2,1)S(1)} custom-call(bf16[384,1024]{1,0:T(8,128)(2,1)S(1)} %get-tuple-element.67.refs_4_.refs_6_.refs_0_, bf16[1024,3072]{1,0:T(8,128)(2,1)S(1)} %get-tuple-element.60.refs_3_.refs_1_, bf16[2,384,512]{2,1,0:T(8,128)(2,1)S(1)} %get-tuple-element.73.refs_2_), custom_call_target="tpu_custom_call" | custom-call | flops 2415919 | bytes 4718 | tf_op jit(solution)/shard_map/pallas_call | solution.py:157
  70.5 5.1 %shard_map.123 = (bf16[2,48,3072]{2,1,0:T(8,128)(2,1)S(1)}, bf16[2,48,3072]{2,1,0:T(8,128)(2,1)S(1)}, bf16[2,2,48,3072]{3,2,1,0:T(8,128)(2,1)S(1)}, bf16[2,2,48,...) custom-call(bf16[2,384,512]{2,1,0:T(8,128)(2,1)S(1)} %shard_map.118.refs_8_.refs_6_.refs_0_, ...), custom_call_target="tpu_custom_call" | custom-call | flops 4831838 | bytes 10813 | tf_op jit(solution)/shard_map/pallas_call | solution.py:157
  75.7 2.7 %collective-permute-start.13 = (bf16[2,48,3072]{2,1,0:T(8,128)(2,1)S(1)}, bf16[2,48,3072]{2,1,0:T(8,128)(2,1)S(1)}, u32[]{:S(2)}, u32[]{:S(2)}) collective-permute-start(bf16[2,48,3072]{2,1,0:T(8,128)(2,1)S(1)} %get-tuple-element.78), channel_id=1, source_target_pairs={{0,3},{1,0},{2,1},{3,2},{4,7},{5,4},{6,5},{7,6},{8,11},{9,8},{10,9... | collective-permute-start | bytes 1769480 | tf_op jit(solution)/shard_map/ppermute | solution.py:43
  78.4 1.4 shard_map.124
  79.8 3.8 %collective-permute-done.14.refs_1_ = bf16[2,384,512]{2,1,0:T(8,128)(2,1)S(1)} collective-permute-done((bf16[2,384,512]{2,1,0:T(8,128)(2,1)S(1)}, bf16[2,384,512]{2,1,0:T(8,128)(2,1)S(1)}, u32[]{:S(2)}, u32[]{:S(2)}) %collective-permute-start.14) | collective-permute-done | bytes 786464 | tf_op jit(solution)/shard_map/ppermute | solution.py:43
  83.7 0.2 shard_map.125.refs_8_
  83.8 1.0 collective-permute-start.19
  84.9 1.9 %collective-permute-done.15.refs_1_ = bf16[2,384,512]{2,1,0:T(8,128)(2,1)S(1)} collective-permute-done((bf16[2,384,512]{2,1,0:T(8,128)(2,1)S(1)}, bf16[2,384,512]{2,1,0:T(8,128)(2,1)S(1)}, u32[]{:S(2)}, u32[]{:S(2)}) %collective-permute-start.15) | collective-permute-done | bytes 786464 | tf_op jit(solution)/shard_map/ppermute | solution.py:43
  86.7 0.7 collective-permute-start.20
  87.4 3.0 %shard_map.126 = (bf16[2,384,512]{2,1,0:T(8,128)(2,1)S(1)}, bf16[2,384,512]{2,1,0:T(8,128)(2,1)S(1)}, bf16[2,384,512]{2,1,0:T(8,128)(2,1)S(1)}, bf16[2,384,512]{2,1,0:T(8,128)(2,1)S(1)}) custom-call(bf16[2,192,3072]{2,1,0:T(8,128)(2,1)S(1)} %shard_map.112.refs_0_, bf16[2,144,3072]{2,1,0:T(8,128)(2,1)S(1)} %shard_map.113.refs_1_, ...), custom_call_target="tpu_custom_call" | custom-call | flops 2415919 | bytes 7274 | tf_op jit(solution)/shard_map/pallas_call | solution.py:157
  90.4 0.2 shard_map.127.refs_4_
  90.6 0.2 collective-permute-done.12.refs_1_
  90.8 0.3 shard_map.128
  91.2 2.7 %collective-permute-start.17 = (bf16[2,2,48,3072]{3,2,1,0:T(8,128)(2,1)S(1)}, bf16[2,2,48,3072]{3,2,1,0:T(8,128)(2,1)S(1)}, u32[]{:S(2)}, u32[]{:S(2)}) collective-permute-start(bf16[2,2,48,3072]{3,2,1,0:T(8,128)(2,1)S(1)} %get-tuple-element.83), channel_id=1, source_target_pairs={{0,3},{1,0},{2,1},{3,2},{4,7},{5,4},{6,5},{7,6},{8,11},{9,8},{10,9... | collective-permute-start | bytes 3538952 | tf_op jit(solution)/shard_map/ppermute | solution.py:43
  93.8 10.1 %collective-permute-done.19.refs_1_ = bf16[2,384,512]{2,1,0:T(8,128)(2,1)S(1)} collective-permute-done((bf16[2,384,512]{2,1,0:T(8,128)(2,1)S(1)}, bf16[2,384,512]{2,1,0:T(8,128)(2,1)S(1)}, u32[]{:S(2)}, u32[]{:S(2)}) %collective-permute-start.19) | collective-permute-done | bytes 786464 | tf_op jit(solution)/shard_map/ppermute | solution.py:43
  104.0 0.3 collective-permute-done.20.refs_2_
  104.2 0.3 shard_map.131.refs_2_
  104.5 0.4 shard_map.134
  104.9 0.4 collective-permute-start.26
  105.3 2.4 %collective-permute-start.27 = (bf16[192,512]{1,0:T(8,128)(2,1)S(1)}, bf16[192,512]{1,0:T(8,128)(2,1)S(1)}, u32[]{:S(2)}, u32[]{:S(2)}) collective-permute-start(bf16[192,512]{1,0:T(8,128)(2,1)S(1)} %get-tuple-element.104), channel_id=1, source_target_pairs={{0,96},{1,97},{2,98},{3,99},{4,100},{5,101},{6,102},{7,103},{8,104... | collective-permute-start | bytes 589832 | tf_op jit(solution)/shard_map/ppermute | solution.py:43
  107.7 0.8 collective-permute-start.24
  108.4 2.6 %collective-permute-done.26.refs_1_ = bf16[192,512]{1,0:T(8,128)(2,1)S(1)} collective-permute-done((bf16[192,512]{1,0:T(8,128)(2,1)S(1)}, bf16[192,512]{1,0:T(8,128)(2,1)S(1)}, u32[]{:S(2)}, u32[]{:S(2)}) %collective-permute-start.26) | collective-permute-done | bytes 196640 | tf_op jit(solution)/shard_map/ppermute | solution.py:43
  111.0 2.7 %collective-permute-start.23 = (bf16[2,384,512]{2,1,0:T(8,128)(2,1)S(1)}, bf16[2,384,512]{2,1,0:T(8,128)(2,1)S(1)}, u32[]{:S(2)}, u32[]{:S(2)}) collective-permute-start(bf16[2,384,512]{2,1,0:T(8,128)(2,1)S(1)} %get-tuple-element.94), channel_id=1, source_target_pairs={{0,96},{1,97},{2,98},{3,99},{4,100},{5,101},{6,102},{7,103},{8,104... | collective-permute-start | bytes 2359304 | tf_op jit(solution)/shard_map/ppermute | solution.py:43
  113.8 4.2 %collective-permute-done.16.refs_1_ = bf16[2,2,48,3072]{3,2,1,0:T(8,128)(2,1)S(1)} collective-permute-done((bf16[2,2,48,3072]{3,2,1,0:T(8,128)(2,1)S(1)}, bf16[2,2,48,3072]{3,2,1,0:T(8,128)(2,1)S(1)}, u32[]{:S(2)}, u32[]{:S(2)}) %collective-permute-start.16) | collective-permute-done | bytes 1179680 | tf_op jit(solution)/shard_map/ppermute | solution.py:43
  118.0 0.7 collective-permute-start.28
  118.7 2.0 %collective-permute-start.29 = (bf16[2,192,512]{2,1,0:T(8,128)(2,1)S(1)}, bf16[2,192,512]{2,1,0:T(8,128)(2,1)S(1)}, u32[]{:S(2)}, u32[]{:S(2)}) collective-permute-start(bf16[2,192,512]{2,1,0:T(8,128)(2,1)S(1)} %get-tuple-element.106), channel_id=1, source_target_pairs={{0,96},{1,97},{2,98},{3,99},{4,100},{5,101},{6,102},{7,103},{8,104... | collective-permute-start | bytes 1179656 | tf_op jit(solution)/shard_map/ppermute | solution.py:43
  120.7 0.4 shard_map.129
  121.1 2.6 %collective-permute-done.24.refs_3_ = bf16[2,384,512]{2,1,0:T(8,128)(2,1)S(1)} collective-permute-done((bf16[2,384,512]{2,1,0:T(8,128)(2,1)S(1)}, bf16[2,384,512]{2,1,0:T(8,128)(2,1)S(1)}, u32[]{:S(2)}, u32[]{:S(2)}) %collective-permute-start.24) | collective-permute-done | bytes 786464 | tf_op jit(solution)/shard_map/ppermute | solution.py:43
  123.7 2.4 %collective-permute-start.18 = (bf16[2,48,3072]{2,1,0:T(8,128)(2,1)S(1)}, bf16[2,48,3072]{2,1,0:T(8,128)(2,1)S(1)}, u32[]{:S(2)}, u32[]{:S(2)}) collective-permute-start(bf16[2,48,3072]{2,1,0:T(8,128)(2,1)S(1)} %get-tuple-element.85), channel_id=1, source_target_pairs={{0,4},{1,5},{2,6},{3,7},{4,0},{5,1},{6,2},{7,3},{8,12},{9,13},{10,... | collective-permute-start | bytes 1769480 | tf_op jit(solution)/shard_map/ppermute | solution.py:43
  126.0 1.9 %collective-permute-done.22.refs_1_ = bf16[2,384,512]{2,1,0:T(8,128)(2,1)S(1)} collective-permute-done((bf16[2,384,512]{2,1,0:T(8,128)(2,1)S(1)}, bf16[2,384,512]{2,1,0:T(8,128)(2,1)S(1)}, u32[]{:S(2)}, u32[]{:S(2)}) %collective-permute-start.22) | collective-permute-done | bytes 786464 | tf_op jit(solution)/shard_map/ppermute | solution.py:43
  127.9 0.8 shard_map.132
  128.8 8.1 %collective-permute-start.25 = (bf16[2,192,512]{2,1,0:T(8,128)(2,1)S(1)}, bf16[2,192,512]{2,1,0:T(8,128)(2,1)S(1)}, u32[]{:S(2)}, u32[]{:S(2)}) collective-permute-start(bf16[2,192,512]{2,1,0:T(8,128)(2,1)S(1)} %get-tuple-element.97), channel_id=1, source_target_pairs={{0,8},{1,9},{2,10},{3,11},{4,12},{5,13},{6,14},{7,15},{8,0},{9,1},... | collective-permute-start | bytes 1179656 | tf_op jit(solution)/shard_map/ppermute | solution.py:43
  136.9 0.3 shard_map.136
  137.2 3.8 %collective-permute-start.30 = (bf16[1,192,512]{2,1,0:T(8,128)(2,1)S(1)}, bf16[1,192,512]{2,1,0:T(8,128)(2,1)S(1)}, u32[]{:S(2)}, u32[]{:S(2)}) collective-permute-start(bf16[1,192,512]{2,1,0:T(8,128)(2,1)S(1)} %get-tuple-element.108), channel_id=1, source_target_pairs={{0,8},{1,9},{2,10},{3,11},{4,12},{5,13},{6,14},{7,15},{8,0},{9,1},... | collective-permute-start | bytes 589832 | tf_op jit(solution)/shard_map/ppermute | solution.py:43
  141.0 1.1 collective-permute-done.30.got
  142.0 0.8 shard_map.137
  142.8 1.7 %shard_map.130 = (bf16[128,3072]{1,0:T(8,128)(2,1)}, bf16[128,3072]{1,0:T(8,128)(2,1)}) custom-call(s32[2,128]{1,0:T(2,128)S(1)} %bitcast.8, f32[1,128]{1,0:T(1,128)S(1)} %bitcast.10, bf16[2,48,3072]{2,1,0:T(8,128)(2,1)S(1)} %get-tuple-element.84.kept, bf16[2,48,3072]{2,1,0:T(8,128)(2,1)S(1)} %collective-permute-done.18.got), custom_call_target="tpu_custom_call" | custom-call | flops 75497 | bytes 2800 | tf_op jit(solution)/shard_map/pallas_call | solution.py:133
  144.5 0.9 shard_map.133
  (30 shorter events, 0.6 us)
Async XLA Ops:
  2.4 17.6 %collective-permute-start.2 = (bf16[2,48,3072]{2,1,0:T(8,128)(2,1)S(1)}, bf16[2,48,3072]{2,1,0:T(8,128)(2,1)S(1)}, u32[]{:S(2)}, u32[]{:S(2)}) collective-permute-start(bf16[2,48,3072]{2,1,0:T(8,128)(2,1)S(1)} %shard_map.110.refs_2_), channel_id=1, source_target_pairs={{0,4},{1,5},{2,6},{3,7},{4,0},{5,1},{6,2},{7,3},{8,12},{9,13},{10,... | collective-permute-start | bytes 1769480 | tf_op jit(solution)/shard_map/ppermute | solution.py:43
  6.9 14.4 %collective-permute-start = (bf16[2,48,3072]{2,1,0:T(8,128)(2,1)S(1)}, bf16[2,48,3072]{2,1,0:T(8,128)(2,1)S(1)}, u32[]{:S(2)}, u32[]{:S(2)}) collective-permute-start(bf16[2,48,3072]{2,1,0:T(8,128)(2,1)S(1)} %shard_map.110.refs_2_), channel_id=1, source_target_pairs={{0,3},{1,0},{2,1},{3,2},{4,7},{5,4},{6,5},{7,6},{8,11},{9,8},{10,9... | collective-permute-start | bytes 1769480 | tf_op jit(solution)/shard_map/ppermute | solution.py:43
  9.6 15.1 %collective-permute-start.1 = (bf16[2,48,3072]{2,1,0:T(8,128)(2,1)S(1)}, bf16[2,48,3072]{2,1,0:T(8,128)(2,1)S(1)}, u32[]{:S(2)}, u32[]{:S(2)}) collective-permute-start(bf16[2,48,3072]{2,1,0:T(8,128)(2,1)S(1)} %shard_map.110.refs_2_), channel_id=1, source_target_pairs={{0,1},{1,2},{2,3},{3,0},{4,5},{5,6},{6,7},{7,4},{8,9},{9,10},{10,1... | collective-permute-start | bytes 1769480 | tf_op jit(solution)/shard_map/ppermute | solution.py:43
  21.3 18.0 %collective-permute-start.4 = (bf16[2,48,3072]{2,1,0:T(8,128)(2,1)S(1)}, bf16[2,48,3072]{2,1,0:T(8,128)(2,1)S(1)}, u32[]{:S(2)}, u32[]{:S(2)}) collective-permute-start(bf16[2,48,3072]{2,1,0:T(8,128)(2,1)S(1)} %collective-permute-done.2.refs_4_.refs_3_), channel_id=1, source_target_pairs={{0,3},{1,0},{2,1},{3,2},{4,7},{5,4},{6,5},{7,6},{8,11},{9,8},{10,9... | collective-permute-start | bytes 1769480 | tf_op jit(solution)/shard_map/ppermute | solution.py:43
  24.7 14.2 %collective-permute-start.5 = (bf16[2,48,3072]{2,1,0:T(8,128)(2,1)S(1)}, bf16[2,48,3072]{2,1,0:T(8,128)(2,1)S(1)}, u32[]{:S(2)}, u32[]{:S(2)}) collective-permute-start(bf16[2,48,3072]{2,1,0:T(8,128)(2,1)S(1)} %collective-permute-done.1.refs_1_), channel_id=1, source_target_pairs={{0,4},{1,5},{2,6},{3,7},{4,0},{5,1},{6,2},{7,3},{8,12},{9,13},{10,... | collective-permute-start | bytes 1769480 | tf_op jit(solution)/shard_map/ppermute | solution.py:43
  25.3 13.9 %collective-permute-start.3 = (bf16[2,48,3072]{2,1,0:T(8,128)(2,1)S(1)}, bf16[2,48,3072]{2,1,0:T(8,128)(2,1)S(1)}, u32[]{:S(2)}, u32[]{:S(2)}) collective-permute-start(bf16[2,48,3072]{2,1,0:T(8,128)(2,1)S(1)} %collective-permute-done.1.refs_1_), channel_id=1, source_target_pairs={{0,1},{1,2},{2,3},{3,0},{4,5},{5,6},{6,7},{7,4},{8,9},{9,10},{10,1... | collective-permute-start | bytes 1769480 | tf_op jit(solution)/shard_map/ppermute | solution.py:43
  31.9 19.3 %collective-permute-start.8 = (bf16[2,192,3072]{2,1,0:T(8,128)(2,1)S(1)}, bf16[2,192,3072]{2,1,0:T(8,128)(2,1)S(1)}, u32[]{:S(2)}, u32[]{:S(2)}) collective-permute-start(bf16[2,192,3072]{2,1,0:T(8,128)(2,1)S(1)} %shard_map.112.refs_0_), channel_id=1, source_target_pairs={{0,8},{1,9},{2,10},{3,11},{4,12},{5,13},{6,14},{7,15},{8,0},{9,1},... | collective-permute-start | bytes 7077896 | tf_op jit(solution)/shard_map/ppermute | solution.py:43
  39.4 11.8 %collective-permute-start.9 = (bf16[2,144,3072]{2,1,0:T(8,128)(2,1)S(1)}, bf16[2,144,3072]{2,1,0:T(8,128)(2,1)S(1)}, u32[]{:S(2)}, u32[]{:S(2)}) collective-permute-start(bf16[2,144,3072]{2,1,0:T(8,128)(2,1)S(1)} %shard_map.113.refs_1_), channel_id=1, source_target_pairs={{0,8},{1,9},{2,10},{3,11},{4,12},{5,13},{6,14},{7,15},{8,0},{9,1},... | collective-permute-start | bytes 5308424 | tf_op jit(solution)/shard_map/ppermute | solution.py:43
  42.5 8.7 %collective-permute-start.7 = (bf16[48,3072]{1,0:T(8,128)(2,1)S(1)}, bf16[48,3072]{1,0:T(8,128)(2,1)S(1)}, u32[]{:S(2)}, u32[]{:S(2)}) collective-permute-start(bf16[48,3072]{1,0:T(8,128)(2,1)S(1)} %get-tuple-element.61.refs_4_), channel_id=1, source_target_pairs={{0,3},{1,0},{2,1},{3,2},{4,7},{5,4},{6,5},{7,6},{8,11},{9,8},{10,9... | collective-permute-start | bytes 884744 | tf_op jit(solution)/shard_map/ppermute | solution.py:43
  42.6 10.9 %collective-permute-start.6 = (bf16[48,3072]{1,0:T(8,128)(2,1)S(1)}, bf16[48,3072]{1,0:T(8,128)(2,1)S(1)}, u32[]{:S(2)}, u32[]{:S(2)}) collective-permute-start(bf16[48,3072]{1,0:T(8,128)(2,1)S(1)} %get-tuple-element.59), channel_id=1, source_target_pairs={{0,1},{1,2},{2,3},{3,0},{4,5},{5,6},{6,7},{7,4},{8,9},{9,10},{10,1... | collective-permute-start | bytes 884744 | tf_op jit(solution)/shard_map/ppermute | solution.py:43
  55.0 4.2 %collective-permute-start.11 = (bf16[3,384,512]{2,1,0:T(8,128)(2,1)S(1)}, bf16[3,384,512]{2,1,0:T(8,128)(2,1)S(1)}, u32[]{:S(2)}, u32[]{:S(2)}) collective-permute-start(bf16[3,384,512]{2,1,0:T(8,128)(2,1)S(1)} %get-tuple-element.71.refs_1_), channel_id=1, source_target_pairs={{0,8},{1,9},{2,10},{3,11},{4,12},{5,13},{6,14},{7,15},{8,0},{9,1},... | collective-permute-start | bytes 3538952 | tf_op jit(solution)/shard_map/ppermute | solution.py:43
  55.9 3.3 %collective-permute-start.10 = (bf16[2,48,3072]{2,1,0:T(8,128)(2,1)S(1)}, bf16[2,48,3072]{2,1,0:T(8,128)(2,1)S(1)}, u32[]{:S(2)}, u32[]{:S(2)}) collective-permute-start(bf16[2,48,3072]{2,1,0:T(8,128)(2,1)S(1)} %shard_map.119.refs_2_), channel_id=1, source_target_pairs={{0,8},{1,9},{2,10},{3,11},{4,12},{5,13},{6,14},{7,15},{8,0},{9,1},... | collective-permute-start | bytes 1769480 | tf_op jit(solution)/shard_map/ppermute | solution.py:43
  64.5 19.1 %collective-permute-start.14 = (bf16[2,384,512]{2,1,0:T(8,128)(2,1)S(1)}, bf16[2,384,512]{2,1,0:T(8,128)(2,1)S(1)}, u32[]{:S(2)}, u32[]{:S(2)}) collective-permute-start(bf16[2,384,512]{2,1,0:T(8,128)(2,1)S(1)} %get-tuple-element.80), channel_id=1, source_target_pairs={{0,96},{1,97},{2,98},{3,99},{4,100},{5,101},{6,102},{7,103},{8,104... | collective-permute-start | bytes 2359304 | tf_op jit(solution)/shard_map/ppermute | solution.py:43
  67.1 19.6 %collective-permute-start.15 = (bf16[2,384,512]{2,1,0:T(8,128)(2,1)S(1)}, bf16[2,384,512]{2,1,0:T(8,128)(2,1)S(1)}, u32[]{:S(2)}, u32[]{:S(2)}) collective-permute-start(bf16[2,384,512]{2,1,0:T(8,128)(2,1)S(1)} %get-tuple-element.73.refs_2_), channel_id=1, source_target_pairs={{0,32},{1,33},{2,34},{3,35},{4,36},{5,37},{6,38},{7,39},{8,40},{9,... | collective-permute-start | bytes 2359304 | tf_op jit(solution)/shard_map/ppermute | solution.py:43
  67.1 37.4 %collective-permute-start.21 = (bf16[4,384,512]{2,1,0:T(8,128)(2,1)S(1)}, bf16[4,384,512]{2,1,0:T(8,128)(2,1)S(1)}, u32[]{:S(2)}, u32[]{:S(2)}) collective-permute-start(bf16[4,384,512]{2,1,0:T(8,128)(2,1)S(1)} %get-tuple-element.92), channel_id=1, source_target_pairs={{0,16},{1,17},{2,18},{3,19},{4,20},{5,21},{6,22},{7,23},{8,24},{9,... | collective-permute-start | bytes 4718600 | tf_op jit(solution)/shard_map/ppermute | solution.py:43
  75.6 15.2 %collective-permute-start.12 = (bf16[2,48,3072]{2,1,0:T(8,128)(2,1)S(1)}, bf16[2,48,3072]{2,1,0:T(8,128)(2,1)S(1)}, u32[]{:S(2)}, u32[]{:S(2)}) collective-permute-start(bf16[2,48,3072]{2,1,0:T(8,128)(2,1)S(1)} %get-tuple-element.76), channel_id=1, source_target_pairs={{0,1},{1,2},{2,3},{3,0},{4,5},{5,6},{6,7},{7,4},{8,9},{9,10},{10,1... | collective-permute-start | bytes 1769480 | tf_op jit(solution)/shard_map/ppermute | solution.py:43
  75.7 15.1 %collective-permute-start.13 = (bf16[2,48,3072]{2,1,0:T(8,128)(2,1)S(1)}, bf16[2,48,3072]{2,1,0:T(8,128)(2,1)S(1)}, u32[]{:S(2)}, u32[]{:S(2)}) collective-permute-start(bf16[2,48,3072]{2,1,0:T(8,128)(2,1)S(1)} %get-tuple-element.78), channel_id=1, source_target_pairs={{0,3},{1,0},{2,1},{3,2},{4,7},{5,4},{6,5},{7,6},{8,11},{9,8},{10,9... | collective-permute-start | bytes 1769480 | tf_op jit(solution)/shard_map/ppermute | solution.py:43
  83.8 20.1 %collective-permute-start.19 = (bf16[2,384,512]{2,1,0:T(8,128)(2,1)S(1)}, bf16[2,384,512]{2,1,0:T(8,128)(2,1)S(1)}, u32[]{:S(2)}, u32[]{:S(2)}) collective-permute-start(bf16[2,384,512]{2,1,0:T(8,128)(2,1)S(1)} %get-tuple-element.91), channel_id=1, source_target_pairs={{0,32},{1,33},{2,34},{3,35},{4,36},{5,37},{6,38},{7,39},{8,40},{9,... | collective-permute-start | bytes 2359304 | tf_op jit(solution)/shard_map/ppermute | solution.py:43
  86.7 17.5 %collective-permute-start.20 = (bf16[2,384,512]{2,1,0:T(8,128)(2,1)S(1)}, bf16[2,384,512]{2,1,0:T(8,128)(2,1)S(1)}, u32[]{:S(2)}, u32[]{:S(2)}) collective-permute-start(bf16[2,384,512]{2,1,0:T(8,128)(2,1)S(1)} %shard_map.125.refs_8_), channel_id=1, source_target_pairs={{0,96},{1,97},{2,98},{3,99},{4,100},{5,101},{6,102},{7,103},{8,104... | collective-permute-start | bytes 2359304 | tf_op jit(solution)/shard_map/ppermute | solution.py:43
  91.1 26.9 %collective-permute-start.16 = (bf16[2,2,48,3072]{3,2,1,0:T(8,128)(2,1)S(1)}, bf16[2,2,48,3072]{3,2,1,0:T(8,128)(2,1)S(1)}, u32[]{:S(2)}, u32[]{:S(2)}) collective-permute-start(bf16[2,2,48,3072]{3,2,1,0:T(8,128)(2,1)S(1)} %get-tuple-element.82), channel_id=1, source_target_pairs={{0,1},{1,2},{2,3},{3,0},{4,5},{5,6},{6,7},{7,4},{8,9},{9,10},{10,1... | collective-permute-start | bytes 3538952 | tf_op jit(solution)/shard_map/ppermute | solution.py:43
  91.2 27.5 %collective-permute-start.17 = (bf16[2,2,48,3072]{3,2,1,0:T(8,128)(2,1)S(1)}, bf16[2,2,48,3072]{3,2,1,0:T(8,128)(2,1)S(1)}, u32[]{:S(2)}, u32[]{:S(2)}) collective-permute-start(bf16[2,2,48,3072]{3,2,1,0:T(8,128)(2,1)S(1)} %get-tuple-element.83), channel_id=1, source_target_pairs={{0,3},{1,0},{2,1},{3,2},{4,7},{5,4},{6,5},{7,6},{8,11},{9,8},{10,9... | collective-permute-start | bytes 3538952 | tf_op jit(solution)/shard_map/ppermute | solution.py:43
  104.9 6.1 %collective-permute-start.26 = (bf16[192,512]{1,0:T(8,128)(2,1)S(1)}, bf16[192,512]{1,0:T(8,128)(2,1)S(1)}, u32[]{:S(2)}, u32[]{:S(2)}) collective-permute-start(bf16[192,512]{1,0:T(8,128)(2,1)S(1)} %get-tuple-element.102), channel_id=1, source_target_pairs={{0,32},{1,33},{2,34},{3,35},{4,36},{5,37},{6,38},{7,39},{8,40},{9,... | collective-permute-start | bytes 589832 | tf_op jit(solution)/shard_map/ppermute | solution.py:43
  105.3 5.7 %collective-permute-start.27 = (bf16[192,512]{1,0:T(8,128)(2,1)S(1)}, bf16[192,512]{1,0:T(8,128)(2,1)S(1)}, u32[]{:S(2)}, u32[]{:S(2)}) collective-permute-start(bf16[192,512]{1,0:T(8,128)(2,1)S(1)} %get-tuple-element.104), channel_id=1, source_target_pairs={{0,96},{1,97},{2,98},{3,99},{4,100},{5,101},{6,102},{7,103},{8,104... | collective-permute-start | bytes 589832 | tf_op jit(solution)/shard_map/ppermute | solution.py:43
  107.7 16.0 %collective-permute-start.24 = (bf16[2,384,512]{2,1,0:T(8,128)(2,1)S(1)}, bf16[2,384,512]{2,1,0:T(8,128)(2,1)S(1)}, u32[]{:S(2)}, u32[]{:S(2)}) collective-permute-start(bf16[2,384,512]{2,1,0:T(8,128)(2,1)S(1)} %shard_map.131.refs_2_), channel_id=1, source_target_pairs={{0,16},{1,17},{2,18},{3,19},{4,20},{5,21},{6,22},{7,23},{8,24},{9,... | collective-permute-start | bytes 2359304 | tf_op jit(solution)/shard_map/ppermute | solution.py:43
  111.0 16.9 %collective-permute-start.22 = (bf16[2,384,512]{2,1,0:T(8,128)(2,1)S(1)}, bf16[2,384,512]{2,1,0:T(8,128)(2,1)S(1)}, u32[]{:S(2)}, u32[]{:S(2)}) collective-permute-start(bf16[2,384,512]{2,1,0:T(8,128)(2,1)S(1)} %shard_map.127.refs_4_), channel_id=1, source_target_pairs={{0,32},{1,33},{2,34},{3,35},{4,36},{5,37},{6,38},{7,39},{8,40},{9,... | collective-permute-start | bytes 2359304 | tf_op jit(solution)/shard_map/ppermute | solution.py:43
  111.0 16.9 %collective-permute-start.23 = (bf16[2,384,512]{2,1,0:T(8,128)(2,1)S(1)}, bf16[2,384,512]{2,1,0:T(8,128)(2,1)S(1)}, u32[]{:S(2)}, u32[]{:S(2)}) collective-permute-start(bf16[2,384,512]{2,1,0:T(8,128)(2,1)S(1)} %get-tuple-element.94), channel_id=1, source_target_pairs={{0,96},{1,97},{2,98},{3,99},{4,100},{5,101},{6,102},{7,103},{8,104... | collective-permute-start | bytes 2359304 | tf_op jit(solution)/shard_map/ppermute | solution.py:43
  118.0 18.9 %collective-permute-start.28 = (bf16[2,192,512]{2,1,0:T(8,128)(2,1)S(1)}, bf16[2,192,512]{2,1,0:T(8,128)(2,1)S(1)}, u32[]{:S(2)}, u32[]{:S(2)}) collective-permute-start(bf16[2,192,512]{2,1,0:T(8,128)(2,1)S(1)} %get-tuple-element.105), channel_id=1, source_target_pairs={{0,32},{1,33},{2,34},{3,35},{4,36},{5,37},{6,38},{7,39},{8,40},{9,... | collective-permute-start | bytes 1179656 | tf_op jit(solution)/shard_map/ppermute | solution.py:43
  118.7 18.2 %collective-permute-start.29 = (bf16[2,192,512]{2,1,0:T(8,128)(2,1)S(1)}, bf16[2,192,512]{2,1,0:T(8,128)(2,1)S(1)}, u32[]{:S(2)}, u32[]{:S(2)}) collective-permute-start(bf16[2,192,512]{2,1,0:T(8,128)(2,1)S(1)} %get-tuple-element.106), channel_id=1, source_target_pairs={{0,96},{1,97},{2,98},{3,99},{4,100},{5,101},{6,102},{7,103},{8,104... | collective-permute-start | bytes 1179656 | tf_op jit(solution)/shard_map/ppermute | solution.py:43
  123.7 19.1 %collective-permute-start.18 = (bf16[2,48,3072]{2,1,0:T(8,128)(2,1)S(1)}, bf16[2,48,3072]{2,1,0:T(8,128)(2,1)S(1)}, u32[]{:S(2)}, u32[]{:S(2)}) collective-permute-start(bf16[2,48,3072]{2,1,0:T(8,128)(2,1)S(1)} %get-tuple-element.85), channel_id=1, source_target_pairs={{0,4},{1,5},{2,6},{3,7},{4,0},{5,1},{6,2},{7,3},{8,12},{9,13},{10,... | collective-permute-start | bytes 1769480 | tf_op jit(solution)/shard_map/ppermute | solution.py:43
  128.7 14.1 %copy-start = (s32[128,2]{0,1:T(2,128)S(1)}, s32[128,2]{0,1:T(2,128)}, u32[]{:S(2)}) copy-start(s32[128,2]{0,1:T(2,128)} %param.9) | copy-start | bytes 3076
  128.7 14.1 %copy-start.1 = (f32[128]{0:T(128)S(1)}, f32[128]{0:T(128)}, u32[]{:S(2)}) copy-start(f32[128]{0:T(128)} %param.10) | copy-start | bytes 1540
  128.8 15.8 %collective-permute-start.25 = (bf16[2,192,512]{2,1,0:T(8,128)(2,1)S(1)}, bf16[2,192,512]{2,1,0:T(8,128)(2,1)S(1)}, u32[]{:S(2)}, u32[]{:S(2)}) collective-permute-start(bf16[2,192,512]{2,1,0:T(8,128)(2,1)S(1)} %get-tuple-element.97), channel_id=1, source_target_pairs={{0,8},{1,9},{2,10},{3,11},{4,12},{5,13},{6,14},{7,15},{8,0},{9,1},... | collective-permute-start | bytes 1179656 | tf_op jit(solution)/shard_map/ppermute | solution.py:43
  137.2 4.9 %collective-permute-start.30 = (bf16[1,192,512]{2,1,0:T(8,128)(2,1)S(1)}, bf16[1,192,512]{2,1,0:T(8,128)(2,1)S(1)}, u32[]{:S(2)}, u32[]{:S(2)}) collective-permute-start(bf16[1,192,512]{2,1,0:T(8,128)(2,1)S(1)} %get-tuple-element.108), channel_id=1, source_target_pairs={{0,8},{1,9},{2,10},{3,11},{4,12},{5,13},{6,14},{7,15},{8,0},{9,1},... | collective-permute-start | bytes 589832 | tf_op jit(solution)/shard_map/ppermute | solution.py:43

commit v2 on v1

--- a/solution.py
+++ b/solution.py
@@ -220,13 +220,13 @@
     return call(pair_kernel, [], [x, d], [(2, SLOTS, DW)], 1)[0]
 
 
-def split_kernel(a, b, x, d):
-    x[...] = a[0]
-    d[...] = b[1]
-
-
-def split(a, b, *earlier):
-    return call(split_kernel, [], [a, b], [(SLOTS, DW)] * 2, 1, earlier)
+def split_kernel(which, chunk, out):
+    out[...] = chunk[which]
+
+
+def split(which, chunk, *earlier):
+    kernel = functools.partial(split_kernel, which)
+    return call(kernel, [], [chunk], [(SLOTS, DW)], 1, earlier)[0]
 
 
 FIRST = ROWS - SLOTS
@@ -539,12 +539,13 @@
     sel = select(ids, weight, tokens, cotangent)
     zhi, up0, down0 = to_zhi(sel), to_y(sel, -1), to_y(sel, 1)
     far0, down1 = to_y(down0, 1), to_zhi(down0)
-    up1 = to_y(after(zhi, up0), -1)
+    up1 = to_y(zhi, -1)
     w_gate, w_up, w_down, there = stage([w_gate, w_up, w_down], up0, zhi)
     four = pack(up0, down0, sel, zhi, earlier=[there])
-    x_far1, d_far1 = split(up1, down1, there)
-    three = pack(far0, up1, down1)
-    first = gate_first(four, three, w_gate, w_up, x_far1)
+    x_far1 = split(0, up1, there)
+    three = pack(far0, up1, down1, earlier=[x_far1])
+    d_far1 = split(1, down1, x_far1)
+    first = gate_first(four, three, w_gate, w_up, d_far1)
     x_far1, d_far1 = to_y(x_far1, -1), to_y(d_far1, 1)
     four_other, three_other = to_core(four), to_core(three)
     far1 = pair(x_far1, d_far1)
@@ -554,11 +555,11 @@
     d_got = to_core(d_sent)
     d_mine = back_own(d_rows, w_down, act, slope)
 
-    down_kept, down_sent = down_grads(parts, hidden, d_got, d_mine)
+    far_a, far_b = gate_up_grads([(2, None)], parts, d_mine, d_got)
+    far_got_a, far_got_b = lax.optimization_barrier((to_x(far_a, 1), to_x(far_b, -1)))
+    down_kept, down_sent = down_grads(parts, hidden, d_got, far_a)
     down_got = to_zlo(down_sent)
-    far_a, far_b = gate_up_grads([(2, None)], parts, d_mine, d_got, down_kept)
-    far_got_a, far_got_b = to_x(far_a, 1), to_x(far_b, -1)
-    out = out_terms(hidden, w_down, far_a)
+    out = out_terms(hidden, w_down, down_kept)
     row_far_a, row_far_b, row_above, row_below, row_own = row_terms(
         d_mine, d_sent, w_gate, w_up, out
     )

time: 146 us -> 142 us (0.973)
  waiting for transfers between devices: 49.7 us -> 43.4 us
  starting transfers between devices: 52.9 us -> 55.8 us
    ppermute x31, waiting for transfers between devices: 49.7 us -> 43.4 us  [shift(): return lax.ppermute(value, ('dp', 'tensor'), pairs)]
    ppermute x31, starting transfers between devices: 52.9 us -> 55.8 us  [shift(): return lax.ppermute(value, ('dp', 'tensor'), pairs)]
    pallas_call x24 -> x25, Pallas kernels: 36.9 us -> 36.9 us  [call(): pl.pallas_call(without(inputs, len(earlier), kernel), in_specs=[IN_SMEM]...]
  transfers between devices with their start and end apart: 31 -> 31, of which waited for: 16 -> 15; matrix products, arithmetic and copies ran while one was open for 0% -> 0% of each run, Pallas kernels for 22% -> 25%
where the time goes in v2:
time: 142 us
  starting transfers between devices  55.8 us (39%)
  waiting for transfers between devices  43.4 us (31%)
  Pallas kernels  42 us (30%)
    ppermute x31, starting transfers between devices, shift(): return lax.ppermute(value, ('dp', 'tensor'), pairs)  55.8 us
    ppermute x31, waiting for transfers between devices, shift(): return lax.ppermute(value, ('dp', 'tensor'), pairs)  43.4 us
    pallas_call x25, Pallas kernels, call(): pl.pallas_call(without(inputs, len(earlier), kernel), in_specs=[IN_SMEM]...  36.9 us
  transfers between devices with their start and end apart: 31, of which 15 were waited for; matrix products, arithmetic and copies ran while one was open for 0% of the time, Pallas kernels for 25%

profile of v2, /device:TPU:1, one launch (start us, length us, event | category | flops | bytes accessed | tf_op | source)
XLA Modules:
  0.0 142.1 jit_solution(14466464546724336600)
XLA Ops:
  0.6 1.7 %shard_map.110.refs_2_ = bf16[2,48,3072]{2,1,0:T(8,128)(2,1)S(1)} custom-call(s32[2,128]{1,0:T(2,128)} %bitcast.7, f32[1,128]{1,0:T(1,128)} %bitcast.9, bf16[128,3072]{1,0:T(8,128)(2,1)} %x.1, bf16[128,3072]{1,0:T(8,128)(2,1)} %d.1), custom_call_target="tpu_custom_call" | custom-call | flops 75497 | bytes 2200 | tf_op jit(solution)/shard_map/pallas_call | solution.py:112
  2.4 2.2 %collective-permute-start.1 = (bf16[2,48,3072]{2,1,0:T(8,128)(2,1)S(1)}, bf16[2,48,3072]{2,1,0:T(8,128)(2,1)S(1)}, u32[]{:S(2)}, u32[]{:S(2)}) collective-permute-start(bf16[2,48,3072]{2,1,0:T(8,128)(2,1)S(1)} %shard_map.110.refs_2_), channel_id=1, source_target_pairs={{0,1},{1,2},{2,3},{3,0},{4,5},{5,6},{6,7},{7,4},{8,9},{9,10},{10,1... | collective-permute-start | bytes 1769480 | tf_op jit(solution)/shard_map/ppermute | solution.py:43
  4.6 3.6 %collective-permute-start.2 = (bf16[2,48,3072]{2,1,0:T(8,128)(2,1)S(1)}, bf16[2,48,3072]{2,1,0:T(8,128)(2,1)S(1)}, u32[]{:S(2)}, u32[]{:S(2)}) collective-permute-start(bf16[2,48,3072]{2,1,0:T(8,128)(2,1)S(1)} %shard_map.110.refs_2_), channel_id=1, source_target_pairs={{0,4},{1,5},{2,6},{3,7},{4,0},{5,1},{6,2},{7,3},{8,12},{9,13},{10,... | collective-permute-start | bytes 1769480 | tf_op jit(solution)/shard_map/ppermute | solution.py:43
  8.2 1.5 %collective-permute-start = (bf16[2,48,3072]{2,1,0:T(8,128)(2,1)S(1)}, bf16[2,48,3072]{2,1,0:T(8,128)(2,1)S(1)}, u32[]{:S(2)}, u32[]{:S(2)}) collective-permute-start(bf16[2,48,3072]{2,1,0:T(8,128)(2,1)S(1)} %shard_map.110.refs_2_), channel_id=1, source_target_pairs={{0,3},{1,0},{2,1},{3,2},{4,7},{5,4},{6,5},{7,6},{8,11},{9,8},{10,9... | collective-permute-start | bytes 1769480 | tf_op jit(solution)/shard_map/ppermute | solution.py:43
  9.7 9.2 %collective-permute-done.1.refs_1_ = bf16[2,48,3072]{2,1,0:T(8,128)(2,1)S(1)} collective-permute-done((bf16[2,48,3072]{2,1,0:T(8,128)(2,1)S(1)}, bf16[2,48,3072]{2,1,0:T(8,128)(2,1)S(1)}, u32[]{:S(2)}, u32[]{:S(2)}) %collective-permute-start.1) | collective-permute-done | bytes 589856 | tf_op jit(solution)/shard_map/ppermute | solution.py:43
  18.9 3.5 %collective-permute-start.5 = (bf16[2,48,3072]{2,1,0:T(8,128)(2,1)S(1)}, bf16[2,48,3072]{2,1,0:T(8,128)(2,1)S(1)}, u32[]{:S(2)}, u32[]{:S(2)}) collective-permute-start(bf16[2,48,3072]{2,1,0:T(8,128)(2,1)S(1)} %collective-permute-done.1.refs_1_), channel_id=1, source_target_pairs={{0,4},{1,5},{2,6},{3,7},{4,0},{5,1},{6,2},{7,3},{8,12},{9,13},{10,... | collective-permute-start | bytes 1769480 | tf_op jit(solution)/shard_map/ppermute | solution.py:43
  22.4 2.7 %collective-permute-start.4 = (bf16[2,48,3072]{2,1,0:T(8,128)(2,1)S(1)}, bf16[2,48,3072]{2,1,0:T(8,128)(2,1)S(1)}, u32[]{:S(2)}, u32[]{:S(2)}) collective-permute-start(bf16[2,48,3072]{2,1,0:T(8,128)(2,1)S(1)} %collective-permute-done.2.refs_4_.refs_3_), channel_id=1, source_target_pairs={{0,3},{1,0},{2,1},{3,2},{4,7},{5,4},{6,5},{7,6},{8,11},{9,8},{10,9... | collective-permute-start | bytes 1769480 | tf_op jit(solution)/shard_map/ppermute | solution.py:43
  25.1 6.4 %shard_map.111 = (bf16[3072,1024]{1,0:T(8,128)(2,1)S(1)}, bf16[3072,1024]{1,0:T(8,128)(2,1)S(1)}, bf16[1024,3072]{1,0:T(8,128)(2,1)S(1)}, f32[8,128]{1,0:T(8,128)S(1)}) custom-call(bf16[3072,1024]{1,0:T(8,128)(2,1)} %refs_0_.1, bf16[3072,1024]{1,0:T(8,128)(2,1)} %refs_1_.1, bf16[1024,3072]{1,0:T(8,128)(2,1)} %refs_2_.1, ...), custom_call_target="tpu_custom_call" | custom-call | bytes 9438 | tf_op jit(solution)/shard_map/pallas_call | solution.py:157
  31.5 0.2 shard_map.112.refs_0_
  31.7 2.4 %collective-permute-start.8 = (bf16[2,192,3072]{2,1,0:T(8,128)(2,1)S(1)}, bf16[2,192,3072]{2,1,0:T(8,128)(2,1)S(1)}, u32[]{:S(2)}, u32[]{:S(2)}) collective-permute-start(bf16[2,192,3072]{2,1,0:T(8,128)(2,1)S(1)} %shard_map.112.refs_0_), channel_id=1, source_target_pairs={{0,8},{1,9},{2,10},{3,11},{4,12},{5,13},{6,14},{7,15},{8,0},{9,1},... | collective-permute-start | bytes 7077896 | tf_op jit(solution)/shard_map/ppermute | solution.py:43
  34.1 1.6 %collective-permute-done.4.refs_0_.refs_1_ = bf16[2,48,3072]{2,1,0:T(8,128)(2,1)S(1)} collective-permute-done((bf16[2,48,3072]{2,1,0:T(8,128)(2,1)S(1)}, bf16[2,48,3072]{2,1,0:T(8,128)(2,1)S(1)}, u32[]{:S(2)}, u32[]{:S(2)}) %collective-permute-start.4) | collective-permute-done | bytes 589856 | tf_op jit(solution)/shard_map/ppermute | solution.py:43
  35.7 1.0 collective-permute-done.3.refs_0_
  36.7 0.1 shard_map.114.refs_1_
  36.8 2.8 %collective-permute-start.9 = (bf16[2,144,3072]{2,1,0:T(8,128)(2,1)S(1)}, bf16[2,144,3072]{2,1,0:T(8,128)(2,1)S(1)}, u32[]{:S(2)}, u32[]{:S(2)}) collective-permute-start(bf16[2,144,3072]{2,1,0:T(8,128)(2,1)S(1)} %shard_map.114.refs_1_), channel_id=1, source_target_pairs={{0,8},{1,9},{2,10},{3,11},{4,12},{5,13},{6,14},{7,15},{8,0},{9,1},... | collective-permute-start | bytes 5308424 | tf_op jit(solution)/shard_map/ppermute | solution.py:43
  39.6 2.7 %collective-permute-start.7 = (bf16[48,3072]{1,0:T(8,128)(2,1)S(1)}, bf16[48,3072]{1,0:T(8,128)(2,1)S(1)}, u32[]{:S(2)}, u32[]{:S(2)}) collective-permute-start(bf16[48,3072]{1,0:T(8,128)(2,1)S(1)} %shard_map.113.refs_3_.refs_1_), channel_id=1, source_target_pairs={{0,3},{1,0},{2,1},{3,2},{4,7},{5,4},{6,5},{7,6},{8,11},{9,8},{10,9... | collective-permute-start | bytes 884744 | tf_op jit(solution)/shard_map/ppermute | solution.py:43
  42.4 4.6 %shard_map.116 = (bf16[384,1024]{1,0:T(8,128)(2,1)S(1)}, f32[384,1024]{1,0:T(8,128)S(1)}, f32[384,1024]{1,0:T(8,128)S(1)}) custom-call(bf16[2,192,3072]{2,1,0:T(8,128)(2,1)S(1)} %shard_map.112.refs_0_, bf16[2,144,3072]{2,1,0:T(8,128)(2,1)S(1)} %shard_map.114.refs_1_, bf16[3072,1024]{1,0:T(8,128)(2,1)S(1)} %get-tuple-element.58.refs_2_.refs_1_, ...), custom_call_target="tpu_custom_call" | custom-call | flops 4227858 | bytes 9535 | tf_op jit(solution)/shard_map/pallas_call | solution.py:157
  47.0 1.7 %collective-permute-done.7.refs_0_ = bf16[48,3072]{1,0:T(8,128)(2,1)S(1)} collective-permute-done((bf16[48,3072]{1,0:T(8,128)(2,1)S(1)}, bf16[48,3072]{1,0:T(8,128)(2,1)S(1)}, u32[]{:S(2)}, u32[]{:S(2)}) %collective-permute-start.7) | collective-permute-done | bytes 294944 | tf_op jit(solution)/shard_map/ppermute | solution.py:43
  48.7 2.3 %shard_map.117 = (bf16[384,1024]{1,0:T(8,128)(2,1)S(1)}, f32[384,1024]{1,0:T(8,128)S(1)}, f32[384,1024]{1,0:T(8,128)S(1)}) custom-call(bf16[48,3072]{1,0:T(8,128)(2,1)S(1)} %collective-permute-done.7.refs_0_, bf16[3072,1024]{1,0:T(8,128)(2,1)S(1)} %get-tuple-element.58.refs_2_.refs_1_, ...), custom_call_target="tpu_custom_call", output_to_operand_aliasing={{0}: (3, {}), {1}: (4, {}), {2}: (5, {})} | custom-call | flops 603979 | bytes 8798 | tf_op jit(solution)/shard_map/pallas_call | solution.py:157
  51.0 0.9 collective-permute-done.6.refs_2_.refs_1_
  51.8 1.4 %shard_map.118 = (bf16[384,3072]{1,0:T(8,128)(2,1)S(1)}, bf16[3,384,512]{2,1,0:T(8,128)(2,1)S(1)}) custom-call(bf16[2,192,3072]{2,1,0:T(8,128)(2,1)S(1)} %shard_map.112.refs_0_, bf16[2,144,3072]{2,1,0:T(8,128)(2,1)S(1)} %shard_map.114.refs_1_, bf16[48,3072]{1,0:T(8,128)(2,1)S(1)} %collective-permute-done.6.refs_2_.refs_1_, ...), custom_call_target="tpu_custom_call" | custom-call | flops 1207959 | bytes 8306 | tf_op jit(solution)/shard_map/pallas_call | solution.py:157
  53.3 1.3 collective-permute-start.11
  54.6 0.3 collective-permute-start.10
  54.9 1.4 %shard_map.119.refs_6_.refs_0_ = bf16[2,384,512]{2,1,0:T(8,128)(2,1)S(1)} custom-call(bf16[384,3072]{1,0:T(8,128)(2,1)S(1)} %get-tuple-element.66.refs_0_, bf16[1024,3072]{1,0:T(8,128)(2,1)S(1)} %get-tuple-element.57.refs_3_.refs_1_, f32[384,1024]{1,0:T(8,128)S(1)} %get-tuple-element.64.refs_5_.refs_2_, f32[384,1024]{1,0:T(8,128)S(1)} %get-tuple-element.65.refs_6_.refs_3_), custom_call_target="tpu_custom_call" | custom-call | flops 1207959 | bytes 5505 | tf_op jit(solution)/shard_map/pallas_call | solution.py:157
  56.3 1.6 %collective-permute-done.10.refs_5_ = bf16[2,48,3072]{2,1,0:T(8,128)(2,1)S(1)} collective-permute-done((bf16[2,48,3072]{2,1,0:T(8,128)(2,1)S(1)}, bf16[2,48,3072]{2,1,0:T(8,128)(2,1)S(1)}, u32[]{:S(2)}, u32[]{:S(2)}) %collective-permute-start.10) | collective-permute-done | bytes 589856 | tf_op jit(solution)/shard_map/ppermute | solution.py:43
  57.9 1.8 %shard_map.121 = (bf16[2,384,512]{2,1,0:T(8,128)(2,1)S(1)}, bf16[2,384,512]{2,1,0:T(8,128)(2,1)S(1)}) custom-call(bf16[2,192,3072]{2,1,0:T(8,128)(2,1)S(1)} %shard_map.112.refs_0_, bf16[2,144,3072]{2,1,0:T(8,128)(2,1)S(1)} %shard_map.114.refs_1_, bf16[2,48,3072]{2,1,0:T(8,128)(2,1)S(1)} %shard_map.120.refs_2_, ...), custom_call_target="tpu_custom_call" | custom-call | flops 1207959 | bytes 6488 | tf_op jit(solution)/shard_map/pallas_call | solution.py:157
  59.7 2.5 %collective-permute-start.15 = (bf16[2,384,512]{2,1,0:T(8,128)(2,1)S(1)}, bf16[2,384,512]{2,1,0:T(8,128)(2,1)S(1)}, u32[]{:S(2)}, u32[]{:S(2)}) collective-permute-start(bf16[2,384,512]{2,1,0:T(8,128)(2,1)S(1)} %get-tuple-element.76), channel_id=1, source_target_pairs={{0,96},{1,97},{2,98},{3,99},{4,100},{5,101},{6,102},{7,103},{8,104... | collective-permute-start | bytes 2359304 | tf_op jit(solution)/shard_map/ppermute | solution.py:43
  62.2 3.6 %shard_map.122 = (bf16[4,384,512]{2,1,0:T(8,128)(2,1)S(1)}, bf16[4,384,512]{2,1,0:T(8,128)(2,1)S(1)}) custom-call(bf16[2,192,3072]{2,1,0:T(8,128)(2,1)S(1)} %shard_map.112.refs_0_, bf16[2,144,3072]{2,1,0:T(8,128)(2,1)S(1)} %shard_map.114.refs_1_, bf16[2,48,3072]{2,1,0:T(8,128)(2,1)S(1)} %shard_map.120.refs_2_, ...), custom_call_target="tpu_custom_call" | custom-call | flops 2415919 | bytes 7274 | tf_op jit(solution)/shard_map/pallas_call | solution.py:157
  65.8 0.8 collective-permute-start.21
  66.6 2.6 %shard_map.123.refs_4_ = bf16[384,3072]{1,0:T(8,128)(2,1)S(1)} custom-call(bf16[384,1024]{1,0:T(8,128)(2,1)S(1)} %get-tuple-element.63.refs_4_.refs_6_.refs_0_, bf16[1024,3072]{1,0:T(8,128)(2,1)S(1)} %get-tuple-element.57.refs_3_.refs_1_, bf16[4,384,512]{2,1,0:T(8,128)(2,1)S(1)} %get-tuple-element.69.refs_2_.refs_0_), custom_call_target="tpu_custom_call" | custom-call | flops 2415919 | bytes 4718 | tf_op jit(solution)/shard_map/pallas_call | solution.py:157
  69.2 5.1 %shard_map.124 = (bf16[2,48,3072]{2,1,0:T(8,128)(2,1)S(1)}, bf16[2,48,3072]{2,1,0:T(8,128)(2,1)S(1)}, bf16[2,2,48,3072]{3,2,1,0:T(8,128)(2,1)S(1)}, bf16[2,2,48,...) custom-call(bf16[2,384,512]{2,1,0:T(8,128)(2,1)S(1)} %shard_map.119.refs_6_.refs_0_, ...), custom_call_target="tpu_custom_call" | custom-call | flops 4831838 | bytes 10813 | tf_op jit(solution)/shard_map/pallas_call | solution.py:157
  74.5 2.7 %collective-permute-start.13 = (bf16[2,48,3072]{2,1,0:T(8,128)(2,1)S(1)}, bf16[2,48,3072]{2,1,0:T(8,128)(2,1)S(1)}, u32[]{:S(2)}, u32[]{:S(2)}) collective-permute-start(bf16[2,48,3072]{2,1,0:T(8,128)(2,1)S(1)} %get-tuple-element.74), channel_id=1, source_target_pairs={{0,3},{1,0},{2,1},{3,2},{4,7},{5,4},{6,5},{7,6},{8,11},{9,8},{10,9... | collective-permute-start | bytes 1769480 | tf_op jit(solution)/shard_map/ppermute | solution.py:43
  77.1 1.4 %shard_map.125 = (bf16[2,384,512]{2,1,0:T(8,128)(2,1)S(1)}, bf16[2,384,512]{2,1,0:T(8,128)(2,1)S(1)}) custom-call(bf16[2,192,3072]{2,1,0:T(8,128)(2,1)S(1)} %shard_map.112.refs_0_, bf16[2,144,3072]{2,1,0:T(8,128)(2,1)S(1)} %shard_map.114.refs_1_, bf16[2,48,3072]{2,1,0:T(8,128)(2,1)S(1)} %shard_map.120.refs_2_, ...), custom_call_target="tpu_custom_call" | custom-call | flops 1207959 | bytes 6488 | tf_op jit(solution)/shard_map/pallas_call | solution.py:157
  78.6 0.2 collective-permute-done.15.refs_1_
  78.8 3.1 %collective-permute-done.14.refs_1_ = bf16[2,384,512]{2,1,0:T(8,128)(2,1)S(1)} collective-permute-done((bf16[2,384,512]{2,1,0:T(8,128)(2,1)S(1)}, bf16[2,384,512]{2,1,0:T(8,128)(2,1)S(1)}, u32[]{:S(2)}, u32[]{:S(2)}) %collective-permute-start.14) | collective-permute-done | bytes 786464 | tf_op jit(solution)/shard_map/ppermute | solution.py:43
  81.8 0.2 shard_map.126.refs_8_
  82.1 2.7 %collective-permute-start.20 = (bf16[2,384,512]{2,1,0:T(8,128)(2,1)S(1)}, bf16[2,384,512]{2,1,0:T(8,128)(2,1)S(1)}, u32[]{:S(2)}, u32[]{:S(2)}) collective-permute-start(bf16[2,384,512]{2,1,0:T(8,128)(2,1)S(1)} %shard_map.126.refs_8_), channel_id=1, source_target_pairs={{0,96},{1,97},{2,98},{3,99},{4,100},{5,101},{6,102},{7,103},{8,104... | collective-permute-start | bytes 2359304 | tf_op jit(solution)/shard_map/ppermute | solution.py:43
  84.8 3.0 %shard_map.127 = (bf16[2,384,512]{2,1,0:T(8,128)(2,1)S(1)}, bf16[2,384,512]{2,1,0:T(8,128)(2,1)S(1)}, bf16[2,384,512]{2,1,0:T(8,128)(2,1)S(1)}, bf16[2,384,512]{2,1,0:T(8,128)(2,1)S(1)}) custom-call(bf16[2,192,3072]{2,1,0:T(8,128)(2,1)S(1)} %shard_map.112.refs_0_, bf16[2,144,3072]{2,1,0:T(8,128)(2,1)S(1)} %shard_map.114.refs_1_, ...), custom_call_target="tpu_custom_call" | custom-call | flops 2415919 | bytes 7274 | tf_op jit(solution)/shard_map/pallas_call | solution.py:157
  87.8 0.2 shard_map.128.refs_4_
  88.0 1.6 %collective-permute-done.12.refs_1_ = bf16[2,48,3072]{2,1,0:T(8,128)(2,1)S(1)} collective-permute-done((bf16[2,48,3072]{2,1,0:T(8,128)(2,1)S(1)}, bf16[2,48,3072]{2,1,0:T(8,128)(2,1)S(1)}, u32[]{:S(2)}, u32[]{:S(2)}) %collective-permute-start.12) | collective-permute-done | bytes 589856 | tf_op jit(solution)/shard_map/ppermute | solution.py:43
  89.5 0.3 shard_map.129
  89.9 0.5 collective-permute-start.16
  90.3 2.3 %collective-permute-start.17 = (bf16[2,2,48,3072]{3,2,1,0:T(8,128)(2,1)S(1)}, bf16[2,2,48,3072]{3,2,1,0:T(8,128)(2,1)S(1)}, u32[]{:S(2)}, u32[]{:S(2)}) collective-permute-start(bf16[2,2,48,3072]{3,2,1,0:T(8,128)(2,1)S(1)} %get-tuple-element.81), channel_id=1, source_target_pairs={{0,3},{1,0},{2,1},{3,2},{4,7},{5,4},{6,5},{7,6},{8,11},{9,8},{10,9... | collective-permute-start | bytes 3538952 | tf_op jit(solution)/shard_map/ppermute | solution.py:43
  92.6 8.2 %collective-permute-done.19.refs_1_ = bf16[2,384,512]{2,1,0:T(8,128)(2,1)S(1)} collective-permute-done((bf16[2,384,512]{2,1,0:T(8,128)(2,1)S(1)}, bf16[2,384,512]{2,1,0:T(8,128)(2,1)S(1)}, u32[]{:S(2)}, u32[]{:S(2)}) %collective-permute-start.19) | collective-permute-done | bytes 786464 | tf_op jit(solution)/shard_map/ppermute | solution.py:43
  100.8 0.3 shard_map.132.refs_2_
  101.2 0.4 shard_map.135
  101.6 2.7 %collective-permute-start.27 = (bf16[192,512]{1,0:T(8,128)(2,1)S(1)}, bf16[192,512]{1,0:T(8,128)(2,1)S(1)}, u32[]{:S(2)}, u32[]{:S(2)}) collective-permute-start(bf16[192,512]{1,0:T(8,128)(2,1)S(1)} %get-tuple-element.102), channel_id=1, source_target_pairs={{0,96},{1,97},{2,98},{3,99},{4,100},{5,101},{6,102},{7,103},{8,104... | collective-permute-start | bytes 589832 | tf_op jit(solution)/shard_map/ppermute | solution.py:43
  104.3 0.7 collective-permute-start.24
  105.0 2.6 %collective-permute-done.26.refs_1_ = bf16[192,512]{1,0:T(8,128)(2,1)S(1)} collective-permute-done((bf16[192,512]{1,0:T(8,128)(2,1)S(1)}, bf16[192,512]{1,0:T(8,128)(2,1)S(1)}, u32[]{:S(2)}, u32[]{:S(2)}) %collective-permute-start.26) | collective-permute-done | bytes 196640 | tf_op jit(solution)/shard_map/ppermute | solution.py:43
  107.6 2.7 %collective-permute-start.23 = (bf16[2,384,512]{2,1,0:T(8,128)(2,1)S(1)}, bf16[2,384,512]{2,1,0:T(8,128)(2,1)S(1)}, u32[]{:S(2)}, u32[]{:S(2)}) collective-permute-start(bf16[2,384,512]{2,1,0:T(8,128)(2,1)S(1)} %get-tuple-element.92), channel_id=1, source_target_pairs={{0,96},{1,97},{2,98},{3,99},{4,100},{5,101},{6,102},{7,103},{8,104... | collective-permute-start | bytes 2359304 | tf_op jit(solution)/shard_map/ppermute | solution.py:43
  110.3 0.1 shard_map.136
  110.4 6.3 %collective-permute-done.16.refs_1_ = bf16[2,2,48,3072]{3,2,1,0:T(8,128)(2,1)S(1)} collective-permute-done((bf16[2,2,48,3072]{3,2,1,0:T(8,128)(2,1)S(1)}, bf16[2,2,48,3072]{3,2,1,0:T(8,128)(2,1)S(1)}, u32[]{:S(2)}, u32[]{:S(2)}) %collective-permute-start.16) | collective-permute-done | bytes 1179680 | tf_op jit(solution)/shard_map/ppermute | solution.py:43
  116.8 2.7 %collective-permute-start.29 = (bf16[2,192,512]{2,1,0:T(8,128)(2,1)S(1)}, bf16[2,192,512]{2,1,0:T(8,128)(2,1)S(1)}, u32[]{:S(2)}, u32[]{:S(2)}) collective-permute-start(bf16[2,192,512]{2,1,0:T(8,128)(2,1)S(1)} %get-tuple-element.104), channel_id=1, source_target_pairs={{0,96},{1,97},{2,98},{3,99},{4,100},{5,101},{6,102},{7,103},{8,104... | collective-permute-start | bytes 1179656 | tf_op jit(solution)/shard_map/ppermute | solution.py:43
  119.4 0.4 shard_map.130
  119.8 0.5 collective-permute-done.24.refs_3_
  120.3 0.5 collective-permute-start.18
  120.8 3.8 %collective-permute-done.22.refs_1_ = bf16[2,384,512]{2,1,0:T(8,128)(2,1)S(1)} collective-permute-done((bf16[2,384,512]{2,1,0:T(8,128)(2,1)S(1)}, bf16[2,384,512]{2,1,0:T(8,128)(2,1)S(1)}, u32[]{:S(2)}, u32[]{:S(2)}) %collective-permute-start.22) | collective-permute-done | bytes 786464 | tf_op jit(solution)/shard_map/ppermute | solution.py:43
  124.6 0.8 shard_map.133
  125.4 8.1 %collective-permute-start.25 = (bf16[2,192,512]{2,1,0:T(8,128)(2,1)S(1)}, bf16[2,192,512]{2,1,0:T(8,128)(2,1)S(1)}, u32[]{:S(2)}, u32[]{:S(2)}) collective-permute-start(bf16[2,192,512]{2,1,0:T(8,128)(2,1)S(1)} %get-tuple-element.95), channel_id=1, source_target_pairs={{0,8},{1,9},{2,10},{3,11},{4,12},{5,13},{6,14},{7,15},{8,0},{9,1},... | collective-permute-start | bytes 1179656 | tf_op jit(solution)/shard_map/ppermute | solution.py:43
  133.5 0.3 shard_map.137
  133.8 3.8 %collective-permute-start.30 = (bf16[1,192,512]{2,1,0:T(8,128)(2,1)S(1)}, bf16[1,192,512]{2,1,0:T(8,128)(2,1)S(1)}, u32[]{:S(2)}, u32[]{:S(2)}) collective-permute-start(bf16[1,192,512]{2,1,0:T(8,128)(2,1)S(1)} %get-tuple-element.106), channel_id=1, source_target_pairs={{0,8},{1,9},{2,10},{3,11},{4,12},{5,13},{6,14},{7,15},{8,0},{9,1},... | collective-permute-start | bytes 589832 | tf_op jit(solution)/shard_map/ppermute | solution.py:43
  137.6 1.1 collective-permute-done.30.got
  138.6 0.8 shard_map.138
  139.4 1.7 %shard_map.131 = (bf16[128,3072]{1,0:T(8,128)(2,1)}, bf16[128,3072]{1,0:T(8,128)(2,1)}) custom-call(s32[2,128]{1,0:T(2,128)S(1)} %bitcast.8, f32[1,128]{1,0:T(1,128)S(1)} %bitcast.10, bf16[2,48,3072]{2,1,0:T(8,128)(2,1)S(1)} %get-tuple-element.82.kept, bf16[2,48,3072]{2,1,0:T(8,128)(2,1)S(1)} %collective-permute-done.18.got), custom_call_target="tpu_custom_call" | custom-call | flops 75497 | bytes 2800 | tf_op jit(solution)/shard_map/pallas_call | solution.py:133
  141.2 0.9 shard_map.134
  (31 shorter events, 0.5 us)
Async XLA Ops:
  2.4 16.5 %collective-permute-start.1 = (bf16[2,48,3072]{2,1,0:T(8,128)(2,1)S(1)}, bf16[2,48,3072]{2,1,0:T(8,128)(2,1)S(1)}, u32[]{:S(2)}, u32[]{:S(2)}) collective-permute-start(bf16[2,48,3072]{2,1,0:T(8,128)(2,1)S(1)} %shard_map.110.refs_2_), channel_id=1, source_target_pairs={{0,1},{1,2},{2,3},{3,0},{4,5},{5,6},{6,7},{7,4},{8,9},{9,10},{10,1... | collective-permute-start | bytes 1769480 | tf_op jit(solution)/shard_map/ppermute | solution.py:43
  4.6 17.9 %collective-permute-start.2 = (bf16[2,48,3072]{2,1,0:T(8,128)(2,1)S(1)}, bf16[2,48,3072]{2,1,0:T(8,128)(2,1)S(1)}, u32[]{:S(2)}, u32[]{:S(2)}) collective-permute-start(bf16[2,48,3072]{2,1,0:T(8,128)(2,1)S(1)} %shard_map.110.refs_2_), channel_id=1, source_target_pairs={{0,4},{1,5},{2,6},{3,7},{4,0},{5,1},{6,2},{7,3},{8,12},{9,13},{10,... | collective-permute-start | bytes 1769480 | tf_op jit(solution)/shard_map/ppermute | solution.py:43
  8.2 16.9 %collective-permute-start = (bf16[2,48,3072]{2,1,0:T(8,128)(2,1)S(1)}, bf16[2,48,3072]{2,1,0:T(8,128)(2,1)S(1)}, u32[]{:S(2)}, u32[]{:S(2)}) collective-permute-start(bf16[2,48,3072]{2,1,0:T(8,128)(2,1)S(1)} %shard_map.110.refs_2_), channel_id=1, source_target_pairs={{0,3},{1,0},{2,1},{3,2},{4,7},{5,4},{6,5},{7,6},{8,11},{9,8},{10,9... | collective-permute-start | bytes 1769480 | tf_op jit(solution)/shard_map/ppermute | solution.py:43
  18.9 16.8 %collective-permute-start.5 = (bf16[2,48,3072]{2,1,0:T(8,128)(2,1)S(1)}, bf16[2,48,3072]{2,1,0:T(8,128)(2,1)S(1)}, u32[]{:S(2)}, u32[]{:S(2)}) collective-permute-start(bf16[2,48,3072]{2,1,0:T(8,128)(2,1)S(1)} %collective-permute-done.1.refs_1_), channel_id=1, source_target_pairs={{0,4},{1,5},{2,6},{3,7},{4,0},{5,1},{6,2},{7,3},{8,12},{9,13},{10,... | collective-permute-start | bytes 1769480 | tf_op jit(solution)/shard_map/ppermute | solution.py:43
  22.4 14.3 %collective-permute-start.3 = (bf16[2,48,3072]{2,1,0:T(8,128)(2,1)S(1)}, bf16[2,48,3072]{2,1,0:T(8,128)(2,1)S(1)}, u32[]{:S(2)}, u32[]{:S(2)}) collective-permute-start(bf16[2,48,3072]{2,1,0:T(8,128)(2,1)S(1)} %collective-permute-done.1.refs_1_), channel_id=1, source_target_pairs={{0,1},{1,2},{2,3},{3,0},{4,5},{5,6},{6,7},{7,4},{8,9},{9,10},{10,1... | collective-permute-start | bytes 1769480 | tf_op jit(solution)/shard_map/ppermute | solution.py:43
  22.4 13.3 %collective-permute-start.4 = (bf16[2,48,3072]{2,1,0:T(8,128)(2,1)S(1)}, bf16[2,48,3072]{2,1,0:T(8,128)(2,1)S(1)}, u32[]{:S(2)}, u32[]{:S(2)}) collective-permute-start(bf16[2,48,3072]{2,1,0:T(8,128)(2,1)S(1)} %collective-permute-done.2.refs_4_.refs_3_), channel_id=1, source_target_pairs={{0,3},{1,0},{2,1},{3,2},{4,7},{5,4},{6,5},{7,6},{8,11},{9,8},{10,9... | collective-permute-start | bytes 1769480 | tf_op jit(solution)/shard_map/ppermute | solution.py:43
  31.7 17.0 %collective-permute-start.8 = (bf16[2,192,3072]{2,1,0:T(8,128)(2,1)S(1)}, bf16[2,192,3072]{2,1,0:T(8,128)(2,1)S(1)}, u32[]{:S(2)}, u32[]{:S(2)}) collective-permute-start(bf16[2,192,3072]{2,1,0:T(8,128)(2,1)S(1)} %shard_map.112.refs_0_), channel_id=1, source_target_pairs={{0,8},{1,9},{2,10},{3,11},{4,12},{5,13},{6,14},{7,15},{8,0},{9,1},... | collective-permute-start | bytes 7077896 | tf_op jit(solution)/shard_map/ppermute | solution.py:43
  36.8 11.9 %collective-permute-start.9 = (bf16[2,144,3072]{2,1,0:T(8,128)(2,1)S(1)}, bf16[2,144,3072]{2,1,0:T(8,128)(2,1)S(1)}, u32[]{:S(2)}, u32[]{:S(2)}) collective-permute-start(bf16[2,144,3072]{2,1,0:T(8,128)(2,1)S(1)} %shard_map.114.refs_1_), channel_id=1, source_target_pairs={{0,8},{1,9},{2,10},{3,11},{4,12},{5,13},{6,14},{7,15},{8,0},{9,1},... | collective-permute-start | bytes 5308424 | tf_op jit(solution)/shard_map/ppermute | solution.py:43
  39.6 9.1 %collective-permute-start.7 = (bf16[48,3072]{1,0:T(8,128)(2,1)S(1)}, bf16[48,3072]{1,0:T(8,128)(2,1)S(1)}, u32[]{:S(2)}, u32[]{:S(2)}) collective-permute-start(bf16[48,3072]{1,0:T(8,128)(2,1)S(1)} %shard_map.113.refs_3_.refs_1_), channel_id=1, source_target_pairs={{0,3},{1,0},{2,1},{3,2},{4,7},{5,4},{6,5},{7,6},{8,11},{9,8},{10,9... | collective-permute-start | bytes 884744 | tf_op jit(solution)/shard_map/ppermute | solution.py:43
  42.3 9.5 %collective-permute-start.6 = (bf16[48,3072]{1,0:T(8,128)(2,1)S(1)}, bf16[48,3072]{1,0:T(8,128)(2,1)S(1)}, u32[]{:S(2)}, u32[]{:S(2)}) collective-permute-start(bf16[48,3072]{1,0:T(8,128)(2,1)S(1)} %shard_map.115.refs_4_), channel_id=1, source_target_pairs={{0,1},{1,2},{2,3},{3,0},{4,5},{5,6},{6,7},{7,4},{8,9},{9,10},{10,1... | collective-permute-start | bytes 884744 | tf_op jit(solution)/shard_map/ppermute | solution.py:43
  53.3 4.6 %collective-permute-start.11 = (bf16[3,384,512]{2,1,0:T(8,128)(2,1)S(1)}, bf16[3,384,512]{2,1,0:T(8,128)(2,1)S(1)}, u32[]{:S(2)}, u32[]{:S(2)}) collective-permute-start(bf16[3,384,512]{2,1,0:T(8,128)(2,1)S(1)} %get-tuple-element.67.refs_1_), channel_id=1, source_target_pairs={{0,8},{1,9},{2,10},{3,11},{4,12},{5,13},{6,14},{7,15},{8,0},{9,1},... | collective-permute-start | bytes 3538952 | tf_op jit(solution)/shard_map/ppermute | solution.py:43
  54.6 3.3 %collective-permute-start.10 = (bf16[2,48,3072]{2,1,0:T(8,128)(2,1)S(1)}, bf16[2,48,3072]{2,1,0:T(8,128)(2,1)S(1)}, u32[]{:S(2)}, u32[]{:S(2)}) collective-permute-start(bf16[2,48,3072]{2,1,0:T(8,128)(2,1)S(1)} %shard_map.120.refs_2_), channel_id=1, source_target_pairs={{0,8},{1,9},{2,10},{3,11},{4,12},{5,13},{6,14},{7,15},{8,0},{9,1},... | collective-permute-start | bytes 1769480 | tf_op jit(solution)/shard_map/ppermute | solution.py:43
  59.7 19.1 %collective-permute-start.15 = (bf16[2,384,512]{2,1,0:T(8,128)(2,1)S(1)}, bf16[2,384,512]{2,1,0:T(8,128)(2,1)S(1)}, u32[]{:S(2)}, u32[]{:S(2)}) collective-permute-start(bf16[2,384,512]{2,1,0:T(8,128)(2,1)S(1)} %get-tuple-element.76), channel_id=1, source_target_pairs={{0,96},{1,97},{2,98},{3,99},{4,100},{5,101},{6,102},{7,103},{8,104... | collective-permute-start | bytes 2359304 | tf_op jit(solution)/shard_map/ppermute | solution.py:43
  62.2 19.6 %collective-permute-start.14 = (bf16[2,384,512]{2,1,0:T(8,128)(2,1)S(1)}, bf16[2,384,512]{2,1,0:T(8,128)(2,1)S(1)}, u32[]{:S(2)}, u32[]{:S(2)}) collective-permute-start(bf16[2,384,512]{2,1,0:T(8,128)(2,1)S(1)} %get-tuple-element.68.refs_8_), channel_id=1, source_target_pairs={{0,32},{1,33},{2,34},{3,35},{4,36},{5,37},{6,38},{7,39},{8,40},{9,... | collective-permute-start | bytes 2359304 | tf_op jit(solution)/shard_map/ppermute | solution.py:43
  65.8 35.4 %collective-permute-start.21 = (bf16[4,384,512]{2,1,0:T(8,128)(2,1)S(1)}, bf16[4,384,512]{2,1,0:T(8,128)(2,1)S(1)}, u32[]{:S(2)}, u32[]{:S(2)}) collective-permute-start(bf16[4,384,512]{2,1,0:T(8,128)(2,1)S(1)} %get-tuple-element.90), channel_id=1, source_target_pairs={{0,16},{1,17},{2,18},{3,19},{4,20},{5,21},{6,22},{7,23},{8,24},{9,... | collective-permute-start | bytes 4718600 | tf_op jit(solution)/shard_map/ppermute | solution.py:43
  74.4 15.2 %collective-permute-start.12 = (bf16[2,48,3072]{2,1,0:T(8,128)(2,1)S(1)}, bf16[2,48,3072]{2,1,0:T(8,128)(2,1)S(1)}, u32[]{:S(2)}, u32[]{:S(2)}) collective-permute-start(bf16[2,48,3072]{2,1,0:T(8,128)(2,1)S(1)} %get-tuple-element.72), channel_id=1, source_target_pairs={{0,1},{1,2},{2,3},{3,0},{4,5},{5,6},{6,7},{7,4},{8,9},{9,10},{10,1... | collective-permute-start | bytes 1769480 | tf_op jit(solution)/shard_map/ppermute | solution.py:43
  74.5 15.1 %collective-permute-start.13 = (bf16[2,48,3072]{2,1,0:T(8,128)(2,1)S(1)}, bf16[2,48,3072]{2,1,0:T(8,128)(2,1)S(1)}, u32[]{:S(2)}, u32[]{:S(2)}) collective-permute-start(bf16[2,48,3072]{2,1,0:T(8,128)(2,1)S(1)} %get-tuple-element.74), channel_id=1, source_target_pairs={{0,3},{1,0},{2,1},{3,2},{4,7},{5,4},{6,5},{7,6},{8,11},{9,8},{10,9... | collective-permute-start | bytes 1769480 | tf_op jit(solution)/shard_map/ppermute | solution.py:43
  82.0 18.8 %collective-permute-start.19 = (bf16[2,384,512]{2,1,0:T(8,128)(2,1)S(1)}, bf16[2,384,512]{2,1,0:T(8,128)(2,1)S(1)}, u32[]{:S(2)}, u32[]{:S(2)}) collective-permute-start(bf16[2,384,512]{2,1,0:T(8,128)(2,1)S(1)} %get-tuple-element.89), channel_id=1, source_target_pairs={{0,32},{1,33},{2,34},{3,35},{4,36},{5,37},{6,38},{7,39},{8,40},{9,... | collective-permute-start | bytes 2359304 | tf_op jit(solution)/shard_map/ppermute | solution.py:43
  82.1 18.7 %collective-permute-start.20 = (bf16[2,384,512]{2,1,0:T(8,128)(2,1)S(1)}, bf16[2,384,512]{2,1,0:T(8,128)(2,1)S(1)}, u32[]{:S(2)}, u32[]{:S(2)}) collective-permute-start(bf16[2,384,512]{2,1,0:T(8,128)(2,1)S(1)} %shard_map.126.refs_8_), channel_id=1, source_target_pairs={{0,96},{1,97},{2,98},{3,99},{4,100},{5,101},{6,102},{7,103},{8,104... | collective-permute-start | bytes 2359304 | tf_op jit(solution)/shard_map/ppermute | solution.py:43
  89.9 26.9 %collective-permute-start.16 = (bf16[2,2,48,3072]{3,2,1,0:T(8,128)(2,1)S(1)}, bf16[2,2,48,3072]{3,2,1,0:T(8,128)(2,1)S(1)}, u32[]{:S(2)}, u32[]{:S(2)}) collective-permute-start(bf16[2,2,48,3072]{3,2,1,0:T(8,128)(2,1)S(1)} %get-tuple-element.80), channel_id=1, source_target_pairs={{0,1},{1,2},{2,3},{3,0},{4,5},{5,6},{6,7},{7,4},{8,9},{9,10},{10,1... | collective-permute-start | bytes 3538952 | tf_op jit(solution)/shard_map/ppermute | solution.py:43
  90.3 26.4 %collective-permute-start.17 = (bf16[2,2,48,3072]{3,2,1,0:T(8,128)(2,1)S(1)}, bf16[2,2,48,3072]{3,2,1,0:T(8,128)(2,1)S(1)}, u32[]{:S(2)}, u32[]{:S(2)}) collective-permute-start(bf16[2,2,48,3072]{3,2,1,0:T(8,128)(2,1)S(1)} %get-tuple-element.81), channel_id=1, source_target_pairs={{0,3},{1,0},{2,1},{3,2},{4,7},{5,4},{6,5},{7,6},{8,11},{9,8},{10,9... | collective-permute-start | bytes 3538952 | tf_op jit(solution)/shard_map/ppermute | solution.py:43
  101.5 6.1 %collective-permute-start.26 = (bf16[192,512]{1,0:T(8,128)(2,1)S(1)}, bf16[192,512]{1,0:T(8,128)(2,1)S(1)}, u32[]{:S(2)}, u32[]{:S(2)}) collective-permute-start(bf16[192,512]{1,0:T(8,128)(2,1)S(1)} %get-tuple-element.100), channel_id=1, source_target_pairs={{0,32},{1,33},{2,34},{3,35},{4,36},{5,37},{6,38},{7,39},{8,40},{9,... | collective-permute-start | bytes 589832 | tf_op jit(solution)/shard_map/ppermute | solution.py:43
  101.6 6.0 %collective-permute-start.27 = (bf16[192,512]{1,0:T(8,128)(2,1)S(1)}, bf16[192,512]{1,0:T(8,128)(2,1)S(1)}, u32[]{:S(2)}, u32[]{:S(2)}) collective-permute-start(bf16[192,512]{1,0:T(8,128)(2,1)S(1)} %get-tuple-element.102), channel_id=1, source_target_pairs={{0,96},{1,97},{2,98},{3,99},{4,100},{5,101},{6,102},{7,103},{8,104... | collective-permute-start | bytes 589832 | tf_op jit(solution)/shard_map/ppermute | solution.py:43
  104.3 16.1 %collective-permute-start.24 = (bf16[2,384,512]{2,1,0:T(8,128)(2,1)S(1)}, bf16[2,384,512]{2,1,0:T(8,128)(2,1)S(1)}, u32[]{:S(2)}, u32[]{:S(2)}) collective-permute-start(bf16[2,384,512]{2,1,0:T(8,128)(2,1)S(1)} %shard_map.132.refs_2_), channel_id=1, source_target_pairs={{0,16},{1,17},{2,18},{3,19},{4,20},{5,21},{6,22},{7,23},{8,24},{9,... | collective-permute-start | bytes 2359304 | tf_op jit(solution)/shard_map/ppermute | solution.py:43
  107.6 17.0 %collective-permute-start.22 = (bf16[2,384,512]{2,1,0:T(8,128)(2,1)S(1)}, bf16[2,384,512]{2,1,0:T(8,128)(2,1)S(1)}, u32[]{:S(2)}, u32[]{:S(2)}) collective-permute-start(bf16[2,384,512]{2,1,0:T(8,128)(2,1)S(1)} %shard_map.128.refs_4_), channel_id=1, source_target_pairs={{0,32},{1,33},{2,34},{3,35},{4,36},{5,37},{6,38},{7,39},{8,40},{9,... | collective-permute-start | bytes 2359304 | tf_op jit(solution)/shard_map/ppermute | solution.py:43
  107.6 17.0 %collective-permute-start.23 = (bf16[2,384,512]{2,1,0:T(8,128)(2,1)S(1)}, bf16[2,384,512]{2,1,0:T(8,128)(2,1)S(1)}, u32[]{:S(2)}, u32[]{:S(2)}) collective-permute-start(bf16[2,384,512]{2,1,0:T(8,128)(2,1)S(1)} %get-tuple-element.92), channel_id=1, source_target_pairs={{0,96},{1,97},{2,98},{3,99},{4,100},{5,101},{6,102},{7,103},{8,104... | collective-permute-start | bytes 2359304 | tf_op jit(solution)/shard_map/ppermute | solution.py:43
  116.7 16.7 %collective-permute-start.28 = (bf16[2,192,512]{2,1,0:T(8,128)(2,1)S(1)}, bf16[2,192,512]{2,1,0:T(8,128)(2,1)S(1)}, u32[]{:S(2)}, u32[]{:S(2)}) collective-permute-start(bf16[2,192,512]{2,1,0:T(8,128)(2,1)S(1)} %get-tuple-element.103), channel_id=1, source_target_pairs={{0,32},{1,33},{2,34},{3,35},{4,36},{5,37},{6,38},{7,39},{8,40},{9,... | collective-permute-start | bytes 1179656 | tf_op jit(solution)/shard_map/ppermute | solution.py:43
  116.8 16.7 %collective-permute-start.29 = (bf16[2,192,512]{2,1,0:T(8,128)(2,1)S(1)}, bf16[2,192,512]{2,1,0:T(8,128)(2,1)S(1)}, u32[]{:S(2)}, u32[]{:S(2)}) collective-permute-start(bf16[2,192,512]{2,1,0:T(8,128)(2,1)S(1)} %get-tuple-element.104), channel_id=1, source_target_pairs={{0,96},{1,97},{2,98},{3,99},{4,100},{5,101},{6,102},{7,103},{8,104... | collective-permute-start | bytes 1179656 | tf_op jit(solution)/shard_map/ppermute | solution.py:43
  120.3 19.1 %collective-permute-start.18 = (bf16[2,48,3072]{2,1,0:T(8,128)(2,1)S(1)}, bf16[2,48,3072]{2,1,0:T(8,128)(2,1)S(1)}, u32[]{:S(2)}, u32[]{:S(2)}) collective-permute-start(bf16[2,48,3072]{2,1,0:T(8,128)(2,1)S(1)} %get-tuple-element.83), channel_id=1, source_target_pairs={{0,4},{1,5},{2,6},{3,7},{4,0},{5,1},{6,2},{7,3},{8,12},{9,13},{10,... | collective-permute-start | bytes 1769480 | tf_op jit(solution)/shard_map/ppermute | solution.py:43
  125.4 14.0 %copy-start = (s32[128,2]{0,1:T(2,128)S(1)}, s32[128,2]{0,1:T(2,128)}, u32[]{:S(2)}) copy-start(s32[128,2]{0,1:T(2,128)} %param.9) | copy-start | bytes 3076
  125.4 14.0 %copy-start.1 = (f32[128]{0:T(128)S(1)}, f32[128]{0:T(128)}, u32[]{:S(2)}) copy-start(f32[128]{0:T(128)} %param.10) | copy-start | bytes 1540
  125.4 15.7 %collective-permute-start.25 = (bf16[2,192,512]{2,1,0:T(8,128)(2,1)S(1)}, bf16[2,192,512]{2,1,0:T(8,128)(2,1)S(1)}, u32[]{:S(2)}, u32[]{:S(2)}) collective-permute-start(bf16[2,192,512]{2,1,0:T(8,128)(2,1)S(1)} %get-tuple-element.95), channel_id=1, source_target_pairs={{0,8},{1,9},{2,10},{3,11},{4,12},{5,13},{6,14},{7,15},{8,0},{9,1},... | collective-permute-start | bytes 1179656 | tf_op jit(solution)/shard_map/ppermute | solution.py:43
  133.8 4.9 %collective-permute-start.30 = (bf16[1,192,512]{2,1,0:T(8,128)(2,1)S(1)}, bf16[1,192,512]{2,1,0:T(8,128)(2,1)S(1)}, u32[]{:S(2)}, u32[]{:S(2)}) collective-permute-start(bf16[1,192,512]{2,1,0:T(8,128)(2,1)S(1)} %get-tuple-element.106), channel_id=1, source_target_pairs={{0,8},{1,9},{2,10},{3,11},{4,12},{5,13},{6,14},{7,15},{8,0},{9,1},... | collective-permute-start | bytes 589832 | tf_op jit(solution)/shard_map/ppermute | solution.py:43

commit v3 on v2

--- a/solution.py
+++ b/solution.py
@@ -300,10 +300,10 @@
     back_half(other, rows, w_down, act, slope, out)
 
 
-def back_other(a, b, last, w_down, hidden, act, slope):
+def back_other(a, b, last, w_down, hidden, act, slope, *earlier):
     arrays = [a, b, last, w_down, hidden, act, slope]
     shapes = [(ROWS, DW), (3, ROWS, HALF)]
-    return call(back_other_kernel, [], arrays, shapes, ROWS * DW * FF)
+    return call(back_other_kernel, [], arrays, shapes, ROWS * DW * FF, earlier)
 
 
 def back_own_kernel(rows, w_down, act, slope, out):
@@ -551,7 +551,7 @@
     far1 = pair(x_far1, d_far1)
     parts = [four, three, far1, four_other, three_other, to_core(far1)]
     hidden, act, slope = gate_last(x_far1, w_gate, w_up, first, four_other, three_other)
-    d_rows, d_sent = back_other(four, three, d_far1, w_down, hidden, act, slope)
+    d_rows, d_sent = back_other(four, three, d_far1, w_down, hidden, act, slope, far1)
     d_got = to_core(d_sent)
     d_mine = back_own(d_rows, w_down, act, slope)
 

time: 142 us -> 142 us (level)
  transfers between devices with their start and end apart: 31 -> 31, of which waited for: 15 -> 14; matrix products, arithmetic and copies ran while one was open for 0% -> 0% of each run, Pallas kernels for 25% -> 24%
where the time goes in v3:
time: 142 us
  starting transfers between devices  55.9 us (39%)
  waiting for transfers between devices  42.9 us (30%)
  Pallas kernels  42 us (30%)
    ppermute x31, starting transfers between devices, shift(): return lax.ppermute(value, ('dp', 'tensor'), pairs)  55.9 us
    ppermute x31, waiting for transfers between devices, shift(): return lax.ppermute(value, ('dp', 'tensor'), pairs)  42.9 us
    pallas_call x25, Pallas kernels, call(): pl.pallas_call(without(inputs, len(earlier), kernel), in_specs=[IN_SMEM]...  36.9 us
  transfers between devices with their start and end apart: 31, of which 14 were waited for; matrix products, arithmetic and copies ran while one was open for 0% of the time, Pallas kernels for 24%

profile of v3, /device:TPU:1, one launch (start us, length us, event | category | flops | bytes accessed | tf_op | source)
XLA Modules:
  0.0 141.8 jit_solution(9080725788395355253)
XLA Ops:
  0.6 1.7 %shard_map.110.refs_2_ = bf16[2,48,3072]{2,1,0:T(8,128)(2,1)S(1)} custom-call(s32[2,128]{1,0:T(2,128)} %bitcast.7, f32[1,128]{1,0:T(1,128)} %bitcast.9, bf16[128,3072]{1,0:T(8,128)(2,1)} %x.1, bf16[128,3072]{1,0:T(8,128)(2,1)} %d.1), custom_call_target="tpu_custom_call" | custom-call | flops 75497 | bytes 2200 | tf_op jit(solution)/shard_map/pallas_call | solution.py:112
  2.4 2.2 %collective-permute-start.1 = (bf16[2,48,3072]{2,1,0:T(8,128)(2,1)S(1)}, bf16[2,48,3072]{2,1,0:T(8,128)(2,1)S(1)}, u32[]{:S(2)}, u32[]{:S(2)}) collective-permute-start(bf16[2,48,3072]{2,1,0:T(8,128)(2,1)S(1)} %shard_map.110.refs_2_), channel_id=1, source_target_pairs={{0,1},{1,2},{2,3},{3,0},{4,5},{5,6},{6,7},{7,4},{8,9},{9,10},{10,1... | collective-permute-start | bytes 1769480 | tf_op jit(solution)/shard_map/ppermute | solution.py:43
  4.6 3.6 %collective-permute-start.2 = (bf16[2,48,3072]{2,1,0:T(8,128)(2,1)S(1)}, bf16[2,48,3072]{2,1,0:T(8,128)(2,1)S(1)}, u32[]{:S(2)}, u32[]{:S(2)}) collective-permute-start(bf16[2,48,3072]{2,1,0:T(8,128)(2,1)S(1)} %shard_map.110.refs_2_), channel_id=1, source_target_pairs={{0,4},{1,5},{2,6},{3,7},{4,0},{5,1},{6,2},{7,3},{8,12},{9,13},{10,... | collective-permute-start | bytes 1769480 | tf_op jit(solution)/shard_map/ppermute | solution.py:43
  8.2 1.5 %collective-permute-start = (bf16[2,48,3072]{2,1,0:T(8,128)(2,1)S(1)}, bf16[2,48,3072]{2,1,0:T(8,128)(2,1)S(1)}, u32[]{:S(2)}, u32[]{:S(2)}) collective-permute-start(bf16[2,48,3072]{2,1,0:T(8,128)(2,1)S(1)} %shard_map.110.refs_2_), channel_id=1, source_target_pairs={{0,3},{1,0},{2,1},{3,2},{4,7},{5,4},{6,5},{7,6},{8,11},{9,8},{10,9... | collective-permute-start | bytes 1769480 | tf_op jit(solution)/shard_map/ppermute | solution.py:43
  9.7 9.2 %collective-permute-done.1.refs_1_ = bf16[2,48,3072]{2,1,0:T(8,128)(2,1)S(1)} collective-permute-done((bf16[2,48,3072]{2,1,0:T(8,128)(2,1)S(1)}, bf16[2,48,3072]{2,1,0:T(8,128)(2,1)S(1)}, u32[]{:S(2)}, u32[]{:S(2)}) %collective-permute-start.1) | collective-permute-done | bytes 589856 | tf_op jit(solution)/shard_map/ppermute | solution.py:43
  18.9 3.5 %collective-permute-start.5 = (bf16[2,48,3072]{2,1,0:T(8,128)(2,1)S(1)}, bf16[2,48,3072]{2,1,0:T(8,128)(2,1)S(1)}, u32[]{:S(2)}, u32[]{:S(2)}) collective-permute-start(bf16[2,48,3072]{2,1,0:T(8,128)(2,1)S(1)} %collective-permute-done.1.refs_1_), channel_id=1, source_target_pairs={{0,4},{1,5},{2,6},{3,7},{4,0},{5,1},{6,2},{7,3},{8,12},{9,13},{10,... | collective-permute-start | bytes 1769480 | tf_op jit(solution)/shard_map/ppermute | solution.py:43
  22.4 2.7 %collective-permute-start.4 = (bf16[2,48,3072]{2,1,0:T(8,128)(2,1)S(1)}, bf16[2,48,3072]{2,1,0:T(8,128)(2,1)S(1)}, u32[]{:S(2)}, u32[]{:S(2)}) collective-permute-start(bf16[2,48,3072]{2,1,0:T(8,128)(2,1)S(1)} %collective-permute-done.2.refs_4_.refs_3_), channel_id=1, source_target_pairs={{0,3},{1,0},{2,1},{3,2},{4,7},{5,4},{6,5},{7,6},{8,11},{9,8},{10,9... | collective-permute-start | bytes 1769480 | tf_op jit(solution)/shard_map/ppermute | solution.py:43
  25.1 6.4 %shard_map.111 = (bf16[3072,1024]{1,0:T(8,128)(2,1)S(1)}, bf16[3072,1024]{1,0:T(8,128)(2,1)S(1)}, bf16[1024,3072]{1,0:T(8,128)(2,1)S(1)}, f32[8,128]{1,0:T(8,128)S(1)}) custom-call(bf16[3072,1024]{1,0:T(8,128)(2,1)} %refs_0_.1, bf16[3072,1024]{1,0:T(8,128)(2,1)} %refs_1_.1, bf16[1024,3072]{1,0:T(8,128)(2,1)} %refs_2_.1, ...), custom_call_target="tpu_custom_call" | custom-call | bytes 9438 | tf_op jit(solution)/shard_map/pallas_call | solution.py:157
  31.5 0.2 shard_map.112.refs_0_
  31.7 2.4 %collective-permute-start.8 = (bf16[2,192,3072]{2,1,0:T(8,128)(2,1)S(1)}, bf16[2,192,3072]{2,1,0:T(8,128)(2,1)S(1)}, u32[]{:S(2)}, u32[]{:S(2)}) collective-permute-start(bf16[2,192,3072]{2,1,0:T(8,128)(2,1)S(1)} %shard_map.112.refs_0_), channel_id=1, source_target_pairs={{0,8},{1,9},{2,10},{3,11},{4,12},{5,13},{6,14},{7,15},{8,0},{9,1},... | collective-permute-start | bytes 7077896 | tf_op jit(solution)/shard_map/ppermute | solution.py:43
  34.1 1.6 %collective-permute-done.4.refs_0_.refs_1_ = bf16[2,48,3072]{2,1,0:T(8,128)(2,1)S(1)} collective-permute-done((bf16[2,48,3072]{2,1,0:T(8,128)(2,1)S(1)}, bf16[2,48,3072]{2,1,0:T(8,128)(2,1)S(1)}, u32[]{:S(2)}, u32[]{:S(2)}) %collective-permute-start.4) | collective-permute-done | bytes 589856 | tf_op jit(solution)/shard_map/ppermute | solution.py:43
  35.7 1.0 collective-permute-done.3.refs_0_
  36.7 0.1 shard_map.114.refs_1_
  36.8 2.8 %collective-permute-start.9 = (bf16[2,144,3072]{2,1,0:T(8,128)(2,1)S(1)}, bf16[2,144,3072]{2,1,0:T(8,128)(2,1)S(1)}, u32[]{:S(2)}, u32[]{:S(2)}) collective-permute-start(bf16[2,144,3072]{2,1,0:T(8,128)(2,1)S(1)} %shard_map.114.refs_1_), channel_id=1, source_target_pairs={{0,8},{1,9},{2,10},{3,11},{4,12},{5,13},{6,14},{7,15},{8,0},{9,1},... | collective-permute-start | bytes 5308424 | tf_op jit(solution)/shard_map/ppermute | solution.py:43
  39.6 0.2 collective-permute-start.6
  39.7 2.7 %collective-permute-start.7 = (bf16[48,3072]{1,0:T(8,128)(2,1)S(1)}, bf16[48,3072]{1,0:T(8,128)(2,1)S(1)}, u32[]{:S(2)}, u32[]{:S(2)}) collective-permute-start(bf16[48,3072]{1,0:T(8,128)(2,1)S(1)} %shard_map.113.refs_3_.refs_1_), channel_id=1, source_target_pairs={{0,3},{1,0},{2,1},{3,2},{4,7},{5,4},{6,5},{7,6},{8,11},{9,8},{10,9... | collective-permute-start | bytes 884744 | tf_op jit(solution)/shard_map/ppermute | solution.py:43
  42.5 4.6 %shard_map.116 = (bf16[384,1024]{1,0:T(8,128)(2,1)S(1)}, f32[384,1024]{1,0:T(8,128)S(1)}, f32[384,1024]{1,0:T(8,128)S(1)}) custom-call(bf16[2,192,3072]{2,1,0:T(8,128)(2,1)S(1)} %shard_map.112.refs_0_, bf16[2,144,3072]{2,1,0:T(8,128)(2,1)S(1)} %shard_map.114.refs_1_, bf16[3072,1024]{1,0:T(8,128)(2,1)S(1)} %get-tuple-element.58.refs_2_.refs_1_, ...), custom_call_target="tpu_custom_call" | custom-call | flops 4227858 | bytes 9535 | tf_op jit(solution)/shard_map/pallas_call | solution.py:157
  47.0 2.6 %collective-permute-done.6.refs_1_.refs_2_ = bf16[48,3072]{1,0:T(8,128)(2,1)S(1)} collective-permute-done((bf16[48,3072]{1,0:T(8,128)(2,1)S(1)}, bf16[48,3072]{1,0:T(8,128)(2,1)S(1)}, u32[]{:S(2)}, u32[]{:S(2)}) %collective-permute-start.6) | collective-permute-done | bytes 294944 | tf_op jit(solution)/shard_map/ppermute | solution.py:43
  49.7 2.3 %shard_map.117 = (bf16[384,1024]{1,0:T(8,128)(2,1)S(1)}, f32[384,1024]{1,0:T(8,128)S(1)}, f32[384,1024]{1,0:T(8,128)S(1)}) custom-call(bf16[48,3072]{1,0:T(8,128)(2,1)S(1)} %collective-permute-done.7.refs_0_, bf16[3072,1024]{1,0:T(8,128)(2,1)S(1)} %get-tuple-element.58.refs_2_.refs_1_, ...), custom_call_target="tpu_custom_call", output_to_operand_aliasing={{0}: (3, {}), {1}: (4, {}), {2}: (5, {})} | custom-call | flops 603979 | bytes 8798 | tf_op jit(solution)/shard_map/pallas_call | solution.py:157
  52.0 1.4 %shard_map.119 = (bf16[384,3072]{1,0:T(8,128)(2,1)S(1)}, bf16[3,384,512]{2,1,0:T(8,128)(2,1)S(1)}) custom-call(bf16[2,192,3072]{2,1,0:T(8,128)(2,1)S(1)} %shard_map.112.refs_0_, bf16[2,144,3072]{2,1,0:T(8,128)(2,1)S(1)} %shard_map.114.refs_1_, bf16[48,3072]{1,0:T(8,128)(2,1)S(1)} %collective-permute-done.6.refs_1_.refs_2_, ...), custom_call_target="tpu_custom_call" | custom-call | flops 1207959 | bytes 8306 | tf_op jit(solution)/shard_map/pallas_call | solution.py:157
  53.4 0.8 collective-permute-start.11
  54.3 0.3 collective-permute-start.10
  54.5 1.4 shard_map.120.refs_6_.refs_0_
  56.0 1.6 %collective-permute-done.10.refs_5_ = bf16[2,48,3072]{2,1,0:T(8,128)(2,1)S(1)} collective-permute-done((bf16[2,48,3072]{2,1,0:T(8,128)(2,1)S(1)}, bf16[2,48,3072]{2,1,0:T(8,128)(2,1)S(1)}, u32[]{:S(2)}, u32[]{:S(2)}) %collective-permute-start.10) | collective-permute-done | bytes 589856 | tf_op jit(solution)/shard_map/ppermute | solution.py:43
  57.6 1.8 %shard_map.121 = (bf16[2,384,512]{2,1,0:T(8,128)(2,1)S(1)}, bf16[2,384,512]{2,1,0:T(8,128)(2,1)S(1)}) custom-call(bf16[2,192,3072]{2,1,0:T(8,128)(2,1)S(1)} %shard_map.112.refs_0_, bf16[2,144,3072]{2,1,0:T(8,128)(2,1)S(1)} %shard_map.114.refs_1_, bf16[2,48,3072]{2,1,0:T(8,128)(2,1)S(1)} %shard_map.118.refs_7_.refs_2_, ...), custom_call_target="tpu_custom_call" | custom-call | flops 1207959 | bytes 6488 | tf_op jit(solution)/shard_map/pallas_call | solution.py:157
  59.4 2.5 %collective-permute-start.15 = (bf16[2,384,512]{2,1,0:T(8,128)(2,1)S(1)}, bf16[2,384,512]{2,1,0:T(8,128)(2,1)S(1)}, u32[]{:S(2)}, u32[]{:S(2)}) collective-permute-start(bf16[2,384,512]{2,1,0:T(8,128)(2,1)S(1)} %get-tuple-element.76), channel_id=1, source_target_pairs={{0,96},{1,97},{2,98},{3,99},{4,100},{5,101},{6,102},{7,103},{8,104... | collective-permute-start | bytes 2359304 | tf_op jit(solution)/shard_map/ppermute | solution.py:43
  61.9 3.6 %shard_map.122 = (bf16[4,384,512]{2,1,0:T(8,128)(2,1)S(1)}, bf16[4,384,512]{2,1,0:T(8,128)(2,1)S(1)}) custom-call(bf16[2,192,3072]{2,1,0:T(8,128)(2,1)S(1)} %shard_map.112.refs_0_, bf16[2,144,3072]{2,1,0:T(8,128)(2,1)S(1)} %shard_map.114.refs_1_, bf16[2,48,3072]{2,1,0:T(8,128)(2,1)S(1)} %shard_map.118.refs_7_.refs_2_, ...), custom_call_target="tpu_custom_call" | custom-call | flops 2415919 | bytes 7274 | tf_op jit(solution)/shard_map/pallas_call | solution.py:157
  65.5 0.8 collective-permute-start.21
  66.3 2.6 %shard_map.123.refs_4_ = bf16[384,3072]{1,0:T(8,128)(2,1)S(1)} custom-call(bf16[384,1024]{1,0:T(8,128)(2,1)S(1)} %get-tuple-element.63.refs_4_.refs_6_.refs_0_, bf16[1024,3072]{1,0:T(8,128)(2,1)S(1)} %get-tuple-element.57.refs_3_.refs_1_, bf16[4,384,512]{2,1,0:T(8,128)(2,1)S(1)} %get-tuple-element.69.refs_2_.refs_0_), custom_call_target="tpu_custom_call" | custom-call | flops 2415919 | bytes 4718 | tf_op jit(solution)/shard_map/pallas_call | solution.py:157
  68.9 5.1 %shard_map.124 = (bf16[2,48,3072]{2,1,0:T(8,128)(2,1)S(1)}, bf16[2,48,3072]{2,1,0:T(8,128)(2,1)S(1)}, bf16[2,2,48,3072]{3,2,1,0:T(8,128)(2,1)S(1)}, bf16[2,2,48,...) custom-call(bf16[2,384,512]{2,1,0:T(8,128)(2,1)S(1)} %shard_map.120.refs_6_.refs_0_, ...), custom_call_target="tpu_custom_call" | custom-call | flops 4831838 | bytes 10813 | tf_op jit(solution)/shard_map/pallas_call | solution.py:157
  74.1 0.9 collective-permute-start.12
  75.0 2.0 %collective-permute-start.13 = (bf16[2,48,3072]{2,1,0:T(8,128)(2,1)S(1)}, bf16[2,48,3072]{2,1,0:T(8,128)(2,1)S(1)}, u32[]{:S(2)}, u32[]{:S(2)}) collective-permute-start(bf16[2,48,3072]{2,1,0:T(8,128)(2,1)S(1)} %get-tuple-element.74), channel_id=1, source_target_pairs={{0,3},{1,0},{2,1},{3,2},{4,7},{5,4},{6,5},{7,6},{8,11},{9,8},{10,9... | collective-permute-start | bytes 1769480 | tf_op jit(solution)/shard_map/ppermute | solution.py:43
  77.0 1.4 %shard_map.125 = (bf16[2,384,512]{2,1,0:T(8,128)(2,1)S(1)}, bf16[2,384,512]{2,1,0:T(8,128)(2,1)S(1)}) custom-call(bf16[2,192,3072]{2,1,0:T(8,128)(2,1)S(1)} %shard_map.112.refs_0_, bf16[2,144,3072]{2,1,0:T(8,128)(2,1)S(1)} %shard_map.114.refs_1_, bf16[2,48,3072]{2,1,0:T(8,128)(2,1)S(1)} %shard_map.118.refs_7_.refs_2_, ...), custom_call_target="tpu_custom_call" | custom-call | flops 1207959 | bytes 6488 | tf_op jit(solution)/shard_map/pallas_call | solution.py:157
  78.5 3.1 %collective-permute-done.14.refs_1_ = bf16[2,384,512]{2,1,0:T(8,128)(2,1)S(1)} collective-permute-done((bf16[2,384,512]{2,1,0:T(8,128)(2,1)S(1)}, bf16[2,384,512]{2,1,0:T(8,128)(2,1)S(1)}, u32[]{:S(2)}, u32[]{:S(2)}) %collective-permute-start.14) | collective-permute-done | bytes 786464 | tf_op jit(solution)/shard_map/ppermute | solution.py:43
  81.5 0.2 shard_map.126.refs_8_
  81.8 2.7 %collective-permute-start.20 = (bf16[2,384,512]{2,1,0:T(8,128)(2,1)S(1)}, bf16[2,384,512]{2,1,0:T(8,128)(2,1)S(1)}, u32[]{:S(2)}, u32[]{:S(2)}) collective-permute-start(bf16[2,384,512]{2,1,0:T(8,128)(2,1)S(1)} %shard_map.126.refs_8_), channel_id=1, source_target_pairs={{0,96},{1,97},{2,98},{3,99},{4,100},{5,101},{6,102},{7,103},{8,104... | collective-permute-start | bytes 2359304 | tf_op jit(solution)/shard_map/ppermute | solution.py:43
  84.5 3.0 %shard_map.127 = (bf16[2,384,512]{2,1,0:T(8,128)(2,1)S(1)}, bf16[2,384,512]{2,1,0:T(8,128)(2,1)S(1)}, bf16[2,384,512]{2,1,0:T(8,128)(2,1)S(1)}, bf16[2,384,512]{2,1,0:T(8,128)(2,1)S(1)}) custom-call(bf16[2,192,3072]{2,1,0:T(8,128)(2,1)S(1)} %shard_map.112.refs_0_, bf16[2,144,3072]{2,1,0:T(8,128)(2,1)S(1)} %shard_map.114.refs_1_, ...), custom_call_target="tpu_custom_call" | custom-call | flops 2415919 | bytes 7274 | tf_op jit(solution)/shard_map/pallas_call | solution.py:157
  87.5 0.2 shard_map.128.refs_4_
  87.6 1.8 %collective-permute-done.12.refs_1_ = bf16[2,48,3072]{2,1,0:T(8,128)(2,1)S(1)} collective-permute-done((bf16[2,48,3072]{2,1,0:T(8,128)(2,1)S(1)}, bf16[2,48,3072]{2,1,0:T(8,128)(2,1)S(1)}, u32[]{:S(2)}, u32[]{:S(2)}) %collective-permute-start.12) | collective-permute-done | bytes 589856 | tf_op jit(solution)/shard_map/ppermute | solution.py:43
  89.4 0.3 shard_map.129
  89.7 0.7 collective-permute-start.16
  90.5 2.2 %collective-permute-start.17 = (bf16[2,2,48,3072]{3,2,1,0:T(8,128)(2,1)S(1)}, bf16[2,2,48,3072]{3,2,1,0:T(8,128)(2,1)S(1)}, u32[]{:S(2)}, u32[]{:S(2)}) collective-permute-start(bf16[2,2,48,3072]{3,2,1,0:T(8,128)(2,1)S(1)} %get-tuple-element.81), channel_id=1, source_target_pairs={{0,3},{1,0},{2,1},{3,2},{4,7},{5,4},{6,5},{7,6},{8,11},{9,8},{10,9... | collective-permute-start | bytes 3538952 | tf_op jit(solution)/shard_map/ppermute | solution.py:43
  92.6 7.9 %collective-permute-done.19.refs_1_ = bf16[2,384,512]{2,1,0:T(8,128)(2,1)S(1)} collective-permute-done((bf16[2,384,512]{2,1,0:T(8,128)(2,1)S(1)}, bf16[2,384,512]{2,1,0:T(8,128)(2,1)S(1)}, u32[]{:S(2)}, u32[]{:S(2)}) %collective-permute-start.19) | collective-permute-done | bytes 786464 | tf_op jit(solution)/shard_map/ppermute | solution.py:43
  100.5 0.3 shard_map.132.refs_2_
  100.9 0.4 shard_map.135
  101.3 2.7 %collective-permute-start.27 = (bf16[192,512]{1,0:T(8,128)(2,1)S(1)}, bf16[192,512]{1,0:T(8,128)(2,1)S(1)}, u32[]{:S(2)}, u32[]{:S(2)}) collective-permute-start(bf16[192,512]{1,0:T(8,128)(2,1)S(1)} %get-tuple-element.102), channel_id=1, source_target_pairs={{0,96},{1,97},{2,98},{3,99},{4,100},{5,101},{6,102},{7,103},{8,104... | collective-permute-start | bytes 589832 | tf_op jit(solution)/shard_map/ppermute | solution.py:43
  104.0 0.7 collective-permute-start.24
  104.7 2.6 %collective-permute-done.26.refs_1_ = bf16[192,512]{1,0:T(8,128)(2,1)S(1)} collective-permute-done((bf16[192,512]{1,0:T(8,128)(2,1)S(1)}, bf16[192,512]{1,0:T(8,128)(2,1)S(1)}, u32[]{:S(2)}, u32[]{:S(2)}) %collective-permute-start.26) | collective-permute-done | bytes 196640 | tf_op jit(solution)/shard_map/ppermute | solution.py:43
  107.3 2.7 %collective-permute-start.23 = (bf16[2,384,512]{2,1,0:T(8,128)(2,1)S(1)}, bf16[2,384,512]{2,1,0:T(8,128)(2,1)S(1)}, u32[]{:S(2)}, u32[]{:S(2)}) collective-permute-start(bf16[2,384,512]{2,1,0:T(8,128)(2,1)S(1)} %get-tuple-element.92), channel_id=1, source_target_pairs={{0,96},{1,97},{2,98},{3,99},{4,100},{5,101},{6,102},{7,103},{8,104... | collective-permute-start | bytes 2359304 | tf_op jit(solution)/shard_map/ppermute | solution.py:43
  110.0 0.1 shard_map.136
  110.1 6.6 %collective-permute-done.16.refs_1_ = bf16[2,2,48,3072]{3,2,1,0:T(8,128)(2,1)S(1)} collective-permute-done((bf16[2,2,48,3072]{3,2,1,0:T(8,128)(2,1)S(1)}, bf16[2,2,48,3072]{3,2,1,0:T(8,128)(2,1)S(1)}, u32[]{:S(2)}, u32[]{:S(2)}) %collective-permute-start.16) | collective-permute-done | bytes 1179680 | tf_op jit(solution)/shard_map/ppermute | solution.py:43
  116.7 2.7 %collective-permute-start.29 = (bf16[2,192,512]{2,1,0:T(8,128)(2,1)S(1)}, bf16[2,192,512]{2,1,0:T(8,128)(2,1)S(1)}, u32[]{:S(2)}, u32[]{:S(2)}) collective-permute-start(bf16[2,192,512]{2,1,0:T(8,128)(2,1)S(1)} %get-tuple-element.104), channel_id=1, source_target_pairs={{0,96},{1,97},{2,98},{3,99},{4,100},{5,101},{6,102},{7,103},{8,104... | collective-permute-start | bytes 1179656 | tf_op jit(solution)/shard_map/ppermute | solution.py:43
  119.4 0.4 shard_map.130
  119.8 0.2 collective-permute-done.24.refs_3_
  120.0 0.7 collective-permute-start.18
  120.8 3.6 %collective-permute-done.22.refs_1_ = bf16[2,384,512]{2,1,0:T(8,128)(2,1)S(1)} collective-permute-done((bf16[2,384,512]{2,1,0:T(8,128)(2,1)S(1)}, bf16[2,384,512]{2,1,0:T(8,128)(2,1)S(1)}, u32[]{:S(2)}, u32[]{:S(2)}) %collective-permute-start.22) | collective-permute-done | bytes 786464 | tf_op jit(solution)/shard_map/ppermute | solution.py:43
  124.3 0.8 shard_map.133
  125.1 8.0 %collective-permute-start.25 = (bf16[2,192,512]{2,1,0:T(8,128)(2,1)S(1)}, bf16[2,192,512]{2,1,0:T(8,128)(2,1)S(1)}, u32[]{:S(2)}, u32[]{:S(2)}) collective-permute-start(bf16[2,192,512]{2,1,0:T(8,128)(2,1)S(1)} %get-tuple-element.95), channel_id=1, source_target_pairs={{0,8},{1,9},{2,10},{3,11},{4,12},{5,13},{6,14},{7,15},{8,0},{9,1},... | collective-permute-start | bytes 1179656 | tf_op jit(solution)/shard_map/ppermute | solution.py:43
  133.2 0.3 shard_map.137
  133.4 3.8 %collective-permute-start.30 = (bf16[1,192,512]{2,1,0:T(8,128)(2,1)S(1)}, bf16[1,192,512]{2,1,0:T(8,128)(2,1)S(1)}, u32[]{:S(2)}, u32[]{:S(2)}) collective-permute-start(bf16[1,192,512]{2,1,0:T(8,128)(2,1)S(1)} %get-tuple-element.106), channel_id=1, source_target_pairs={{0,8},{1,9},{2,10},{3,11},{4,12},{5,13},{6,14},{7,15},{8,0},{9,1},... | collective-permute-start | bytes 589832 | tf_op jit(solution)/shard_map/ppermute | solution.py:43
  137.3 1.1 collective-permute-done.30.got
  138.3 0.8 shard_map.138
  139.1 1.7 %shard_map.131 = (bf16[128,3072]{1,0:T(8,128)(2,1)}, bf16[128,3072]{1,0:T(8,128)(2,1)}) custom-call(s32[2,128]{1,0:T(2,128)S(1)} %bitcast.8, f32[1,128]{1,0:T(1,128)S(1)} %bitcast.10, bf16[2,48,3072]{2,1,0:T(8,128)(2,1)S(1)} %get-tuple-element.82.kept, bf16[2,48,3072]{2,1,0:T(8,128)(2,1)S(1)} %collective-permute-done.18.got), custom_call_target="tpu_custom_call" | custom-call | flops 75497 | bytes 2800 | tf_op jit(solution)/shard_map/pallas_call | solution.py:133
  140.9 0.9 shard_map.134
  (31 shorter events, 0.4 us)
Async XLA Ops:
  2.4 16.5 %collective-permute-start.1 = (bf16[2,48,3072]{2,1,0:T(8,128)(2,1)S(1)}, bf16[2,48,3072]{2,1,0:T(8,128)(2,1)S(1)}, u32[]{:S(2)}, u32[]{:S(2)}) collective-permute-start(bf16[2,48,3072]{2,1,0:T(8,128)(2,1)S(1)} %shard_map.110.refs_2_), channel_id=1, source_target_pairs={{0,1},{1,2},{2,3},{3,0},{4,5},{5,6},{6,7},{7,4},{8,9},{9,10},{10,1... | collective-permute-start | bytes 1769480 | tf_op jit(solution)/shard_map/ppermute | solution.py:43
  4.6 17.9 %collective-permute-start.2 = (bf16[2,48,3072]{2,1,0:T(8,128)(2,1)S(1)}, bf16[2,48,3072]{2,1,0:T(8,128)(2,1)S(1)}, u32[]{:S(2)}, u32[]{:S(2)}) collective-permute-start(bf16[2,48,3072]{2,1,0:T(8,128)(2,1)S(1)} %shard_map.110.refs_2_), channel_id=1, source_target_pairs={{0,4},{1,5},{2,6},{3,7},{4,0},{5,1},{6,2},{7,3},{8,12},{9,13},{10,... | collective-permute-start | bytes 1769480 | tf_op jit(solution)/shard_map/ppermute | solution.py:43
  8.2 16.9 %collective-permute-start = (bf16[2,48,3072]{2,1,0:T(8,128)(2,1)S(1)}, bf16[2,48,3072]{2,1,0:T(8,128)(2,1)S(1)}, u32[]{:S(2)}, u32[]{:S(2)}) collective-permute-start(bf16[2,48,3072]{2,1,0:T(8,128)(2,1)S(1)} %shard_map.110.refs_2_), channel_id=1, source_target_pairs={{0,3},{1,0},{2,1},{3,2},{4,7},{5,4},{6,5},{7,6},{8,11},{9,8},{10,9... | collective-permute-start | bytes 1769480 | tf_op jit(solution)/shard_map/ppermute | solution.py:43
  18.9 16.8 %collective-permute-start.5 = (bf16[2,48,3072]{2,1,0:T(8,128)(2,1)S(1)}, bf16[2,48,3072]{2,1,0:T(8,128)(2,1)S(1)}, u32[]{:S(2)}, u32[]{:S(2)}) collective-permute-start(bf16[2,48,3072]{2,1,0:T(8,128)(2,1)S(1)} %collective-permute-done.1.refs_1_), channel_id=1, source_target_pairs={{0,4},{1,5},{2,6},{3,7},{4,0},{5,1},{6,2},{7,3},{8,12},{9,13},{10,... | collective-permute-start | bytes 1769480 | tf_op jit(solution)/shard_map/ppermute | solution.py:43
  22.4 14.3 %collective-permute-start.3 = (bf16[2,48,3072]{2,1,0:T(8,128)(2,1)S(1)}, bf16[2,48,3072]{2,1,0:T(8,128)(2,1)S(1)}, u32[]{:S(2)}, u32[]{:S(2)}) collective-permute-start(bf16[2,48,3072]{2,1,0:T(8,128)(2,1)S(1)} %collective-permute-done.1.refs_1_), channel_id=1, source_target_pairs={{0,1},{1,2},{2,3},{3,0},{4,5},{5,6},{6,7},{7,4},{8,9},{9,10},{10,1... | collective-permute-start | bytes 1769480 | tf_op jit(solution)/shard_map/ppermute | solution.py:43
  22.4 13.3 %collective-permute-start.4 = (bf16[2,48,3072]{2,1,0:T(8,128)(2,1)S(1)}, bf16[2,48,3072]{2,1,0:T(8,128)(2,1)S(1)}, u32[]{:S(2)}, u32[]{:S(2)}) collective-permute-start(bf16[2,48,3072]{2,1,0:T(8,128)(2,1)S(1)} %collective-permute-done.2.refs_4_.refs_3_), channel_id=1, source_target_pairs={{0,3},{1,0},{2,1},{3,2},{4,7},{5,4},{6,5},{7,6},{8,11},{9,8},{10,9... | collective-permute-start | bytes 1769480 | tf_op jit(solution)/shard_map/ppermute | solution.py:43
  31.7 18.0 %collective-permute-start.8 = (bf16[2,192,3072]{2,1,0:T(8,128)(2,1)S(1)}, bf16[2,192,3072]{2,1,0:T(8,128)(2,1)S(1)}, u32[]{:S(2)}, u32[]{:S(2)}) collective-permute-start(bf16[2,192,3072]{2,1,0:T(8,128)(2,1)S(1)} %shard_map.112.refs_0_), channel_id=1, source_target_pairs={{0,8},{1,9},{2,10},{3,11},{4,12},{5,13},{6,14},{7,15},{8,0},{9,1},... | collective-permute-start | bytes 7077896 | tf_op jit(solution)/shard_map/ppermute | solution.py:43
  36.8 12.9 %collective-permute-start.9 = (bf16[2,144,3072]{2,1,0:T(8,128)(2,1)S(1)}, bf16[2,144,3072]{2,1,0:T(8,128)(2,1)S(1)}, u32[]{:S(2)}, u32[]{:S(2)}) collective-permute-start(bf16[2,144,3072]{2,1,0:T(8,128)(2,1)S(1)} %shard_map.114.refs_1_), channel_id=1, source_target_pairs={{0,8},{1,9},{2,10},{3,11},{4,12},{5,13},{6,14},{7,15},{8,0},{9,1},... | collective-permute-start | bytes 5308424 | tf_op jit(solution)/shard_map/ppermute | solution.py:43
  39.6 10.0 %collective-permute-start.6 = (bf16[48,3072]{1,0:T(8,128)(2,1)S(1)}, bf16[48,3072]{1,0:T(8,128)(2,1)S(1)}, u32[]{:S(2)}, u32[]{:S(2)}) collective-permute-start(bf16[48,3072]{1,0:T(8,128)(2,1)S(1)} %shard_map.115.refs_4_), channel_id=1, source_target_pairs={{0,1},{1,2},{2,3},{3,0},{4,5},{5,6},{6,7},{7,4},{8,9},{9,10},{10,1... | collective-permute-start | bytes 884744 | tf_op jit(solution)/shard_map/ppermute | solution.py:43
  39.7 9.9 %collective-permute-start.7 = (bf16[48,3072]{1,0:T(8,128)(2,1)S(1)}, bf16[48,3072]{1,0:T(8,128)(2,1)S(1)}, u32[]{:S(2)}, u32[]{:S(2)}) collective-permute-start(bf16[48,3072]{1,0:T(8,128)(2,1)S(1)} %shard_map.113.refs_3_.refs_1_), channel_id=1, source_target_pairs={{0,3},{1,0},{2,1},{3,2},{4,7},{5,4},{6,5},{7,6},{8,11},{9,8},{10,9... | collective-permute-start | bytes 884744 | tf_op jit(solution)/shard_map/ppermute | solution.py:43
  53.4 4.2 %collective-permute-start.11 = (bf16[3,384,512]{2,1,0:T(8,128)(2,1)S(1)}, bf16[3,384,512]{2,1,0:T(8,128)(2,1)S(1)}, u32[]{:S(2)}, u32[]{:S(2)}) collective-permute-start(bf16[3,384,512]{2,1,0:T(8,128)(2,1)S(1)} %get-tuple-element.67.refs_1_), channel_id=1, source_target_pairs={{0,8},{1,9},{2,10},{3,11},{4,12},{5,13},{6,14},{7,15},{8,0},{9,1},... | collective-permute-start | bytes 3538952 | tf_op jit(solution)/shard_map/ppermute | solution.py:43
  54.3 3.3 %collective-permute-start.10 = (bf16[2,48,3072]{2,1,0:T(8,128)(2,1)S(1)}, bf16[2,48,3072]{2,1,0:T(8,128)(2,1)S(1)}, u32[]{:S(2)}, u32[]{:S(2)}) collective-permute-start(bf16[2,48,3072]{2,1,0:T(8,128)(2,1)S(1)} %shard_map.118.refs_7_.refs_2_), channel_id=1, source_target_pairs={{0,8},{1,9},{2,10},{3,11},{4,12},{5,13},{6,14},{7,15},{8,0},{9,1},... | collective-permute-start | bytes 1769480 | tf_op jit(solution)/shard_map/ppermute | solution.py:43
  59.4 19.1 %collective-permute-start.15 = (bf16[2,384,512]{2,1,0:T(8,128)(2,1)S(1)}, bf16[2,384,512]{2,1,0:T(8,128)(2,1)S(1)}, u32[]{:S(2)}, u32[]{:S(2)}) collective-permute-start(bf16[2,384,512]{2,1,0:T(8,128)(2,1)S(1)} %get-tuple-element.76), channel_id=1, source_target_pairs={{0,96},{1,97},{2,98},{3,99},{4,100},{5,101},{6,102},{7,103},{8,104... | collective-permute-start | bytes 2359304 | tf_op jit(solution)/shard_map/ppermute | solution.py:43
  61.9 19.6 %collective-permute-start.14 = (bf16[2,384,512]{2,1,0:T(8,128)(2,1)S(1)}, bf16[2,384,512]{2,1,0:T(8,128)(2,1)S(1)}, u32[]{:S(2)}, u32[]{:S(2)}) collective-permute-start(bf16[2,384,512]{2,1,0:T(8,128)(2,1)S(1)} %get-tuple-element.68.refs_8_), channel_id=1, source_target_pairs={{0,32},{1,33},{2,34},{3,35},{4,36},{5,37},{6,38},{7,39},{8,40},{9,... | collective-permute-start | bytes 2359304 | tf_op jit(solution)/shard_map/ppermute | solution.py:43
  65.5 35.4 %collective-permute-start.21 = (bf16[4,384,512]{2,1,0:T(8,128)(2,1)S(1)}, bf16[4,384,512]{2,1,0:T(8,128)(2,1)S(1)}, u32[]{:S(2)}, u32[]{:S(2)}) collective-permute-start(bf16[4,384,512]{2,1,0:T(8,128)(2,1)S(1)} %get-tuple-element.90), channel_id=1, source_target_pairs={{0,16},{1,17},{2,18},{3,19},{4,20},{5,21},{6,22},{7,23},{8,24},{9,... | collective-permute-start | bytes 4718600 | tf_op jit(solution)/shard_map/ppermute | solution.py:43
  74.1 15.4 %collective-permute-start.12 = (bf16[2,48,3072]{2,1,0:T(8,128)(2,1)S(1)}, bf16[2,48,3072]{2,1,0:T(8,128)(2,1)S(1)}, u32[]{:S(2)}, u32[]{:S(2)}) collective-permute-start(bf16[2,48,3072]{2,1,0:T(8,128)(2,1)S(1)} %get-tuple-element.72), channel_id=1, source_target_pairs={{0,1},{1,2},{2,3},{3,0},{4,5},{5,6},{6,7},{7,4},{8,9},{9,10},{10,1... | collective-permute-start | bytes 1769480 | tf_op jit(solution)/shard_map/ppermute | solution.py:43
  75.0 14.4 %collective-permute-start.13 = (bf16[2,48,3072]{2,1,0:T(8,128)(2,1)S(1)}, bf16[2,48,3072]{2,1,0:T(8,128)(2,1)S(1)}, u32[]{:S(2)}, u32[]{:S(2)}) collective-permute-start(bf16[2,48,3072]{2,1,0:T(8,128)(2,1)S(1)} %get-tuple-element.74), channel_id=1, source_target_pairs={{0,3},{1,0},{2,1},{3,2},{4,7},{5,4},{6,5},{7,6},{8,11},{9,8},{10,9... | collective-permute-start | bytes 1769480 | tf_op jit(solution)/shard_map/ppermute | solution.py:43
  81.7 18.8 %collective-permute-start.19 = (bf16[2,384,512]{2,1,0:T(8,128)(2,1)S(1)}, bf16[2,384,512]{2,1,0:T(8,128)(2,1)S(1)}, u32[]{:S(2)}, u32[]{:S(2)}) collective-permute-start(bf16[2,384,512]{2,1,0:T(8,128)(2,1)S(1)} %get-tuple-element.89), channel_id=1, source_target_pairs={{0,32},{1,33},{2,34},{3,35},{4,36},{5,37},{6,38},{7,39},{8,40},{9,... | collective-permute-start | bytes 2359304 | tf_op jit(solution)/shard_map/ppermute | solution.py:43
  81.8 18.7 %collective-permute-start.20 = (bf16[2,384,512]{2,1,0:T(8,128)(2,1)S(1)}, bf16[2,384,512]{2,1,0:T(8,128)(2,1)S(1)}, u32[]{:S(2)}, u32[]{:S(2)}) collective-permute-start(bf16[2,384,512]{2,1,0:T(8,128)(2,1)S(1)} %shard_map.126.refs_8_), channel_id=1, source_target_pairs={{0,96},{1,97},{2,98},{3,99},{4,100},{5,101},{6,102},{7,103},{8,104... | collective-permute-start | bytes 2359304 | tf_op jit(solution)/shard_map/ppermute | solution.py:43
  89.7 27.0 %collective-permute-start.16 = (bf16[2,2,48,3072]{3,2,1,0:T(8,128)(2,1)S(1)}, bf16[2,2,48,3072]{3,2,1,0:T(8,128)(2,1)S(1)}, u32[]{:S(2)}, u32[]{:S(2)}) collective-permute-start(bf16[2,2,48,3072]{3,2,1,0:T(8,128)(2,1)S(1)} %get-tuple-element.80), channel_id=1, source_target_pairs={{0,1},{1,2},{2,3},{3,0},{4,5},{5,6},{6,7},{7,4},{8,9},{9,10},{10,1... | collective-permute-start | bytes 3538952 | tf_op jit(solution)/shard_map/ppermute | solution.py:43
  90.5 26.3 %collective-permute-start.17 = (bf16[2,2,48,3072]{3,2,1,0:T(8,128)(2,1)S(1)}, bf16[2,2,48,3072]{3,2,1,0:T(8,128)(2,1)S(1)}, u32[]{:S(2)}, u32[]{:S(2)}) collective-permute-start(bf16[2,2,48,3072]{3,2,1,0:T(8,128)(2,1)S(1)} %get-tuple-element.81), channel_id=1, source_target_pairs={{0,3},{1,0},{2,1},{3,2},{4,7},{5,4},{6,5},{7,6},{8,11},{9,8},{10,9... | collective-permute-start | bytes 3538952 | tf_op jit(solution)/shard_map/ppermute | solution.py:43
  101.2 6.1 %collective-permute-start.26 = (bf16[192,512]{1,0:T(8,128)(2,1)S(1)}, bf16[192,512]{1,0:T(8,128)(2,1)S(1)}, u32[]{:S(2)}, u32[]{:S(2)}) collective-permute-start(bf16[192,512]{1,0:T(8,128)(2,1)S(1)} %get-tuple-element.100), channel_id=1, source_target_pairs={{0,32},{1,33},{2,34},{3,35},{4,36},{5,37},{6,38},{7,39},{8,40},{9,... | collective-permute-start | bytes 589832 | tf_op jit(solution)/shard_map/ppermute | solution.py:43
  101.3 6.0 %collective-permute-start.27 = (bf16[192,512]{1,0:T(8,128)(2,1)S(1)}, bf16[192,512]{1,0:T(8,128)(2,1)S(1)}, u32[]{:S(2)}, u32[]{:S(2)}) collective-permute-start(bf16[192,512]{1,0:T(8,128)(2,1)S(1)} %get-tuple-element.102), channel_id=1, source_target_pairs={{0,96},{1,97},{2,98},{3,99},{4,100},{5,101},{6,102},{7,103},{8,104... | collective-permute-start | bytes 589832 | tf_op jit(solution)/shard_map/ppermute | solution.py:43
  104.0 16.1 %collective-permute-start.24 = (bf16[2,384,512]{2,1,0:T(8,128)(2,1)S(1)}, bf16[2,384,512]{2,1,0:T(8,128)(2,1)S(1)}, u32[]{:S(2)}, u32[]{:S(2)}) collective-permute-start(bf16[2,384,512]{2,1,0:T(8,128)(2,1)S(1)} %shard_map.132.refs_2_), channel_id=1, source_target_pairs={{0,16},{1,17},{2,18},{3,19},{4,20},{5,21},{6,22},{7,23},{8,24},{9,... | collective-permute-start | bytes 2359304 | tf_op jit(solution)/shard_map/ppermute | solution.py:43
  107.3 17.0 %collective-permute-start.22 = (bf16[2,384,512]{2,1,0:T(8,128)(2,1)S(1)}, bf16[2,384,512]{2,1,0:T(8,128)(2,1)S(1)}, u32[]{:S(2)}, u32[]{:S(2)}) collective-permute-start(bf16[2,384,512]{2,1,0:T(8,128)(2,1)S(1)} %shard_map.128.refs_4_), channel_id=1, source_target_pairs={{0,32},{1,33},{2,34},{3,35},{4,36},{5,37},{6,38},{7,39},{8,40},{9,... | collective-permute-start | bytes 2359304 | tf_op jit(solution)/shard_map/ppermute | solution.py:43
  107.3 17.0 %collective-permute-start.23 = (bf16[2,384,512]{2,1,0:T(8,128)(2,1)S(1)}, bf16[2,384,512]{2,1,0:T(8,128)(2,1)S(1)}, u32[]{:S(2)}, u32[]{:S(2)}) collective-permute-start(bf16[2,384,512]{2,1,0:T(8,128)(2,1)S(1)} %get-tuple-element.92), channel_id=1, source_target_pairs={{0,96},{1,97},{2,98},{3,99},{4,100},{5,101},{6,102},{7,103},{8,104... | collective-permute-start | bytes 2359304 | tf_op jit(solution)/shard_map/ppermute | solution.py:43
  116.7 16.5 %collective-permute-start.28 = (bf16[2,192,512]{2,1,0:T(8,128)(2,1)S(1)}, bf16[2,192,512]{2,1,0:T(8,128)(2,1)S(1)}, u32[]{:S(2)}, u32[]{:S(2)}) collective-permute-start(bf16[2,192,512]{2,1,0:T(8,128)(2,1)S(1)} %get-tuple-element.103), channel_id=1, source_target_pairs={{0,32},{1,33},{2,34},{3,35},{4,36},{5,37},{6,38},{7,39},{8,40},{9,... | collective-permute-start | bytes 1179656 | tf_op jit(solution)/shard_map/ppermute | solution.py:43
  116.7 16.5 %collective-permute-start.29 = (bf16[2,192,512]{2,1,0:T(8,128)(2,1)S(1)}, bf16[2,192,512]{2,1,0:T(8,128)(2,1)S(1)}, u32[]{:S(2)}, u32[]{:S(2)}) collective-permute-start(bf16[2,192,512]{2,1,0:T(8,128)(2,1)S(1)} %get-tuple-element.104), channel_id=1, source_target_pairs={{0,96},{1,97},{2,98},{3,99},{4,100},{5,101},{6,102},{7,103},{8,104... | collective-permute-start | bytes 1179656 | tf_op jit(solution)/shard_map/ppermute | solution.py:43
  120.0 19.1 %collective-permute-start.18 = (bf16[2,48,3072]{2,1,0:T(8,128)(2,1)S(1)}, bf16[2,48,3072]{2,1,0:T(8,128)(2,1)S(1)}, u32[]{:S(2)}, u32[]{:S(2)}) collective-permute-start(bf16[2,48,3072]{2,1,0:T(8,128)(2,1)S(1)} %get-tuple-element.83), channel_id=1, source_target_pairs={{0,4},{1,5},{2,6},{3,7},{4,0},{5,1},{6,2},{7,3},{8,12},{9,13},{10,... | collective-permute-start | bytes 1769480 | tf_op jit(solution)/shard_map/ppermute | solution.py:43
  125.1 14.0 %copy-start = (s32[128,2]{0,1:T(2,128)S(1)}, s32[128,2]{0,1:T(2,128)}, u32[]{:S(2)}) copy-start(s32[128,2]{0,1:T(2,128)} %param.9) | copy-start | bytes 3076
  125.1 14.0 %copy-start.1 = (f32[128]{0:T(128)S(1)}, f32[128]{0:T(128)}, u32[]{:S(2)}) copy-start(f32[128]{0:T(128)} %param.10) | copy-start | bytes 1540
  125.1 15.7 %collective-permute-start.25 = (bf16[2,192,512]{2,1,0:T(8,128)(2,1)S(1)}, bf16[2,192,512]{2,1,0:T(8,128)(2,1)S(1)}, u32[]{:S(2)}, u32[]{:S(2)}) collective-permute-start(bf16[2,192,512]{2,1,0:T(8,128)(2,1)S(1)} %get-tuple-element.95), channel_id=1, source_target_pairs={{0,8},{1,9},{2,10},{3,11},{4,12},{5,13},{6,14},{7,15},{8,0},{9,1},... | collective-permute-start | bytes 1179656 | tf_op jit(solution)/shard_map/ppermute | solution.py:43
  133.4 4.9 %collective-permute-start.30 = (bf16[1,192,512]{2,1,0:T(8,128)(2,1)S(1)}, bf16[1,192,512]{2,1,0:T(8,128)(2,1)S(1)}, u32[]{:S(2)}, u32[]{:S(2)}) collective-permute-start(bf16[1,192,512]{2,1,0:T(8,128)(2,1)S(1)} %get-tuple-element.106), channel_id=1, source_target_pairs={{0,8},{1,9},{2,10},{3,11},{4,12},{5,13},{6,14},{7,15},{8,0},{9,1},... | collective-permute-start | bytes 589832 | tf_op jit(solution)/shard_map/ppermute | solution.py:43

commit v4 on v3

--- a/solution.py
+++ b/solution.py
@@ -543,8 +543,8 @@
     w_gate, w_up, w_down, there = stage([w_gate, w_up, w_down], up0, zhi)
     four = pack(up0, down0, sel, zhi, earlier=[there])
     x_far1 = split(0, up1, there)
-    three = pack(far0, up1, down1, earlier=[x_far1])
     d_far1 = split(1, down1, x_far1)
+    three = pack(far0, up1, down1, earlier=[d_far1])
     first = gate_first(four, three, w_gate, w_up, d_far1)
     x_far1, d_far1 = to_y(x_far1, -1), to_y(d_far1, 1)
     four_other, three_other = to_core(four), to_core(three)

time: 142 us -> 142 us (level)
  transfers between devices with their start and end apart: 31 -> 31, of which waited for: 14 -> 15; matrix products, arithmetic and copies ran while one was open for 0% -> 0% of each run, Pallas kernels for 24% -> 24%
where the time goes in v4:
time: 142 us
  starting transfers between devices  55.6 us (39%)
  waiting for transfers between devices  43.2 us (30%)
  Pallas kernels  42 us (30%)
    ppermute x31, starting transfers between devices, shift(): return lax.ppermute(value, ('dp', 'tensor'), pairs)  55.6 us
    ppermute x31, waiting for transfers between devices, shift(): return lax.ppermute(value, ('dp', 'tensor'), pairs)  43.2 us
    pallas_call x25, Pallas kernels, call(): pl.pallas_call(without(inputs, len(earlier), kernel), in_specs=[IN_SMEM]...  36.9 us
  transfers between devices with their start and end apart: 31, of which 15 were waited for; matrix products, arithmetic and copies ran while one was open for 0% of the time, Pallas kernels for 24%

profile of v4, /device:TPU:1, one launch (start us, length us, event | category | flops | bytes accessed | tf_op | source)
XLA Modules:
  0.0 141.7 jit_solution(4661879371578403329)
XLA Ops:
  0.6 1.7 %shard_map.110.refs_2_ = bf16[2,48,3072]{2,1,0:T(8,128)(2,1)S(1)} custom-call(s32[2,128]{1,0:T(2,128)} %bitcast.7, f32[1,128]{1,0:T(1,128)} %bitcast.9, bf16[128,3072]{1,0:T(8,128)(2,1)} %x.1, bf16[128,3072]{1,0:T(8,128)(2,1)} %d.1), custom_call_target="tpu_custom_call" | custom-call | flops 75497 | bytes 2200 | tf_op jit(solution)/shard_map/pallas_call | solution.py:112
  2.4 2.2 %collective-permute-start.1 = (bf16[2,48,3072]{2,1,0:T(8,128)(2,1)S(1)}, bf16[2,48,3072]{2,1,0:T(8,128)(2,1)S(1)}, u32[]{:S(2)}, u32[]{:S(2)}) collective-permute-start(bf16[2,48,3072]{2,1,0:T(8,128)(2,1)S(1)} %shard_map.110.refs_2_), channel_id=1, source_target_pairs={{0,1},{1,2},{2,3},{3,0},{4,5},{5,6},{6,7},{7,4},{8,9},{9,10},{10,1... | collective-permute-start | bytes 1769480 | tf_op jit(solution)/shard_map/ppermute | solution.py:43
  4.6 3.6 %collective-permute-start.2 = (bf16[2,48,3072]{2,1,0:T(8,128)(2,1)S(1)}, bf16[2,48,3072]{2,1,0:T(8,128)(2,1)S(1)}, u32[]{:S(2)}, u32[]{:S(2)}) collective-permute-start(bf16[2,48,3072]{2,1,0:T(8,128)(2,1)S(1)} %shard_map.110.refs_2_), channel_id=1, source_target_pairs={{0,4},{1,5},{2,6},{3,7},{4,0},{5,1},{6,2},{7,3},{8,12},{9,13},{10,... | collective-permute-start | bytes 1769480 | tf_op jit(solution)/shard_map/ppermute | solution.py:43
  8.2 1.5 %collective-permute-start = (bf16[2,48,3072]{2,1,0:T(8,128)(2,1)S(1)}, bf16[2,48,3072]{2,1,0:T(8,128)(2,1)S(1)}, u32[]{:S(2)}, u32[]{:S(2)}) collective-permute-start(bf16[2,48,3072]{2,1,0:T(8,128)(2,1)S(1)} %shard_map.110.refs_2_), channel_id=1, source_target_pairs={{0,3},{1,0},{2,1},{3,2},{4,7},{5,4},{6,5},{7,6},{8,11},{9,8},{10,9... | collective-permute-start | bytes 1769480 | tf_op jit(solution)/shard_map/ppermute | solution.py:43
  9.7 9.2 %collective-permute-done.1.refs_1_ = bf16[2,48,3072]{2,1,0:T(8,128)(2,1)S(1)} collective-permute-done((bf16[2,48,3072]{2,1,0:T(8,128)(2,1)S(1)}, bf16[2,48,3072]{2,1,0:T(8,128)(2,1)S(1)}, u32[]{:S(2)}, u32[]{:S(2)}) %collective-permute-start.1) | collective-permute-done | bytes 589856 | tf_op jit(solution)/shard_map/ppermute | solution.py:43
  18.9 3.5 %collective-permute-start.5 = (bf16[2,48,3072]{2,1,0:T(8,128)(2,1)S(1)}, bf16[2,48,3072]{2,1,0:T(8,128)(2,1)S(1)}, u32[]{:S(2)}, u32[]{:S(2)}) collective-permute-start(bf16[2,48,3072]{2,1,0:T(8,128)(2,1)S(1)} %collective-permute-done.1.refs_1_), channel_id=1, source_target_pairs={{0,4},{1,5},{2,6},{3,7},{4,0},{5,1},{6,2},{7,3},{8,12},{9,13},{10,... | collective-permute-start | bytes 1769480 | tf_op jit(solution)/shard_map/ppermute | solution.py:43
  22.4 2.7 %collective-permute-start.4 = (bf16[2,48,3072]{2,1,0:T(8,128)(2,1)S(1)}, bf16[2,48,3072]{2,1,0:T(8,128)(2,1)S(1)}, u32[]{:S(2)}, u32[]{:S(2)}) collective-permute-start(bf16[2,48,3072]{2,1,0:T(8,128)(2,1)S(1)} %collective-permute-done.2.refs_4_.refs_3_), channel_id=1, source_target_pairs={{0,3},{1,0},{2,1},{3,2},{4,7},{5,4},{6,5},{7,6},{8,11},{9,8},{10,9... | collective-permute-start | bytes 1769480 | tf_op jit(solution)/shard_map/ppermute | solution.py:43
  25.1 6.4 %shard_map.111 = (bf16[3072,1024]{1,0:T(8,128)(2,1)S(1)}, bf16[3072,1024]{1,0:T(8,128)(2,1)S(1)}, bf16[1024,3072]{1,0:T(8,128)(2,1)S(1)}, f32[8,128]{1,0:T(8,128)S(1)}) custom-call(bf16[3072,1024]{1,0:T(8,128)(2,1)} %refs_0_.1, bf16[3072,1024]{1,0:T(8,128)(2,1)} %refs_1_.1, bf16[1024,3072]{1,0:T(8,128)(2,1)} %refs_2_.1, ...), custom_call_target="tpu_custom_call" | custom-call | bytes 9438 | tf_op jit(solution)/shard_map/pallas_call | solution.py:157
  31.5 0.2 shard_map.112.refs_0_
  31.7 2.4 %collective-permute-start.8 = (bf16[2,192,3072]{2,1,0:T(8,128)(2,1)S(1)}, bf16[2,192,3072]{2,1,0:T(8,128)(2,1)S(1)}, u32[]{:S(2)}, u32[]{:S(2)}) collective-permute-start(bf16[2,192,3072]{2,1,0:T(8,128)(2,1)S(1)} %shard_map.112.refs_0_), channel_id=1, source_target_pairs={{0,8},{1,9},{2,10},{3,11},{4,12},{5,13},{6,14},{7,15},{8,0},{9,1},... | collective-permute-start | bytes 7077896 | tf_op jit(solution)/shard_map/ppermute | solution.py:43
  34.1 1.6 %collective-permute-done.4.refs_0_.refs_1_ = bf16[2,48,3072]{2,1,0:T(8,128)(2,1)S(1)} collective-permute-done((bf16[2,48,3072]{2,1,0:T(8,128)(2,1)S(1)}, bf16[2,48,3072]{2,1,0:T(8,128)(2,1)S(1)}, u32[]{:S(2)}, u32[]{:S(2)}) %collective-permute-start.4) | collective-permute-done | bytes 589856 | tf_op jit(solution)/shard_map/ppermute | solution.py:43
  35.7 0.9 collective-permute-done.3.refs_0_
  36.7 0.1 shard_map.115.refs_1_
  36.8 2.8 %collective-permute-start.9 = (bf16[2,144,3072]{2,1,0:T(8,128)(2,1)S(1)}, bf16[2,144,3072]{2,1,0:T(8,128)(2,1)S(1)}, u32[]{:S(2)}, u32[]{:S(2)}) collective-permute-start(bf16[2,144,3072]{2,1,0:T(8,128)(2,1)S(1)} %shard_map.115.refs_1_), channel_id=1, source_target_pairs={{0,8},{1,9},{2,10},{3,11},{4,12},{5,13},{6,14},{7,15},{8,0},{9,1},... | collective-permute-start | bytes 5308424 | tf_op jit(solution)/shard_map/ppermute | solution.py:43
  39.6 0.1 collective-permute-start.6
  39.7 2.6 %collective-permute-start.7 = (bf16[48,3072]{1,0:T(8,128)(2,1)S(1)}, bf16[48,3072]{1,0:T(8,128)(2,1)S(1)}, u32[]{:S(2)}, u32[]{:S(2)}) collective-permute-start(bf16[48,3072]{1,0:T(8,128)(2,1)S(1)} %shard_map.113.refs_1_), channel_id=1, source_target_pairs={{0,3},{1,0},{2,1},{3,2},{4,7},{5,4},{6,5},{7,6},{8,11},{9,8},{10,9... | collective-permute-start | bytes 884744 | tf_op jit(solution)/shard_map/ppermute | solution.py:43
  42.3 4.6 %shard_map.116 = (bf16[384,1024]{1,0:T(8,128)(2,1)S(1)}, f32[384,1024]{1,0:T(8,128)S(1)}, f32[384,1024]{1,0:T(8,128)S(1)}) custom-call(bf16[2,192,3072]{2,1,0:T(8,128)(2,1)S(1)} %shard_map.112.refs_0_, bf16[2,144,3072]{2,1,0:T(8,128)(2,1)S(1)} %shard_map.115.refs_1_, bf16[3072,1024]{1,0:T(8,128)(2,1)S(1)} %get-tuple-element.58.refs_2_.refs_1_, ...), custom_call_target="tpu_custom_call" | custom-call | flops 4227858 | bytes 9535 | tf_op jit(solution)/shard_map/pallas_call | solution.py:157
  46.9 2.6 %collective-permute-done.6.refs_1_.refs_2_ = bf16[48,3072]{1,0:T(8,128)(2,1)S(1)} collective-permute-done((bf16[48,3072]{1,0:T(8,128)(2,1)S(1)}, bf16[48,3072]{1,0:T(8,128)(2,1)S(1)}, u32[]{:S(2)}, u32[]{:S(2)}) %collective-permute-start.6) | collective-permute-done | bytes 294944 | tf_op jit(solution)/shard_map/ppermute | solution.py:43
  49.6 2.3 %shard_map.117 = (bf16[384,1024]{1,0:T(8,128)(2,1)S(1)}, f32[384,1024]{1,0:T(8,128)S(1)}, f32[384,1024]{1,0:T(8,128)S(1)}) custom-call(bf16[48,3072]{1,0:T(8,128)(2,1)S(1)} %collective-permute-done.7.refs_0_, bf16[3072,1024]{1,0:T(8,128)(2,1)S(1)} %get-tuple-element.58.refs_2_.refs_1_, ...), custom_call_target="tpu_custom_call", output_to_operand_aliasing={{0}: (3, {}), {1}: (4, {}), {2}: (5, {})} | custom-call | flops 603979 | bytes 8798 | tf_op jit(solution)/shard_map/pallas_call | solution.py:157
  51.9 1.4 %shard_map.119 = (bf16[384,3072]{1,0:T(8,128)(2,1)S(1)}, bf16[3,384,512]{2,1,0:T(8,128)(2,1)S(1)}) custom-call(bf16[2,192,3072]{2,1,0:T(8,128)(2,1)S(1)} %shard_map.112.refs_0_, bf16[2,144,3072]{2,1,0:T(8,128)(2,1)S(1)} %shard_map.115.refs_1_, bf16[48,3072]{1,0:T(8,128)(2,1)S(1)} %collective-permute-done.6.refs_1_.refs_2_, ...), custom_call_target="tpu_custom_call" | custom-call | flops 1207959 | bytes 8306 | tf_op jit(solution)/shard_map/pallas_call | solution.py:157
  53.3 0.9 collective-permute-start.11
  54.2 0.3 collective-permute-start.10
  54.5 1.4 %shard_map.120.refs_6_.refs_0_ = bf16[2,384,512]{2,1,0:T(8,128)(2,1)S(1)} custom-call(bf16[384,3072]{1,0:T(8,128)(2,1)S(1)} %get-tuple-element.66.refs_0_, bf16[1024,3072]{1,0:T(8,128)(2,1)S(1)} %get-tuple-element.57.refs_3_.refs_1_, f32[384,1024]{1,0:T(8,128)S(1)} %get-tuple-element.64.refs_5_.refs_2_, f32[384,1024]{1,0:T(8,128)S(1)} %get-tuple-element.65.refs_6_.refs_3_), custom_call_target="tpu_custom_call" | custom-call | flops 1207959 | bytes 5505 | tf_op jit(solution)/shard_map/pallas_call | solution.py:157
  55.9 1.6 %collective-permute-done.10.refs_5_ = bf16[2,48,3072]{2,1,0:T(8,128)(2,1)S(1)} collective-permute-done((bf16[2,48,3072]{2,1,0:T(8,128)(2,1)S(1)}, bf16[2,48,3072]{2,1,0:T(8,128)(2,1)S(1)}, u32[]{:S(2)}, u32[]{:S(2)}) %collective-permute-start.10) | collective-permute-done | bytes 589856 | tf_op jit(solution)/shard_map/ppermute | solution.py:43
  57.5 1.8 %shard_map.121 = (bf16[2,384,512]{2,1,0:T(8,128)(2,1)S(1)}, bf16[2,384,512]{2,1,0:T(8,128)(2,1)S(1)}) custom-call(bf16[2,192,3072]{2,1,0:T(8,128)(2,1)S(1)} %shard_map.112.refs_0_, bf16[2,144,3072]{2,1,0:T(8,128)(2,1)S(1)} %shard_map.115.refs_1_, bf16[2,48,3072]{2,1,0:T(8,128)(2,1)S(1)} %shard_map.118.refs_7_.refs_2_, ...), custom_call_target="tpu_custom_call" | custom-call | flops 1207959 | bytes 6488 | tf_op jit(solution)/shard_map/pallas_call | solution.py:157
  59.3 2.5 %collective-permute-start.15 = (bf16[2,384,512]{2,1,0:T(8,128)(2,1)S(1)}, bf16[2,384,512]{2,1,0:T(8,128)(2,1)S(1)}, u32[]{:S(2)}, u32[]{:S(2)}) collective-permute-start(bf16[2,384,512]{2,1,0:T(8,128)(2,1)S(1)} %get-tuple-element.76), channel_id=1, source_target_pairs={{0,96},{1,97},{2,98},{3,99},{4,100},{5,101},{6,102},{7,103},{8,104... | collective-permute-start | bytes 2359304 | tf_op jit(solution)/shard_map/ppermute | solution.py:43
  61.8 3.6 %shard_map.122 = (bf16[4,384,512]{2,1,0:T(8,128)(2,1)S(1)}, bf16[4,384,512]{2,1,0:T(8,128)(2,1)S(1)}) custom-call(bf16[2,192,3072]{2,1,0:T(8,128)(2,1)S(1)} %shard_map.112.refs_0_, bf16[2,144,3072]{2,1,0:T(8,128)(2,1)S(1)} %shard_map.115.refs_1_, bf16[2,48,3072]{2,1,0:T(8,128)(2,1)S(1)} %shard_map.118.refs_7_.refs_2_, ...), custom_call_target="tpu_custom_call" | custom-call | flops 2415919 | bytes 7274 | tf_op jit(solution)/shard_map/pallas_call | solution.py:157
  65.4 0.8 collective-permute-start.21
  66.3 2.6 %shard_map.123.refs_4_ = bf16[384,3072]{1,0:T(8,128)(2,1)S(1)} custom-call(bf16[384,1024]{1,0:T(8,128)(2,1)S(1)} %get-tuple-element.63.refs_4_.refs_6_.refs_0_, bf16[1024,3072]{1,0:T(8,128)(2,1)S(1)} %get-tuple-element.57.refs_3_.refs_1_, bf16[4,384,512]{2,1,0:T(8,128)(2,1)S(1)} %get-tuple-element.69.refs_2_.refs_0_), custom_call_target="tpu_custom_call" | custom-call | flops 2415919 | bytes 4718 | tf_op jit(solution)/shard_map/pallas_call | solution.py:157
  68.9 5.1 %shard_map.124 = (bf16[2,48,3072]{2,1,0:T(8,128)(2,1)S(1)}, bf16[2,48,3072]{2,1,0:T(8,128)(2,1)S(1)}, bf16[2,2,48,3072]{3,2,1,0:T(8,128)(2,1)S(1)}, bf16[2,2,48,...) custom-call(bf16[2,384,512]{2,1,0:T(8,128)(2,1)S(1)} %shard_map.120.refs_6_.refs_0_, ...), custom_call_target="tpu_custom_call" | custom-call | flops 4831838 | bytes 10813 | tf_op jit(solution)/shard_map/pallas_call | solution.py:157
  74.0 0.9 collective-permute-start.12
  75.0 1.9 %collective-permute-start.13 = (bf16[2,48,3072]{2,1,0:T(8,128)(2,1)S(1)}, bf16[2,48,3072]{2,1,0:T(8,128)(2,1)S(1)}, u32[]{:S(2)}, u32[]{:S(2)}) collective-permute-start(bf16[2,48,3072]{2,1,0:T(8,128)(2,1)S(1)} %get-tuple-element.74), channel_id=1, source_target_pairs={{0,3},{1,0},{2,1},{3,2},{4,7},{5,4},{6,5},{7,6},{8,11},{9,8},{10,9... | collective-permute-start | bytes 1769480 | tf_op jit(solution)/shard_map/ppermute | solution.py:43
  76.8 1.4 %shard_map.125 = (bf16[2,384,512]{2,1,0:T(8,128)(2,1)S(1)}, bf16[2,384,512]{2,1,0:T(8,128)(2,1)S(1)}) custom-call(bf16[2,192,3072]{2,1,0:T(8,128)(2,1)S(1)} %shard_map.112.refs_0_, bf16[2,144,3072]{2,1,0:T(8,128)(2,1)S(1)} %shard_map.115.refs_1_, bf16[2,48,3072]{2,1,0:T(8,128)(2,1)S(1)} %shard_map.118.refs_7_.refs_2_, ...), custom_call_target="tpu_custom_call" | custom-call | flops 1207959 | bytes 6488 | tf_op jit(solution)/shard_map/pallas_call | solution.py:157
  78.4 3.1 %collective-permute-done.14.refs_1_ = bf16[2,384,512]{2,1,0:T(8,128)(2,1)S(1)} collective-permute-done((bf16[2,384,512]{2,1,0:T(8,128)(2,1)S(1)}, bf16[2,384,512]{2,1,0:T(8,128)(2,1)S(1)}, u32[]{:S(2)}, u32[]{:S(2)}) %collective-permute-start.14) | collective-permute-done | bytes 786464 | tf_op jit(solution)/shard_map/ppermute | solution.py:43
  81.5 0.2 shard_map.126.refs_8_
  81.7 2.7 %collective-permute-start.20 = (bf16[2,384,512]{2,1,0:T(8,128)(2,1)S(1)}, bf16[2,384,512]{2,1,0:T(8,128)(2,1)S(1)}, u32[]{:S(2)}, u32[]{:S(2)}) collective-permute-start(bf16[2,384,512]{2,1,0:T(8,128)(2,1)S(1)} %shard_map.126.refs_8_), channel_id=1, source_target_pairs={{0,96},{1,97},{2,98},{3,99},{4,100},{5,101},{6,102},{7,103},{8,104... | collective-permute-start | bytes 2359304 | tf_op jit(solution)/shard_map/ppermute | solution.py:43
  84.4 3.0 %shard_map.127 = (bf16[2,384,512]{2,1,0:T(8,128)(2,1)S(1)}, bf16[2,384,512]{2,1,0:T(8,128)(2,1)S(1)}, bf16[2,384,512]{2,1,0:T(8,128)(2,1)S(1)}, bf16[2,384,512]{2,1,0:T(8,128)(2,1)S(1)}) custom-call(bf16[2,192,3072]{2,1,0:T(8,128)(2,1)S(1)} %shard_map.112.refs_0_, bf16[2,144,3072]{2,1,0:T(8,128)(2,1)S(1)} %shard_map.115.refs_1_, ...), custom_call_target="tpu_custom_call" | custom-call | flops 2415919 | bytes 7274 | tf_op jit(solution)/shard_map/pallas_call | solution.py:157
  87.4 0.2 shard_map.128.refs_4_
  87.6 1.6 %collective-permute-done.12.refs_1_ = bf16[2,48,3072]{2,1,0:T(8,128)(2,1)S(1)} collective-permute-done((bf16[2,48,3072]{2,1,0:T(8,128)(2,1)S(1)}, bf16[2,48,3072]{2,1,0:T(8,128)(2,1)S(1)}, u32[]{:S(2)}, u32[]{:S(2)}) %collective-permute-start.12) | collective-permute-done | bytes 589856 | tf_op jit(solution)/shard_map/ppermute | solution.py:43
  89.2 0.3 shard_map.129
  89.5 0.9 collective-permute-start.16
  90.4 2.0 %collective-permute-start.17 = (bf16[2,2,48,3072]{3,2,1,0:T(8,128)(2,1)S(1)}, bf16[2,2,48,3072]{3,2,1,0:T(8,128)(2,1)S(1)}, u32[]{:S(2)}, u32[]{:S(2)}) collective-permute-start(bf16[2,2,48,3072]{3,2,1,0:T(8,128)(2,1)S(1)} %get-tuple-element.81), channel_id=1, source_target_pairs={{0,3},{1,0},{2,1},{3,2},{4,7},{5,4},{6,5},{7,6},{8,11},{9,8},{10,9... | collective-permute-start | bytes 3538952 | tf_op jit(solution)/shard_map/ppermute | solution.py:43
  92.4 8.0 %collective-permute-done.19.refs_1_ = bf16[2,384,512]{2,1,0:T(8,128)(2,1)S(1)} collective-permute-done((bf16[2,384,512]{2,1,0:T(8,128)(2,1)S(1)}, bf16[2,384,512]{2,1,0:T(8,128)(2,1)S(1)}, u32[]{:S(2)}, u32[]{:S(2)}) %collective-permute-start.19) | collective-permute-done | bytes 786464 | tf_op jit(solution)/shard_map/ppermute | solution.py:43
  100.4 0.3 shard_map.132.refs_2_
  100.8 0.4 shard_map.135
  101.2 2.7 %collective-permute-start.27 = (bf16[192,512]{1,0:T(8,128)(2,1)S(1)}, bf16[192,512]{1,0:T(8,128)(2,1)S(1)}, u32[]{:S(2)}, u32[]{:S(2)}) collective-permute-start(bf16[192,512]{1,0:T(8,128)(2,1)S(1)} %get-tuple-element.102), channel_id=1, source_target_pairs={{0,96},{1,97},{2,98},{3,99},{4,100},{5,101},{6,102},{7,103},{8,104... | collective-permute-start | bytes 589832 | tf_op jit(solution)/shard_map/ppermute | solution.py:43
  103.9 0.7 collective-permute-start.24
  104.6 2.6 %collective-permute-done.26.refs_1_ = bf16[192,512]{1,0:T(8,128)(2,1)S(1)} collective-permute-done((bf16[192,512]{1,0:T(8,128)(2,1)S(1)}, bf16[192,512]{1,0:T(8,128)(2,1)S(1)}, u32[]{:S(2)}, u32[]{:S(2)}) %collective-permute-start.26) | collective-permute-done | bytes 196640 | tf_op jit(solution)/shard_map/ppermute | solution.py:43
  107.3 2.7 %collective-permute-start.23 = (bf16[2,384,512]{2,1,0:T(8,128)(2,1)S(1)}, bf16[2,384,512]{2,1,0:T(8,128)(2,1)S(1)}, u32[]{:S(2)}, u32[]{:S(2)}) collective-permute-start(bf16[2,384,512]{2,1,0:T(8,128)(2,1)S(1)} %get-tuple-element.92), channel_id=1, source_target_pairs={{0,96},{1,97},{2,98},{3,99},{4,100},{5,101},{6,102},{7,103},{8,104... | collective-permute-start | bytes 2359304 | tf_op jit(solution)/shard_map/ppermute | solution.py:43
  109.9 0.1 shard_map.136
  110.0 6.4 %collective-permute-done.16.refs_1_ = bf16[2,2,48,3072]{3,2,1,0:T(8,128)(2,1)S(1)} collective-permute-done((bf16[2,2,48,3072]{3,2,1,0:T(8,128)(2,1)S(1)}, bf16[2,2,48,3072]{3,2,1,0:T(8,128)(2,1)S(1)}, u32[]{:S(2)}, u32[]{:S(2)}) %collective-permute-start.16) | collective-permute-done | bytes 1179680 | tf_op jit(solution)/shard_map/ppermute | solution.py:43
  116.4 2.7 %collective-permute-start.29 = (bf16[2,192,512]{2,1,0:T(8,128)(2,1)S(1)}, bf16[2,192,512]{2,1,0:T(8,128)(2,1)S(1)}, u32[]{:S(2)}, u32[]{:S(2)}) collective-permute-start(bf16[2,192,512]{2,1,0:T(8,128)(2,1)S(1)} %get-tuple-element.104), channel_id=1, source_target_pairs={{0,96},{1,97},{2,98},{3,99},{4,100},{5,101},{6,102},{7,103},{8,104... | collective-permute-start | bytes 1179656 | tf_op jit(solution)/shard_map/ppermute | solution.py:43
  119.1 0.4 shard_map.130
  119.5 0.5 collective-permute-done.24.refs_3_
  120.0 0.5 collective-permute-start.18
  120.4 3.8 %collective-permute-done.22.refs_1_ = bf16[2,384,512]{2,1,0:T(8,128)(2,1)S(1)} collective-permute-done((bf16[2,384,512]{2,1,0:T(8,128)(2,1)S(1)}, bf16[2,384,512]{2,1,0:T(8,128)(2,1)S(1)}, u32[]{:S(2)}, u32[]{:S(2)}) %collective-permute-start.22) | collective-permute-done | bytes 786464 | tf_op jit(solution)/shard_map/ppermute | solution.py:43
  124.2 0.8 shard_map.133
  125.1 8.0 %collective-permute-start.25 = (bf16[2,192,512]{2,1,0:T(8,128)(2,1)S(1)}, bf16[2,192,512]{2,1,0:T(8,128)(2,1)S(1)}, u32[]{:S(2)}, u32[]{:S(2)}) collective-permute-start(bf16[2,192,512]{2,1,0:T(8,128)(2,1)S(1)} %get-tuple-element.95), channel_id=1, source_target_pairs={{0,8},{1,9},{2,10},{3,11},{4,12},{5,13},{6,14},{7,15},{8,0},{9,1},... | collective-permute-start | bytes 1179656 | tf_op jit(solution)/shard_map/ppermute | solution.py:43
  133.1 0.3 shard_map.137
  133.4 3.8 %collective-permute-start.30 = (bf16[1,192,512]{2,1,0:T(8,128)(2,1)S(1)}, bf16[1,192,512]{2,1,0:T(8,128)(2,1)S(1)}, u32[]{:S(2)}, u32[]{:S(2)}) collective-permute-start(bf16[1,192,512]{2,1,0:T(8,128)(2,1)S(1)} %get-tuple-element.106), channel_id=1, source_target_pairs={{0,8},{1,9},{2,10},{3,11},{4,12},{5,13},{6,14},{7,15},{8,0},{9,1},... | collective-permute-start | bytes 589832 | tf_op jit(solution)/shard_map/ppermute | solution.py:43
  137.2 1.1 collective-permute-done.30.got
  138.3 0.8 shard_map.138
  139.1 1.7 %shard_map.131 = (bf16[128,3072]{1,0:T(8,128)(2,1)}, bf16[128,3072]{1,0:T(8,128)(2,1)}) custom-call(s32[2,128]{1,0:T(2,128)S(1)} %bitcast.8, f32[1,128]{1,0:T(1,128)S(1)} %bitcast.10, bf16[2,48,3072]{2,1,0:T(8,128)(2,1)S(1)} %get-tuple-element.82.kept, bf16[2,48,3072]{2,1,0:T(8,128)(2,1)S(1)} %collective-permute-done.18.got), custom_call_target="tpu_custom_call" | custom-call | flops 75497 | bytes 2800 | tf_op jit(solution)/shard_map/pallas_call | solution.py:133
  140.8 0.9 shard_map.134
  (31 shorter events, 0.5 us)
Async XLA Ops:
  2.4 16.5 %collective-permute-start.1 = (bf16[2,48,3072]{2,1,0:T(8,128)(2,1)S(1)}, bf16[2,48,3072]{2,1,0:T(8,128)(2,1)S(1)}, u32[]{:S(2)}, u32[]{:S(2)}) collective-permute-start(bf16[2,48,3072]{2,1,0:T(8,128)(2,1)S(1)} %shard_map.110.refs_2_), channel_id=1, source_target_pairs={{0,1},{1,2},{2,3},{3,0},{4,5},{5,6},{6,7},{7,4},{8,9},{9,10},{10,1... | collective-permute-start | bytes 1769480 | tf_op jit(solution)/shard_map/ppermute | solution.py:43
  4.6 17.9 %collective-permute-start.2 = (bf16[2,48,3072]{2,1,0:T(8,128)(2,1)S(1)}, bf16[2,48,3072]{2,1,0:T(8,128)(2,1)S(1)}, u32[]{:S(2)}, u32[]{:S(2)}) collective-permute-start(bf16[2,48,3072]{2,1,0:T(8,128)(2,1)S(1)} %shard_map.110.refs_2_), channel_id=1, source_target_pairs={{0,4},{1,5},{2,6},{3,7},{4,0},{5,1},{6,2},{7,3},{8,12},{9,13},{10,... | collective-permute-start | bytes 1769480 | tf_op jit(solution)/shard_map/ppermute | solution.py:43
  8.2 16.9 %collective-permute-start = (bf16[2,48,3072]{2,1,0:T(8,128)(2,1)S(1)}, bf16[2,48,3072]{2,1,0:T(8,128)(2,1)S(1)}, u32[]{:S(2)}, u32[]{:S(2)}) collective-permute-start(bf16[2,48,3072]{2,1,0:T(8,128)(2,1)S(1)} %shard_map.110.refs_2_), channel_id=1, source_target_pairs={{0,3},{1,0},{2,1},{3,2},{4,7},{5,4},{6,5},{7,6},{8,11},{9,8},{10,9... | collective-permute-start | bytes 1769480 | tf_op jit(solution)/shard_map/ppermute | solution.py:43
  18.9 16.8 %collective-permute-start.5 = (bf16[2,48,3072]{2,1,0:T(8,128)(2,1)S(1)}, bf16[2,48,3072]{2,1,0:T(8,128)(2,1)S(1)}, u32[]{:S(2)}, u32[]{:S(2)}) collective-permute-start(bf16[2,48,3072]{2,1,0:T(8,128)(2,1)S(1)} %collective-permute-done.1.refs_1_), channel_id=1, source_target_pairs={{0,4},{1,5},{2,6},{3,7},{4,0},{5,1},{6,2},{7,3},{8,12},{9,13},{10,... | collective-permute-start | bytes 1769480 | tf_op jit(solution)/shard_map/ppermute | solution.py:43
  22.4 14.3 %collective-permute-start.3 = (bf16[2,48,3072]{2,1,0:T(8,128)(2,1)S(1)}, bf16[2,48,3072]{2,1,0:T(8,128)(2,1)S(1)}, u32[]{:S(2)}, u32[]{:S(2)}) collective-permute-start(bf16[2,48,3072]{2,1,0:T(8,128)(2,1)S(1)} %collective-permute-done.1.refs_1_), channel_id=1, source_target_pairs={{0,1},{1,2},{2,3},{3,0},{4,5},{5,6},{6,7},{7,4},{8,9},{9,10},{10,1... | collective-permute-start | bytes 1769480 | tf_op jit(solution)/shard_map/ppermute | solution.py:43
  22.4 13.3 %collective-permute-start.4 = (bf16[2,48,3072]{2,1,0:T(8,128)(2,1)S(1)}, bf16[2,48,3072]{2,1,0:T(8,128)(2,1)S(1)}, u32[]{:S(2)}, u32[]{:S(2)}) collective-permute-start(bf16[2,48,3072]{2,1,0:T(8,128)(2,1)S(1)} %collective-permute-done.2.refs_4_.refs_3_), channel_id=1, source_target_pairs={{0,3},{1,0},{2,1},{3,2},{4,7},{5,4},{6,5},{7,6},{8,11},{9,8},{10,9... | collective-permute-start | bytes 1769480 | tf_op jit(solution)/shard_map/ppermute | solution.py:43
  31.7 17.9 %collective-permute-start.8 = (bf16[2,192,3072]{2,1,0:T(8,128)(2,1)S(1)}, bf16[2,192,3072]{2,1,0:T(8,128)(2,1)S(1)}, u32[]{:S(2)}, u32[]{:S(2)}) collective-permute-start(bf16[2,192,3072]{2,1,0:T(8,128)(2,1)S(1)} %shard_map.112.refs_0_), channel_id=1, source_target_pairs={{0,8},{1,9},{2,10},{3,11},{4,12},{5,13},{6,14},{7,15},{8,0},{9,1},... | collective-permute-start | bytes 7077896 | tf_op jit(solution)/shard_map/ppermute | solution.py:43
  36.8 12.8 %collective-permute-start.9 = (bf16[2,144,3072]{2,1,0:T(8,128)(2,1)S(1)}, bf16[2,144,3072]{2,1,0:T(8,128)(2,1)S(1)}, u32[]{:S(2)}, u32[]{:S(2)}) collective-permute-start(bf16[2,144,3072]{2,1,0:T(8,128)(2,1)S(1)} %shard_map.115.refs_1_), channel_id=1, source_target_pairs={{0,8},{1,9},{2,10},{3,11},{4,12},{5,13},{6,14},{7,15},{8,0},{9,1},... | collective-permute-start | bytes 5308424 | tf_op jit(solution)/shard_map/ppermute | solution.py:43
  39.6 9.9 %collective-permute-start.6 = (bf16[48,3072]{1,0:T(8,128)(2,1)S(1)}, bf16[48,3072]{1,0:T(8,128)(2,1)S(1)}, u32[]{:S(2)}, u32[]{:S(2)}) collective-permute-start(bf16[48,3072]{1,0:T(8,128)(2,1)S(1)} %shard_map.114.refs_3_.refs_4_), channel_id=1, source_target_pairs={{0,1},{1,2},{2,3},{3,0},{4,5},{5,6},{6,7},{7,4},{8,9},{9,10},{10,1... | collective-permute-start | bytes 884744 | tf_op jit(solution)/shard_map/ppermute | solution.py:43
  39.7 9.8 %collective-permute-start.7 = (bf16[48,3072]{1,0:T(8,128)(2,1)S(1)}, bf16[48,3072]{1,0:T(8,128)(2,1)S(1)}, u32[]{:S(2)}, u32[]{:S(2)}) collective-permute-start(bf16[48,3072]{1,0:T(8,128)(2,1)S(1)} %shard_map.113.refs_1_), channel_id=1, source_target_pairs={{0,3},{1,0},{2,1},{3,2},{4,7},{5,4},{6,5},{7,6},{8,11},{9,8},{10,9... | collective-permute-start | bytes 884744 | tf_op jit(solution)/shard_map/ppermute | solution.py:43
  53.3 4.2 %collective-permute-start.11 = (bf16[3,384,512]{2,1,0:T(8,128)(2,1)S(1)}, bf16[3,384,512]{2,1,0:T(8,128)(2,1)S(1)}, u32[]{:S(2)}, u32[]{:S(2)}) collective-permute-start(bf16[3,384,512]{2,1,0:T(8,128)(2,1)S(1)} %get-tuple-element.67.refs_1_), channel_id=1, source_target_pairs={{0,8},{1,9},{2,10},{3,11},{4,12},{5,13},{6,14},{7,15},{8,0},{9,1},... | collective-permute-start | bytes 3538952 | tf_op jit(solution)/shard_map/ppermute | solution.py:43
  54.2 3.3 %collective-permute-start.10 = (bf16[2,48,3072]{2,1,0:T(8,128)(2,1)S(1)}, bf16[2,48,3072]{2,1,0:T(8,128)(2,1)S(1)}, u32[]{:S(2)}, u32[]{:S(2)}) collective-permute-start(bf16[2,48,3072]{2,1,0:T(8,128)(2,1)S(1)} %shard_map.118.refs_7_.refs_2_), channel_id=1, source_target_pairs={{0,8},{1,9},{2,10},{3,11},{4,12},{5,13},{6,14},{7,15},{8,0},{9,1},... | collective-permute-start | bytes 1769480 | tf_op jit(solution)/shard_map/ppermute | solution.py:43
  59.3 19.1 %collective-permute-start.15 = (bf16[2,384,512]{2,1,0:T(8,128)(2,1)S(1)}, bf16[2,384,512]{2,1,0:T(8,128)(2,1)S(1)}, u32[]{:S(2)}, u32[]{:S(2)}) collective-permute-start(bf16[2,384,512]{2,1,0:T(8,128)(2,1)S(1)} %get-tuple-element.76), channel_id=1, source_target_pairs={{0,96},{1,97},{2,98},{3,99},{4,100},{5,101},{6,102},{7,103},{8,104... | collective-permute-start | bytes 2359304 | tf_op jit(solution)/shard_map/ppermute | solution.py:43
  61.8 19.6 %collective-permute-start.14 = (bf16[2,384,512]{2,1,0:T(8,128)(2,1)S(1)}, bf16[2,384,512]{2,1,0:T(8,128)(2,1)S(1)}, u32[]{:S(2)}, u32[]{:S(2)}) collective-permute-start(bf16[2,384,512]{2,1,0:T(8,128)(2,1)S(1)} %get-tuple-element.68.refs_8_), channel_id=1, source_target_pairs={{0,32},{1,33},{2,34},{3,35},{4,36},{5,37},{6,38},{7,39},{8,40},{9,... | collective-permute-start | bytes 2359304 | tf_op jit(solution)/shard_map/ppermute | solution.py:43
  65.4 35.4 %collective-permute-start.21 = (bf16[4,384,512]{2,1,0:T(8,128)(2,1)S(1)}, bf16[4,384,512]{2,1,0:T(8,128)(2,1)S(1)}, u32[]{:S(2)}, u32[]{:S(2)}) collective-permute-start(bf16[4,384,512]{2,1,0:T(8,128)(2,1)S(1)} %get-tuple-element.90), channel_id=1, source_target_pairs={{0,16},{1,17},{2,18},{3,19},{4,20},{5,21},{6,22},{7,23},{8,24},{9,... | collective-permute-start | bytes 4718600 | tf_op jit(solution)/shard_map/ppermute | solution.py:43
  74.0 15.2 %collective-permute-start.12 = (bf16[2,48,3072]{2,1,0:T(8,128)(2,1)S(1)}, bf16[2,48,3072]{2,1,0:T(8,128)(2,1)S(1)}, u32[]{:S(2)}, u32[]{:S(2)}) collective-permute-start(bf16[2,48,3072]{2,1,0:T(8,128)(2,1)S(1)} %get-tuple-element.72), channel_id=1, source_target_pairs={{0,1},{1,2},{2,3},{3,0},{4,5},{5,6},{6,7},{7,4},{8,9},{9,10},{10,1... | collective-permute-start | bytes 1769480 | tf_op jit(solution)/shard_map/ppermute | solution.py:43
  75.0 14.2 %collective-permute-start.13 = (bf16[2,48,3072]{2,1,0:T(8,128)(2,1)S(1)}, bf16[2,48,3072]{2,1,0:T(8,128)(2,1)S(1)}, u32[]{:S(2)}, u32[]{:S(2)}) collective-permute-start(bf16[2,48,3072]{2,1,0:T(8,128)(2,1)S(1)} %get-tuple-element.74), channel_id=1, source_target_pairs={{0,3},{1,0},{2,1},{3,2},{4,7},{5,4},{6,5},{7,6},{8,11},{9,8},{10,9... | collective-permute-start | bytes 1769480 | tf_op jit(solution)/shard_map/ppermute | solution.py:43
  81.7 18.8 %collective-permute-start.19 = (bf16[2,384,512]{2,1,0:T(8,128)(2,1)S(1)}, bf16[2,384,512]{2,1,0:T(8,128)(2,1)S(1)}, u32[]{:S(2)}, u32[]{:S(2)}) collective-permute-start(bf16[2,384,512]{2,1,0:T(8,128)(2,1)S(1)} %get-tuple-element.89), channel_id=1, source_target_pairs={{0,32},{1,33},{2,34},{3,35},{4,36},{5,37},{6,38},{7,39},{8,40},{9,... | collective-permute-start | bytes 2359304 | tf_op jit(solution)/shard_map/ppermute | solution.py:43
  81.7 18.7 %collective-permute-start.20 = (bf16[2,384,512]{2,1,0:T(8,128)(2,1)S(1)}, bf16[2,384,512]{2,1,0:T(8,128)(2,1)S(1)}, u32[]{:S(2)}, u32[]{:S(2)}) collective-permute-start(bf16[2,384,512]{2,1,0:T(8,128)(2,1)S(1)} %shard_map.126.refs_8_), channel_id=1, source_target_pairs={{0,96},{1,97},{2,98},{3,99},{4,100},{5,101},{6,102},{7,103},{8,104... | collective-permute-start | bytes 2359304 | tf_op jit(solution)/shard_map/ppermute | solution.py:43
  89.5 26.9 %collective-permute-start.16 = (bf16[2,2,48,3072]{3,2,1,0:T(8,128)(2,1)S(1)}, bf16[2,2,48,3072]{3,2,1,0:T(8,128)(2,1)S(1)}, u32[]{:S(2)}, u32[]{:S(2)}) collective-permute-start(bf16[2,2,48,3072]{3,2,1,0:T(8,128)(2,1)S(1)} %get-tuple-element.80), channel_id=1, source_target_pairs={{0,1},{1,2},{2,3},{3,0},{4,5},{5,6},{6,7},{7,4},{8,9},{9,10},{10,1... | collective-permute-start | bytes 3538952 | tf_op jit(solution)/shard_map/ppermute | solution.py:43
  90.4 26.0 %collective-permute-start.17 = (bf16[2,2,48,3072]{3,2,1,0:T(8,128)(2,1)S(1)}, bf16[2,2,48,3072]{3,2,1,0:T(8,128)(2,1)S(1)}, u32[]{:S(2)}, u32[]{:S(2)}) collective-permute-start(bf16[2,2,48,3072]{3,2,1,0:T(8,128)(2,1)S(1)} %get-tuple-element.81), channel_id=1, source_target_pairs={{0,3},{1,0},{2,1},{3,2},{4,7},{5,4},{6,5},{7,6},{8,11},{9,8},{10,9... | collective-permute-start | bytes 3538952 | tf_op jit(solution)/shard_map/ppermute | solution.py:43
  101.2 6.1 %collective-permute-start.26 = (bf16[192,512]{1,0:T(8,128)(2,1)S(1)}, bf16[192,512]{1,0:T(8,128)(2,1)S(1)}, u32[]{:S(2)}, u32[]{:S(2)}) collective-permute-start(bf16[192,512]{1,0:T(8,128)(2,1)S(1)} %get-tuple-element.100), channel_id=1, source_target_pairs={{0,32},{1,33},{2,34},{3,35},{4,36},{5,37},{6,38},{7,39},{8,40},{9,... | collective-permute-start | bytes 589832 | tf_op jit(solution)/shard_map/ppermute | solution.py:43
  101.2 6.0 %collective-permute-start.27 = (bf16[192,512]{1,0:T(8,128)(2,1)S(1)}, bf16[192,512]{1,0:T(8,128)(2,1)S(1)}, u32[]{:S(2)}, u32[]{:S(2)}) collective-permute-start(bf16[192,512]{1,0:T(8,128)(2,1)S(1)} %get-tuple-element.102), channel_id=1, source_target_pairs={{0,96},{1,97},{2,98},{3,99},{4,100},{5,101},{6,102},{7,103},{8,104... | collective-permute-start | bytes 589832 | tf_op jit(solution)/shard_map/ppermute | solution.py:43
  103.9 16.1 %collective-permute-start.24 = (bf16[2,384,512]{2,1,0:T(8,128)(2,1)S(1)}, bf16[2,384,512]{2,1,0:T(8,128)(2,1)S(1)}, u32[]{:S(2)}, u32[]{:S(2)}) collective-permute-start(bf16[2,384,512]{2,1,0:T(8,128)(2,1)S(1)} %shard_map.132.refs_2_), channel_id=1, source_target_pairs={{0,16},{1,17},{2,18},{3,19},{4,20},{5,21},{6,22},{7,23},{8,24},{9,... | collective-permute-start | bytes 2359304 | tf_op jit(solution)/shard_map/ppermute | solution.py:43
  107.3 17.0 %collective-permute-start.22 = (bf16[2,384,512]{2,1,0:T(8,128)(2,1)S(1)}, bf16[2,384,512]{2,1,0:T(8,128)(2,1)S(1)}, u32[]{:S(2)}, u32[]{:S(2)}) collective-permute-start(bf16[2,384,512]{2,1,0:T(8,128)(2,1)S(1)} %shard_map.128.refs_4_), channel_id=1, source_target_pairs={{0,32},{1,33},{2,34},{3,35},{4,36},{5,37},{6,38},{7,39},{8,40},{9,... | collective-permute-start | bytes 2359304 | tf_op jit(solution)/shard_map/ppermute | solution.py:43
  107.3 17.0 %collective-permute-start.23 = (bf16[2,384,512]{2,1,0:T(8,128)(2,1)S(1)}, bf16[2,384,512]{2,1,0:T(8,128)(2,1)S(1)}, u32[]{:S(2)}, u32[]{:S(2)}) collective-permute-start(bf16[2,384,512]{2,1,0:T(8,128)(2,1)S(1)} %get-tuple-element.92), channel_id=1, source_target_pairs={{0,96},{1,97},{2,98},{3,99},{4,100},{5,101},{6,102},{7,103},{8,104... | collective-permute-start | bytes 2359304 | tf_op jit(solution)/shard_map/ppermute | solution.py:43
  116.4 16.7 %collective-permute-start.28 = (bf16[2,192,512]{2,1,0:T(8,128)(2,1)S(1)}, bf16[2,192,512]{2,1,0:T(8,128)(2,1)S(1)}, u32[]{:S(2)}, u32[]{:S(2)}) collective-permute-start(bf16[2,192,512]{2,1,0:T(8,128)(2,1)S(1)} %get-tuple-element.103), channel_id=1, source_target_pairs={{0,32},{1,33},{2,34},{3,35},{4,36},{5,37},{6,38},{7,39},{8,40},{9,... | collective-permute-start | bytes 1179656 | tf_op jit(solution)/shard_map/ppermute | solution.py:43
  116.4 16.7 %collective-permute-start.29 = (bf16[2,192,512]{2,1,0:T(8,128)(2,1)S(1)}, bf16[2,192,512]{2,1,0:T(8,128)(2,1)S(1)}, u32[]{:S(2)}, u32[]{:S(2)}) collective-permute-start(bf16[2,192,512]{2,1,0:T(8,128)(2,1)S(1)} %get-tuple-element.104), channel_id=1, source_target_pairs={{0,96},{1,97},{2,98},{3,99},{4,100},{5,101},{6,102},{7,103},{8,104... | collective-permute-start | bytes 1179656 | tf_op jit(solution)/shard_map/ppermute | solution.py:43
  120.0 19.1 %collective-permute-start.18 = (bf16[2,48,3072]{2,1,0:T(8,128)(2,1)S(1)}, bf16[2,48,3072]{2,1,0:T(8,128)(2,1)S(1)}, u32[]{:S(2)}, u32[]{:S(2)}) collective-permute-start(bf16[2,48,3072]{2,1,0:T(8,128)(2,1)S(1)} %get-tuple-element.83), channel_id=1, source_target_pairs={{0,4},{1,5},{2,6},{3,7},{4,0},{5,1},{6,2},{7,3},{8,12},{9,13},{10,... | collective-permute-start | bytes 1769480 | tf_op jit(solution)/shard_map/ppermute | solution.py:43
  125.0 14.0 %copy-start = (s32[128,2]{0,1:T(2,128)S(1)}, s32[128,2]{0,1:T(2,128)}, u32[]{:S(2)}) copy-start(s32[128,2]{0,1:T(2,128)} %param.9) | copy-start | bytes 3076
  125.0 14.0 %copy-start.1 = (f32[128]{0:T(128)S(1)}, f32[128]{0:T(128)}, u32[]{:S(2)}) copy-start(f32[128]{0:T(128)} %param.10) | copy-start | bytes 1540
  125.1 15.7 %collective-permute-start.25 = (bf16[2,192,512]{2,1,0:T(8,128)(2,1)S(1)}, bf16[2,192,512]{2,1,0:T(8,128)(2,1)S(1)}, u32[]{:S(2)}, u32[]{:S(2)}) collective-permute-start(bf16[2,192,512]{2,1,0:T(8,128)(2,1)S(1)} %get-tuple-element.95), channel_id=1, source_target_pairs={{0,8},{1,9},{2,10},{3,11},{4,12},{5,13},{6,14},{7,15},{8,0},{9,1},... | collective-permute-start | bytes 1179656 | tf_op jit(solution)/shard_map/ppermute | solution.py:43
  133.4 4.9 %collective-permute-start.30 = (bf16[1,192,512]{2,1,0:T(8,128)(2,1)S(1)}, bf16[1,192,512]{2,1,0:T(8,128)(2,1)S(1)}, u32[]{:S(2)}, u32[]{:S(2)}) collective-permute-start(bf16[1,192,512]{2,1,0:T(8,128)(2,1)S(1)} %get-tuple-element.106), channel_id=1, source_target_pairs={{0,8},{1,9},{2,10},{3,11},{4,12},{5,13},{6,14},{7,15},{8,0},{9,1},... | collective-permute-start | bytes 589832 | tf_op jit(solution)/shard_map/ppermute | solution.py:43
